TPU v7x, 32 devices: a whole 2x2x4 slice. The times are simulated.
32 devices in a mesh: row: 4 (over y, core), col: 8 (over z, x).
Axes of the slice: x: 2, y: 2, z: 4, core: 2. Of those that a mesh axis runs over, the one named last changes fastest.
Arguments:
- state: float32 [3, 512, 2048], P(None, 'row', 'col'), may hold values from -0.675 to 1.5, as said below
- row_count: int32 [4, 8], P('row', 'col'), may hold values from 0 to 64, as said below
- col_count: int32 [4, 8], P('row', 'col'), may hold values from 0 to 64, as said below
- patch_pos: int32 [4, 8, 2], P('row', 'col'), may hold values from 0 to 192, as said below
- patch_ext: int32 [4, 8, 2], P('row', 'col'), may hold values from 16 to 64, as said below
Outputs:
- richardson_error: float32 [256, 1024], P('row', 'col')
- moved_state: float32 [3, 512, 2048], P(None, 'row', 'col')
- refined_patch: float32 [3, 512, 1024], P(None, 'row', 'col')
Inputs may be any that keep to these rules, and one draw needn't show every extreme that they name: `state`: depth lies in [0.5, 1.5]; the momenta are depth times a velocity of magnitude at most 0.45. `row_count`: some tile takes over exactly 64 rows and some none. `col_count`: some tile takes over exactly 64 columns and some none. `patch_pos`: component 0 is at most 64 and component 1 at most 192; both ends are reached. `patch_ext`: some tile is flagged over its whole patch.
All inputs are finite; a program needn't handle non-finite values.
Results may differ from a plain program's by a relative error of at most 0.0003.
Values sent between devices are 32-bit elements; how exact they have to be, the bound alone decides.
No kernel may reach another device: no remote copies, remote signals or barrier semaphores. Data moves between devices by JAX's collectives and lax.ppermute only.
A program may use at most 128 MiB of HBM per device.

v0:
```python
import math

import jax
import jax.numpy as jnp
from jax import lax
from jax.sharding import PartitionSpec as P

SLAB = 64
PATCH = 64


GRAV = 1.0
RATIO = 0.1
ERR_SCALE = 10.0


def with_halo(value, sides, width):
    for axis, dim in sides:
        devices, length = (lax.axis_size(axis), value.shape[dim])
        up = [(i, (i + 1) % devices) for i in range(devices)]
        down = [(j, i) for i, j in up]
        last = lax.slice_in_dim(value, length - width, length, axis=dim)
        first = lax.slice_in_dim(value, 0, width, axis=dim)
        before = lax.ppermute(last, axis, up)
        after = lax.ppermute(first, axis, down)
        value = jnp.concatenate([before, value, after], axis=dim)
    return value


def shifted(value, axis, by):
    devices = lax.axis_size(axis)
    return lax.ppermute(value, axis, [(i, (i + by) % devices) for i in range(devices)])


def face_flux(left_vals, right_vals, normal):
    tangent = 3 - normal

    def physical(fields):
        depth = fields[0]
        velocity = fields[normal] / depth
        flux = [None, None, None]
        flux[0] = fields[normal]
        flux[normal] = fields[normal] * velocity + 0.5 * GRAV * depth * depth
        flux[tangent] = fields[tangent] * velocity
        return (flux, jnp.abs(velocity) + jnp.sqrt(GRAV * depth))

    flux_left, speed_left = physical(left_vals)
    flux_right, speed_right = physical(right_vals)
    speed = jnp.maximum(speed_left, speed_right)
    return [
        0.5 * (flux_left[comp] + flux_right[comp])
        - 0.5 * speed * (right_vals[comp] - left_vals[comp])
        for comp in range(3)
    ]


def rusanov_step(cells):
    fields = [cells[comp] for comp in range(3)]
    flux_row = face_flux([f[:-1, 1:-1] for f in fields], [f[1:, 1:-1] for f in fields], 1)
    flux_col = face_flux([f[1:-1, :-1] for f in fields], [f[1:-1, 1:] for f in fields], 2)
    result = [
        fields[comp][1:-1, 1:-1]
        - RATIO * (flux_row[comp][1:] - flux_row[comp][:-1])
        - RATIO * (flux_col[comp][:, 1:] - flux_col[comp][:, :-1])
        for comp in range(3)
    ]
    return jnp.stack(result)


def coarsen(cells):
    shaped = cells.reshape(cells.shape[0], cells.shape[1] // 2, 2, cells.shape[2] // 2, 2)
    return 0.25 * (
        shaped[:, :, 0, :, 0]
        + shaped[:, :, 1, :, 0]
        + shaped[:, :, 0, :, 1]
        + shaped[:, :, 1, :, 1]
    )


def richardson(fine_two, coarse_one):
    return ERR_SCALE * jnp.sum(jnp.abs(coarsen(fine_two) - coarse_one), axis=0)


def minmod(lower_diff, upper_diff):
    chosen = jnp.where(jnp.abs(lower_diff) < jnp.abs(upper_diff), lower_diff, upper_diff)
    return jnp.where(lower_diff * upper_diff > 0, chosen, 0.0)


def muscl_step(cells):
    fields = [cells[comp] for comp in range(3)]
    inner_rows = cells.shape[1] - 4
    inner_cols = cells.shape[2] - 4
    row_band = [f[:, 2:-2] for f in fields]
    deltas = [b[1:] - b[:-1] for b in row_band]
    slopes = [minmod(d[:-1], d[1:]) for d in deltas]
    left_vals = [
        row_band[c][1 : inner_rows + 2] + 0.5 * slopes[c][: inner_rows + 1] for c in range(3)
    ]
    right_vals = [
        row_band[c][2 : inner_rows + 3] - 0.5 * slopes[c][1 : inner_rows + 2] for c in range(3)
    ]
    flux_row = face_flux(left_vals, right_vals, 1)
    col_band = [f[2:-2, :] for f in fields]
    deltas = [b[:, 1:] - b[:, :-1] for b in col_band]
    slopes = [minmod(d[:, :-1], d[:, 1:]) for d in deltas]
    left_vals = [
        col_band[c][:, 1 : inner_cols + 2] + 0.5 * slopes[c][:, : inner_cols + 1] for c in range(3)
    ]
    right_vals = [
        col_band[c][:, 2 : inner_cols + 3] - 0.5 * slopes[c][:, 1 : inner_cols + 2]
        for c in range(3)
    ]
    flux_col = face_flux(left_vals, right_vals, 2)
    result = [
        fields[comp][2:-2, 2:-2]
        - RATIO * (flux_row[comp][1:] - flux_row[comp][:-1])
        - RATIO * (flux_col[comp][:, 1:] - flux_col[comp][:, :-1])
        for comp in range(3)
    ]
    return jnp.stack(result)


def by_blocks(step_fn, padded, rows_out, rim):
    block = math.gcd(rows_out, 16)
    count = rows_out // block

    def one_block(index):
        piece = lax.dynamic_slice_in_dim(padded, index * block, block + 2 * rim, padded.ndim - 2)
        return step_fn(piece)

    stacked = lax.map(one_block, jnp.arange(count, dtype=jnp.int32))
    stacked = jnp.moveaxis(stacked, 0, -3)
    shape = stacked.shape
    return stacked.reshape(shape[:-3] + (shape[-3] * shape[-2], shape[-1]))


def place_top(own_cells, slab_in, count_in):
    buffer = jnp.concatenate([slab_in, jnp.zeros_like(slab_in)], axis=1)
    aligned = lax.dynamic_slice_in_dim(buffer, SLAB - count_in, SLAB, 1)
    row_ids = lax.broadcasted_iota(jnp.int32, (1, SLAB, 1), 1)
    return jnp.where(row_ids < count_in, aligned, own_cells)


def place_cols(own_cells, slab_in, count_in):
    buffer = jnp.concatenate([slab_in, jnp.zeros_like(slab_in)], axis=2)
    aligned = lax.dynamic_slice_in_dim(buffer, SLAB - count_in, SLAB, 2)
    col_ids = lax.broadcasted_iota(jnp.int32, (1, 1, SLAB), 2)
    left_part = jnp.where(col_ids < count_in, aligned, own_cells[:, :, :SLAB])
    return jnp.concatenate([left_part, own_cells[:, :, SLAB:]], axis=2)


def refine_patch(padded, row_start, col_start, extent):
    zero_index = jnp.zeros((), jnp.int32)
    region = lax.dynamic_slice(
        padded, (zero_index, row_start, col_start), (3, PATCH + 4, PATCH + 4)
    )
    refined_cells = jnp.broadcast_to(
        region[:, :, None, :, None], (3, PATCH + 4, 2, PATCH + 4, 2)
    ).reshape(3, 2 * PATCH + 8, 2 * PATCH + 8)
    halfway = muscl_step(refined_cells)
    finished = muscl_step(halfway)
    row_ids = lax.broadcasted_iota(jnp.int32, (1, 2 * PATCH, 1), 1)
    col_ids = lax.broadcasted_iota(jnp.int32, (1, 1, 2 * PATCH), 2)
    inside = (row_ids < 2 * extent[0]) & (col_ids < 2 * extent[1])
    return jnp.where(inside, finished, 0.0)


def per_device(state, row_count, col_count, patch_pos, patch_ext):
    tile_rows = state.shape[1]
    tile_cols = state.shape[2]
    padded = with_halo(state, (("row", 1), ("col", 2)), 1)
    fine_one = by_blocks(rusanov_step, padded, tile_rows, 1)
    fine_rim = with_halo(fine_one, (("row", 1), ("col", 2)), 1)
    fine_two = by_blocks(rusanov_step, fine_rim, tile_rows, 1)
    coarse_rim = with_halo(coarsen(state), (("row", 1), ("col", 2)), 1)
    coarse_one = by_blocks(rusanov_step, coarse_rim, tile_rows // 2, 1)
    error_field = richardson(fine_two, coarse_one)
    upper_slab = shifted(state[:, tile_rows - SLAB :, :], "row", 1)
    top_rows = place_top(state[:, :SLAB, :], upper_slab, row_count[0, 0])
    row_moved = jnp.concatenate([top_rows, state[:, SLAB:, :]], axis=1)
    left_slab = shifted(row_moved[:, :, tile_cols - SLAB :], "col", 1)
    moved_state = place_cols(row_moved, left_slab, col_count[0, 0])
    padded_moved = with_halo(moved_state, (("row", 1), ("col", 2)), 2)
    patch_start = patch_pos[0, 0]
    refined = refine_patch(padded_moved, patch_start[0], patch_start[1], patch_ext[0, 0])
    return (error_field, moved_state, refined)


def solution(mesh):
    placed = (
        P(None, "row", "col"),
        P("row", "col"),
        P("row", "col"),
        P("row", "col", None),
        P("row", "col", None),
    )
    return jax.shard_map(
        per_device,
        mesh=mesh,
        in_specs=placed,
        out_specs=(P("row", "col"), P(None, "row", "col"), P(None, "row", "col")),
        check_vma=False,
    )
```

profile of v0, /device:TPU:0, one launch (start us, length us, event | category | flops | bytes accessed | tf_op | source)
XLA Modules:
  0.0 235.9 jit_solution(483710690816946957)
XLA Ops:
  3.8 27.3 %reshape.134 = f32[3,64,2,128,2]{4,3,2,1,0:T(8,128)} reshape(f32[3,128,256]{2,1,0:T(8,128)} %param.11) | data formatting | bytes 786432 | tf_op jit(solution)/shard_map/reshape | solution.py:71
  31.1 19.6 %fusion.79 = f32[3,64,128]{2,1,0:T(8,128)S(1)} fusion(f32[3,64,2,128,2]{4,3,2,1,0:T(8,128)} %reshape.134), kind=kLoop, calls=%fused_computation.152 | loop fusion | flops 98304 | bytes 491520 | tf_op jit(solution)/shard_map/mul | solution.py:72
  61.1 4.6 %collective-permute-start.3 = (f32[3,130,1]{2,1,0:T(8,128)S(1)}, f32[3,130,1]{2,1,0:T(8,128)S(1)}, u32[]{:S(2)}, u32[]{:S(2)}) collective-permute-start(f32[3,130,1]{2,1,0:T(8,128)S(1)} %get-tuple-element.144), channel_id=1, source_target_pairs={{1,0},{2,1},{3,2},{4,3},{5,4},{6,5},{7,6},{0,7},{9,8},{10,9},{11,1... | collective-permute-start | bytes 4688 | tf_op jit(solution)/shard_map/ppermute | solution.py:25
  65.8 4.8 %collective-permute-start.11 = (f32[3,66,1]{2,1,0:T(8,128)S(1)}, f32[3,66,1]{2,1,0:T(8,128)S(1)}, u32[]{:S(2)}, u32[]{:S(2)}) collective-permute-start(f32[3,66,1]{2,1,0:T(8,128)S(1)} %get-tuple-element.156), channel_id=1, source_target_pairs={{1,0},{2,1},{3,2},{4,3},{5,4},{6,5},{7,6},{0,7},{9,8},{10,9},{11,1... | collective-permute-start | bytes 2384 | tf_op jit(solution)/shard_map/ppermute | solution.py:25
  70.5 4.7 %collective-permute-done.2 = f32[3,130,1]{2,1,0:T(8,128)S(1)} collective-permute-done((f32[3,130,1]{2,1,0:T(8,128)S(1)}, f32[3,130,1]{2,1,0:T(8,128)S(1)}, u32[]{:S(2)}, u32[]{:S(2)}) %collective-permute-start.2) | collective-permute-done | bytes 1592 | tf_op jit(solution)/shard_map/ppermute | solution.py:24
  75.6 14.3 %while.30 = (s32[]{:T(128)}, f32[8,3,16,256]{3,2,1,0:T(8,128)S(1)}, s32[8]{0:T(128)S(1)}, f32[3,130,258]{2,1,0:T(8,128)S(1)}, s32[]{:T(128)}, /*index=5*/s32[]{:T(128)}, s32[]{}, s32[1]{0:T(128)}, s32[]{:T(128)}, s32[]{}) while((s32[]{:T(128)}, f32[8,3,16,256]{3,2,1,0:T(8,128)S(1)}, s32[8]{0:T(128)S(1)}, f32[3,130,258]{2,1,0:T(8,128)S(1)}, ...), condition=%wide.region_1.2_spmd, body=%wide.region_0.1_spmd.sunk | while | flops 377624 | bytes 809583 | solution.py:131
  94.0 5.1 %collective-permute-start.7 = (f32[3,130,1]{2,1,0:T(8,128)S(1)}, f32[3,130,1]{2,1,0:T(8,128)S(1)}, u32[]{:S(2)}, u32[]{:S(2)}) collective-permute-start(f32[3,130,1]{2,1,0:T(8,128)S(1)} %get-tuple-element.142), channel_id=1, source_target_pairs={{1,0},{2,1},{3,2},{4,3},{5,4},{6,5},{7,6},{0,7},{9,8},{10,9},{11,1... | collective-permute-start | bytes 4688 | tf_op jit(solution)/shard_map/ppermute | solution.py:25
  99.1 6.5 %while.32 = (s32[]{:T(128)}, f32[4,3,16,128]{3,2,0,1:T(8,128)S(1)}, s32[4]{0:T(128)S(1)}, f32[3,66,130]{2,1,0:T(8,128)S(1)}, s32[]{:T(128)}, /*index=5*/s32[]{:T(128)}, s32[]{}, s32[1]{0:T(128)}, s32[]{:T(128)}, s32[]{}) while((s32[]{:T(128)}, f32[4,3,16,128]{3,2,0,1:T(8,128)S(1)}, s32[4]{0:T(128)S(1)}, f32[3,66,130]{2,1,0:T(8,128)S(1)}, ...), condition=%wide.region_5.6_spmd, body=%wide.region_4.5_spmd.sunk | while | flops 189080 | bytes 405615 | solution.py:131
  108.7 13.6 %while.31 = (s32[]{:T(128)}, f32[8,3,16,256]{3,2,1,0:T(8,128)S(1)}, s32[8]{0:T(128)S(1)}, f32[3,130,258]{2,1,0:T(8,128)S(1)}, s32[]{:T(128)}, /*index=5*/s32[]{:T(128)}, s32[]{}, s32[1]{0:T(128)}, s32[]{:T(128)}, s32[]{}) while((s32[]{:T(128)}, f32[8,3,16,256]{3,2,1,0:T(8,128)S(1)}, s32[8]{0:T(128)S(1)}, f32[3,130,258]{2,1,0:T(8,128)S(1)}, ...), condition=%wide.region_3.4_spmd, body=%wide.region_2.3_spmd.sunk | while | flops 377624 | bytes 809583 | solution.py:131
  122.3 26.6 %reshape_reshape.3 = f32[3,64,2,128,2]{4,3,2,1,0:T(8,128)} reshape(f32[3,8,16,256]{3,2,1,0:T(8,128)S(1)} %copy.13) | data formatting | bytes 786432 | tf_op jit(solution)/shard_map/reshape;reshape | solution.py:71
  148.9 19.5 %fusion.81 = f32[3,64,128]{2,1,0:T(8,128)S(1)} fusion(f32[3,64,2,128,2]{4,3,2,1,0:T(8,128)} %reshape_reshape.3), kind=kLoop, calls=%fused_computation.157 | loop fusion | flops 98304 | bytes 491520 | tf_op jit(solution)/shard_map/mul | solution.py:72
  168.8 8.2 %collective-permute-done.13 = f32[3,128,64]{2,1,0:T(8,128)S(1)} collective-permute-done((f32[3,128,64]{2,1,0:T(8,128)S(1)}, f32[3,128,64]{2,1,0:T(8,128)S(1)}, u32[]{:S(2)}, u32[]{:S(2)}) %collective-permute-start.13) | collective-permute-done | bytes 98336 | tf_op jit(solution)/shard_map/ppermute | solution.py:32
  180.7 4.7 %collective-permute-start.17 = (f32[3,132,2]{2,1,0:T(8,128)S(1)}, f32[3,132,2]{2,1,0:T(8,128)S(1)}, u32[]{:S(2)}, u32[]{:S(2)}) collective-permute-start(f32[3,132,2]{2,1,0:T(8,128)S(1)} %get-tuple-element.139), channel_id=1, source_target_pairs={{1,0},{2,1},{3,2},{4,3},{5,4},{6,5},{7,6},{0,7},{9,8},{10,9},{11,1... | collective-permute-start | bytes 9512 | tf_op jit(solution)/shard_map/ppermute | solution.py:25
  186.4 3.2 %collective-permute-done.16 = f32[3,132,2]{2,1,0:T(8,128)S(1)} collective-permute-done((f32[3,132,2]{2,1,0:T(8,128)S(1)}, f32[3,132,2]{2,1,0:T(8,128)S(1)}, u32[]{:S(2)}, u32[]{:S(2)}) %collective-permute-start.16) | collective-permute-done | bytes 3200 | tf_op jit(solution)/shard_map/ppermute | solution.py:24
  191.9 2.7 %broadcast_in_dim.96 = f32[66,2,68,2]{3,2,1,0:T(8,128)} broadcast(f32[66,68]{1,0:T(8,128)S(1)} %get-tuple-element.151), dimensions={0,2} | broadcast | bytes 89760 | tf_op jit(solution)/shard_map/broadcast_in_dim | solution.py:157
  194.6 3.6 %broadcast_in_dim.97 = f32[132,136]{1,0:T(8,128)S(1)} reshape(f32[66,2,68,2]{3,2,1,0:T(8,128)} %broadcast_in_dim.96) | data formatting | bytes 143616 | tf_op jit(solution)/shard_map/broadcast_in_dim | solution.py:157
  201.1 3.6 %broadcast_in_dim.99 = f32[132,136]{1,0:T(8,128)S(1)} reshape(f32[66,2,68,2]{3,2,1,0:T(8,128)} %broadcast_in_dim.98) | data formatting | bytes 143616 | tf_op jit(solution)/shard_map/broadcast_in_dim | solution.py:157
  204.9 2.7 %broadcast_in_dim.102 = f32[68,2,68,2]{3,2,1,0:T(8,128)} broadcast(f32[68,68]{1,0:T(8,128)S(1)} %get-tuple-element.154), dimensions={0,2} | broadcast | bytes 92480 | tf_op jit(solution)/shard_map/broadcast_in_dim | solution.py:157
  207.6 3.6 %broadcast_in_dim.103 = f32[136,136]{1,0:T(8,128)S(1)} reshape(f32[68,2,68,2]{3,2,1,0:T(8,128)} %broadcast_in_dim.102) | data formatting | bytes 147968 | tf_op jit(solution)/shard_map/broadcast_in_dim | solution.py:157
  211.4 2.7 %broadcast_in_dim.94 = f32[68,2,68,2]{3,2,1,0:T(8,128)} broadcast(f32[68,68]{1,0:T(8,128)S(1)} %get-tuple-element.153), dimensions={0,2} | broadcast | bytes 92480 | tf_op jit(solution)/shard_map/broadcast_in_dim | solution.py:157
  214.1 3.6 %broadcast_in_dim.95 = f32[136,136]{1,0:T(8,128)S(1)} reshape(f32[68,2,68,2]{3,2,1,0:T(8,128)} %broadcast_in_dim.94) | data formatting | bytes 147968 | tf_op jit(solution)/shard_map/broadcast_in_dim | solution.py:157
  217.9 2.7 %broadcast_in_dim.92 = f32[68,2,68,2]{3,2,1,0:T(8,128)} broadcast(f32[68,68]{1,0:T(8,128)S(1)} %get-tuple-element.152), dimensions={0,2} | broadcast | bytes 92480 | tf_op jit(solution)/shard_map/broadcast_in_dim | solution.py:157
  220.7 3.6 %broadcast_in_dim.93 = f32[136,136]{1,0:T(8,128)S(1)} reshape(f32[68,2,68,2]{3,2,1,0:T(8,128)} %broadcast_in_dim.92) | data formatting | bytes 147968 | tf_op jit(solution)/shard_map/broadcast_in_dim | solution.py:157
  228.8 3.6 %broadcast_in_dim.101 = f32[132,136]{1,0:T(8,128)S(1)} reshape(f32[66,2,68,2]{3,2,1,0:T(8,128)} %broadcast_in_dim.100) | data formatting | bytes 143616 | tf_op jit(solution)/shard_map/broadcast_in_dim | solution.py:157
  (255 shorter events, 53.8 us)
Async XLA Ops:
  1.4 59.5 %collective-permute-start.1 = (f32[3,1,256]{2,1,0:T(1,128)S(1)}, f32[3,1,256]{2,1,0:T(1,128)S(1)}, u32[]{:S(2)}, u32[]{:S(2)}) collective-permute-start(f32[3,1,256]{2,1,0:T(1,128)S(1)} %get-tuple-element.148), channel_id=1, source_target_pairs={{8,0},{16,8},{24,16},{0,24},{9,1},{17,9},{25,17},{1,25},{10,2},{18... | collective-permute-start | bytes 9224 | tf_op jit(solution)/shard_map/ppermute | solution.py:25
  3.8 57.1 %collective-permute-start = (f32[3,1,256]{2,1,0:T(1,128)S(1)}, f32[3,1,256]{2,1,0:T(1,128)S(1)}, u32[]{:S(2)}, u32[]{:S(2)}) collective-permute-start(f32[3,1,256]{2,1,0:T(1,128)S(1)} %get-tuple-element.147), channel_id=1, source_target_pairs={{0,8},{8,16},{16,24},{24,0},{1,9},{9,17},{17,25},{25,1},{2,10},{10... | collective-permute-start | bytes 9224 | tf_op jit(solution)/shard_map/ppermute | solution.py:24
  31.1 21.4 %copy-start = (f32[3,128,256]{2,1,0:T(8,128)S(1)}, f32[3,128,256]{2,1,0:T(8,128)}, u32[]{:S(2)}) copy-start(f32[3,128,256]{2,1,0:T(8,128)} %param.11) | copy-start | bytes 1179652
  31.1 23.5 %copy-start.1 = (s32[1,1,2]{2,1,0:T(1,128)S(1)}, s32[1,1,2]{2,1,0:T(1,128)}, u32[]{:S(2)}) copy-start(s32[1,1,2]{2,1,0:T(1,128)} %param.14) | copy-start | bytes 28
  31.1 24.2 %copy-start.2 = (s32[1,1,2]{2,1,0:T(1,128)S(1)}, s32[1,1,2]{2,1,0:T(1,128)}, u32[]{:S(2)}) copy-start(s32[1,1,2]{2,1,0:T(1,128)} %param.15) | copy-start | bytes 28
  50.7 10.1 %collective-permute-start.9 = (f32[3,1,128]{2,1,0:T(1,128)S(1)}, f32[3,1,128]{2,1,0:T(1,128)S(1)}, u32[]{:S(2)}, u32[]{:S(2)}) collective-permute-start(f32[3,1,128]{2,1,0:T(1,128)S(1)} %get-tuple-element.158), channel_id=1, source_target_pairs={{8,0},{16,8},{24,16},{0,24},{9,1},{17,9},{25,17},{1,25},{10,2},{18... | collective-permute-start | bytes 4616 | tf_op jit(solution)/shard_map/ppermute | solution.py:25
  52.5 8.3 %collective-permute-start.8 = (f32[3,1,128]{2,1,0:T(1,128)S(1)}, f32[3,1,128]{2,1,0:T(1,128)S(1)}, u32[]{:S(2)}, u32[]{:S(2)}) collective-permute-start(f32[3,1,128]{2,1,0:T(1,128)S(1)} %get-tuple-element.157), channel_id=1, source_target_pairs={{0,8},{8,16},{16,24},{24,0},{1,9},{9,17},{17,25},{25,1},{2,10},{10... | collective-permute-start | bytes 4616 | tf_op jit(solution)/shard_map/ppermute | solution.py:24
  52.5 115.8 %collective-permute-start.12 = (f32[3,64,256]{2,1,0:T(8,128)S(1)}, f32[3,64,256]{2,1,0:T(8,128)S(1)}, u32[]{:S(2)}, u32[]{:S(2)}) collective-permute-start(f32[3,64,256]{2,1,0:T(8,128)S(1)} %slice.870), channel_id=1, source_target_pairs={{0,8},{8,16},{16,24},{24,0},{1,9},{9,17},{17,25},{25,1},{2,10},{10... | collective-permute-start | bytes 589832 | tf_op jit(solution)/shard_map/ppermute | solution.py:32
  61.1 9.5 %collective-permute-start.3 = (f32[3,130,1]{2,1,0:T(8,128)S(1)}, f32[3,130,1]{2,1,0:T(8,128)S(1)}, u32[]{:S(2)}, u32[]{:S(2)}) collective-permute-start(f32[3,130,1]{2,1,0:T(8,128)S(1)} %get-tuple-element.144), channel_id=1, source_target_pairs={{1,0},{2,1},{3,2},{4,3},{5,4},{6,5},{7,6},{0,7},{9,8},{10,9},{11,1... | collective-permute-start | bytes 4688 | tf_op jit(solution)/shard_map/ppermute | solution.py:25
  65.7 9.6 %collective-permute-start.2 = (f32[3,130,1]{2,1,0:T(8,128)S(1)}, f32[3,130,1]{2,1,0:T(8,128)S(1)}, u32[]{:S(2)}, u32[]{:S(2)}) collective-permute-start(f32[3,130,1]{2,1,0:T(8,128)S(1)} %get-tuple-element.143), channel_id=1, source_target_pairs={{0,1},{1,2},{2,3},{3,4},{4,5},{5,6},{6,7},{7,0},{8,9},{9,10},{10,1... | collective-permute-start | bytes 4688 | tf_op jit(solution)/shard_map/ppermute | solution.py:24
  65.8 25.0 %collective-permute-start.11 = (f32[3,66,1]{2,1,0:T(8,128)S(1)}, f32[3,66,1]{2,1,0:T(8,128)S(1)}, u32[]{:S(2)}, u32[]{:S(2)}) collective-permute-start(f32[3,66,1]{2,1,0:T(8,128)S(1)} %get-tuple-element.156), channel_id=1, source_target_pairs={{1,0},{2,1},{3,2},{4,3},{5,4},{6,5},{7,6},{0,7},{9,8},{10,9},{11,1... | collective-permute-start | bytes 2384 | tf_op jit(solution)/shard_map/ppermute | solution.py:25
  70.5 20.2 %collective-permute-start.10 = (f32[3,66,1]{2,1,0:T(8,128)S(1)}, f32[3,66,1]{2,1,0:T(8,128)S(1)}, u32[]{:S(2)}, u32[]{:S(2)}) collective-permute-start(f32[3,66,1]{2,1,0:T(8,128)S(1)} %get-tuple-element.155), channel_id=1, source_target_pairs={{0,1},{1,2},{2,3},{3,4},{4,5},{5,6},{6,7},{7,0},{8,9},{9,10},{10,1... | collective-permute-start | bytes 2384 | tf_op jit(solution)/shard_map/ppermute | solution.py:24
  90.0 2.1 collective-permute-start.5
  90.8 3.0 %collective-permute-start.4 = (f32[3,1,256]{2,1,0:T(1,128)S(1)}, f32[3,1,256]{2,1,0:T(1,128)S(1)}, u32[]{:S(2)}, u32[]{:S(2)}) collective-permute-start(f32[3,1,256]{2,1,0:T(1,128)S(1)} %get-tuple-element.145), channel_id=1, source_target_pairs={{0,8},{8,16},{16,24},{24,0},{1,9},{9,17},{17,25},{25,1},{2,10},{10... | collective-permute-start | bytes 9224 | tf_op jit(solution)/shard_map/ppermute | solution.py:24
  94.0 11.7 %collective-permute-start.7 = (f32[3,130,1]{2,1,0:T(8,128)S(1)}, f32[3,130,1]{2,1,0:T(8,128)S(1)}, u32[]{:S(2)}, u32[]{:S(2)}) collective-permute-start(f32[3,130,1]{2,1,0:T(8,128)S(1)} %get-tuple-element.142), channel_id=1, source_target_pairs={{1,0},{2,1},{3,2},{4,3},{5,4},{6,5},{7,6},{0,7},{9,8},{10,9},{11,1... | collective-permute-start | bytes 4688 | tf_op jit(solution)/shard_map/ppermute | solution.py:25
  99.1 9.2 %collective-permute-start.6 = (f32[3,130,1]{2,1,0:T(8,128)S(1)}, f32[3,130,1]{2,1,0:T(8,128)S(1)}, u32[]{:S(2)}, u32[]{:S(2)}) collective-permute-start(f32[3,130,1]{2,1,0:T(8,128)S(1)} %get-tuple-element.141), channel_id=1, source_target_pairs={{0,1},{1,2},{2,3},{3,4},{4,5},{5,6},{6,7},{7,0},{8,9},{9,10},{10,1... | collective-permute-start | bytes 4688 | tf_op jit(solution)/shard_map/ppermute | solution.py:24
  168.6 8.4 %collective-permute-start.13 = (f32[3,128,64]{2,1,0:T(8,128)S(1)}, f32[3,128,64]{2,1,0:T(8,128)S(1)}, u32[]{:S(2)}, u32[]{:S(2)}) collective-permute-start(f32[3,128,64]{2,1,0:T(8,128)S(1)} %fusion.85), channel_id=1, source_target_pairs={{0,1},{1,2},{2,3},{3,4},{4,5},{5,6},{6,7},{7,0},{8,9},{9,10},{10,1... | collective-permute-start | bytes 294920 | tf_op jit(solution)/shard_map/ppermute | solution.py:32
  177.2 1.4 collective-permute-start.15
  177.3 3.1 %collective-permute-start.14 = (f32[3,2,256]{2,1,0:T(2,128)S(1)}, f32[3,2,256]{2,1,0:T(2,128)S(1)}, u32[]{:S(2)}, u32[]{:S(2)}) collective-permute-start(f32[3,2,256]{2,1,0:T(2,128)S(1)} %get-tuple-element.129), channel_id=1, source_target_pairs={{0,8},{8,16},{16,24},{24,0},{1,9},{9,17},{17,25},{25,1},{2,10},{10... | collective-permute-start | bytes 18440 | tf_op jit(solution)/shard_map/ppermute | solution.py:24
  180.7 8.9 %collective-permute-start.16 = (f32[3,132,2]{2,1,0:T(8,128)S(1)}, f32[3,132,2]{2,1,0:T(8,128)S(1)}, u32[]{:S(2)}, u32[]{:S(2)}) collective-permute-start(f32[3,132,2]{2,1,0:T(8,128)S(1)} %get-tuple-element.140), channel_id=1, source_target_pairs={{0,1},{1,2},{2,3},{3,4},{4,5},{5,6},{6,7},{7,0},{8,9},{9,10},{10,1... | collective-permute-start | bytes 9512 | tf_op jit(solution)/shard_map/ppermute | solution.py:24
  180.7 10.8 %collective-permute-start.17 = (f32[3,132,2]{2,1,0:T(8,128)S(1)}, f32[3,132,2]{2,1,0:T(8,128)S(1)}, u32[]{:S(2)}, u32[]{:S(2)}) collective-permute-start(f32[3,132,2]{2,1,0:T(8,128)S(1)} %get-tuple-element.139), channel_id=1, source_target_pairs={{1,0},{2,1},{3,2},{4,3},{5,4},{6,5},{7,6},{0,7},{9,8},{10,9},{11,1... | collective-permute-start | bytes 9512 | tf_op jit(solution)/shard_map/ppermute | solution.py:25
where the time goes:
time: 237 us; the launch traced here: 236 us
  local copies, waits for them, and re-layouts  107 us (45%)
  other arithmetic  56.4 us (24%)
  starting transfers between devices  25.7 us (11%)
  waiting for transfers between devices  25.6 us (11%)
  loops' own time  14 us (6%)
  between operations  7.44 us (3%)
    mul x2, other arithmetic, coarsen(): 0.25 * (shaped[:, :, 0, :, 0] + shaped[:, :, 1, :, 0] + shaped[:, :, 0, :...  39.1 us
    broadcast_in_dim x12, local copies, waits for them, and re-layouts, refine_patch(): jnp.broadcast_to(region[:, :, None, :, None], (3, PATCH + 4, 2, PATCH + 4...  37.7 us
    reshape x1, local copies, waits for them, and re-layouts, coarsen(): cells.reshape(cells.shape[0], cells.shape[1] // 2, 2, cells.shape[2] // 2...  27.3 us
    another operation x1, local copies, waits for them, and re-layouts, coarsen(): cells.reshape(cells.shape[0], cells.shape[1] // 2, 2, cells.shape[2] // 2...  26.6 us
    ppermute x8, starting transfers between devices, with_halo(): after = lax.ppermute(first, axis, down)  24.3 us
    ppermute x8, waiting for transfers between devices, with_halo(): before = lax.ppermute(last, axis, up)  14.1 us
    another operation x3, loops' own time, by_blocks(): stacked = lax.map(one_block, jnp.arange(count, dtype=jnp.int32))  14 us
    dynamic_slice x20, local copies, waits for them, and re-layouts, by_blocks(): stacked = lax.map(one_block, jnp.arange(count, dtype=jnp.int32))  12.2 us
  transfers between devices with their start and end apart: 18, of which 9 were waited for; matrix products, arithmetic and copies ran while one was open for 50% of the time, Pallas kernels for 0%

commit v1 on v0

v1 whole, which is shorter than its diff:
```python
import jax
import jax.numpy as jnp
from jax import lax
from jax.experimental import pallas as pl
from jax.experimental.pallas import tpu as pltpu
from jax.sharding import PartitionSpec as P

SLAB = 64
PATCH = 64
LANES = 128

RATIO = 0.1
ERR_SCALE = 10.0

RIGHT_ROWS, RIGHT_COLS, LEFT_ROWS, LEFT_COLS, OWN_ROWS, OWN_COLS = 6, 7, 8, 9, 10, 11

VMEM = pl.BlockSpec(memory_space=pltpu.VMEM)
SMEM = pl.BlockSpec(memory_space=pltpu.SMEM)
PARAMS = pltpu.CompilerParams(vmem_limit_bytes=32 * 1024 * 1024)


def f32(*shape):
    return jax.ShapeDtypeStruct(shape, jnp.float32)


def lane_ids(rows, width=LANES):
    return lax.broadcasted_iota(jnp.int32, (rows, width), 1)


def row_ids(rows, width=LANES):
    return lax.broadcasted_iota(jnp.int32, (rows, width), 0)


def roll(value, by, axis):
    return pltpu.roll(value, by % value.shape[axis], axis)


def cell_terms(depth, first, second):
    inverse_root = lax.rsqrt(depth)
    wave = depth * inverse_root
    inverse = inverse_root * inverse_root
    first_vel = first * inverse
    second_vel = second * inverse
    pressure = 0.5 * depth * depth
    cross = first * second_vel
    row_terms = (first, first * first_vel + pressure, cross, jnp.abs(first_vel) + wave)
    col_terms = (second, cross, second * second_vel + pressure, jnp.abs(second_vel) + wave)
    return row_terms, col_terms


def doubled_flux(left, right, left_terms, right_terms):
    speed = jnp.maximum(left_terms[3], right_terms[3])
    return [(left_terms[c] + right_terms[c]) - speed * (right[c] - left[c]) for c in range(3)]


def spread_step(fields, row_by, col_by):
    row_terms, col_terms = cell_terms(*fields)
    total = None
    for terms, by, axis in ((row_terms, row_by, 0), (col_terms, col_by, 1)):
        lower = [roll(f, by, axis) for f in fields]
        momentum = lower[1 + axis]
        lower_terms = [momentum if c == 0 else roll(terms[c], by, axis) for c in range(4)]
        flux = doubled_flux(lower, fields, lower_terms, terms)
        change = [roll(f, -by, axis) - f for f in flux]
        total = change if total is None else [t + c for t, c in zip(total, change)]
    return [f - (0.5 * RATIO) * t for f, t in zip(fields, total)]


def block_sum(field):
    pair = field + roll(field, -1, 0)
    return pair + roll(pair, -1, 1)


def error_rows(fields, halved):
    fine_two = spread_step(spread_step(fields, 1, 1), 1, 1)
    coarse_one = spread_step([0.25 * block_sum(f) for f in fields], 2, 2)
    total = None
    for fine, coarse in zip(fine_two, coarse_one):
        part = jnp.abs(0.25 * block_sum(fine) - coarse)
        total = part if total is None else total + part
    total = ERR_SCALE * total
    halved[0] = total[4:20, 0:LANES]
    halved[1] = total[4:20, LANES : 2 * LANES]
    lanes = lane_ids(8)
    even = (2 * lanes) % LANES
    low = jnp.take_along_axis(halved[0, pl.ds(0, 8, stride=2), :], even, axis=1)
    high = jnp.take_along_axis(halved[1, pl.ds(0, 8, stride=2), :], even, axis=1)
    return jnp.where(lanes < LANES // 2, low, high)


def pack_cols(row_count, col_count, last_ref, first_ref, left_ref, right_ref):
    rows = last_ref.shape[1]
    half = rows // 2
    rc = row_count[0, 0].astype(jnp.float32)
    cc = col_count[0, 0].astype(jnp.float32)
    lanes = lane_ids(half)
    for comp in range(3):
        upper = last_ref[comp, 0:half, :]
        lower = roll(last_ref[comp, half:rows, :], LANES // 2, 1)
        left_ref[comp, 0:half, :] = jnp.where(lanes >= LANES // 2, upper, lower)
        left_ref[comp, half : half + 8, :] = jnp.where(lane_ids(8) == LEFT_ROWS, rc, cc)
    lanes = lane_ids(rows)
    packed = jnp.where(lanes == RIGHT_ROWS, rc, cc)
    for comp in (2, 1, 0):
        packed = jnp.where(lanes < 2 * comp + 2, roll(first_ref[comp], 2 * comp, 1), packed)
    right_ref[...] = packed.T[0:8]


def pack_rows(row_count, col_count, left_ref, right_ref, state_ref, rim_ref, down_ref, up_ref):
    rows, cols = state_ref.shape[1], state_ref.shape[2]
    half = rows // 2
    rc = row_count[0, 0].astype(jnp.float32)
    cc = col_count[0, 0].astype(jnp.float32)
    right = jnp.concatenate([right_ref[...], jnp.zeros((LANES - 8, LANES), jnp.float32)], axis=0).T
    lanes = lane_ids(rows)
    from_left = (lanes == LEFT_ROWS) | (lanes == LEFT_COLS)
    counts = jnp.where(from_left, left_ref[0, half : half + 1, :], jnp.where(lanes == OWN_ROWS, rc, cc))
    for comp in range(3):
        packed = left_ref[comp, 0:half, :]
        left = jnp.concatenate([packed, roll(packed, LANES // 2, 1)], axis=0)
        inner = right if comp == 0 else roll(right, -2 * comp, 1)
        inner = jnp.where(lanes < LEFT_ROWS, inner, counts)
        rim = jnp.where(lanes >= LANES // 2, left, inner)
        rim_ref[comp] = rim
        down_ref[comp, :, 0:cols] = state_ref[comp, rows - SLAB : rows, :]
        down_ref[comp, :, cols : cols + LANES] = rim[rows - SLAB : rows]
        up_ref[comp, :, 0:cols] = state_ref[comp, 0:8, :]
        up_ref[comp, :, cols : cols + LANES] = rim[0:8]


def inner_error(state_ref, rim_ref, error_ref, halved):
    blocks = state_ref.shape[1] // 16

    def one(block, carry):
        start = pl.multiple_of(16 * block - 8, 8)
        fields = [
            jnp.concatenate(
                [state_ref[c, pl.ds(start, 32), :][4:28], rim_ref[c, pl.ds(start, 32), :][4:28]], axis=1
            )
            for c in range(3)
        ]
        error_ref[pl.ds(pl.multiple_of(8 * block, 8), 8), :] = error_rows(fields, halved)
        return carry

    lax.fori_loop(1, blocks - 1, one, 0)


def minmod(lower_diff, upper_diff):
    return jnp.maximum(jnp.minimum(lower_diff, upper_diff), 0.0) + jnp.minimum(
        jnp.maximum(lower_diff, upper_diff), 0.0
    )


def paired_change(near, far, axis):
    down = lambda v: roll(v, 1, axis)
    up = lambda v: roll(v, -1, axis)
    inner = [f - n for n, f in zip(near, far)]
    outer = [n - down(f) for n, f in zip(near, far)]
    near_half = [0.5 * minmod(o, i) for o, i in zip(outer, inner)]
    far_half = [0.5 * minmod(i, up(o)) for o, i in zip(outer, inner)]
    near_hi = [n + s for n, s in zip(near, near_half)]
    near_lo = [n - s for n, s in zip(near, near_half)]
    far_hi = [down(f + s) for f, s in zip(far, far_half)]
    far_lo = [f - s for f, s in zip(far, far_half)]
    terms = lambda cells: cell_terms(*cells)[axis]
    inner_flux = doubled_flux(near_hi, far_lo, terms(near_hi), terms(far_lo))
    outer_flux = doubled_flux(far_hi, near_lo, terms(far_hi), terms(near_lo))
    near_change = [i - o for i, o in zip(inner_flux, outer_flux)]
    far_change = [up(o) - i for i, o in zip(inner_flux, outer_flux)]
    return near_change, far_change


def doubled_first_step(cells):
    all_terms = cell_terms(*cells)
    changes = []
    for axis in (0, 1):
        terms = all_terms[axis]
        lower = [roll(f, 1, axis) for f in cells]
        lower_terms = [lower[1 + axis] if c == 0 else roll(terms[c], 1, axis) for c in range(4)]
        flux = doubled_flux(lower, cells, lower_terms, terms)
        own = [2.0 * terms[c] for c in range(3)]
        changes.append(
            (
                [o - f for o, f in zip(own, flux)],
                [roll(f, -1, axis) - o for o, f in zip(own, flux)],
            )
        )
    rows, cols = changes
    return [
        [
            [cells[c] - (0.5 * RATIO) * (rows[a][c] + cols[b][c]) for c in range(3)]
            for b in range(2)
        ]
        for a in range(2)
    ]


def patch_rows(cells):
    half = doubled_first_step(cells)
    by_row = [paired_change(half[0][b], half[1][b], 0) for b in range(2)]
    by_col = [paired_change(half[a][0], half[a][1], 1) for a in range(2)]
    lanes = lane_ids(16)
    result = []
    for a in range(2):
        fine = [
            [half[a][b][c] - (0.5 * RATIO) * (by_row[b][a][c] + by_col[a][b][c]) for c in range(3)]
            for b in range(2)
        ]
        parts = []
        for c in range(3):
            pick = lanes // 2 + 2
            even = jnp.take_along_axis(fine[0][c][4:20], pick, axis=1)
            odd = jnp.take_along_axis(fine[1][c][4:20], pick, axis=1)
            parts.append(jnp.where(lanes % 2 == 0, even, odd))
        result.append(parts)
    return result


def finish(
    row_count, col_count, patch_pos, patch_ext, state_ref, rim_ref, above_ref, below_ref, inner_ref,
    error_ref, moved_ref, patch_ref, edge, wide, window, halved,
):
    rows, cols = state_ref.shape[1], state_ref.shape[2]
    slab = slice(rows - SLAB, rows)
    top = slice(0, SLAB)
    right = slice(cols, cols + LANES)
    last = slice(cols - LANES, cols)

    rim_counts = rim_ref[0, 0:8, :]
    above_counts = above_ref[0, 0:8, right]
    below_counts = below_ref[0, 0:8, right]
    get = lambda counts, lane: counts[0, lane].astype(jnp.int32)
    rc, cc = row_count[0, 0], col_count[0, 0]
    rc_left, rc_right, cc_right = [get(rim_counts, k) for k in (LEFT_ROWS, RIGHT_ROWS, RIGHT_COLS)]
    cc_above, cc_above_right = [get(above_counts, k) for k in (OWN_COLS, RIGHT_COLS)]
    rc_below, cc_below, rc_below_left, rc_below_right, cc_below_right = [
        get(below_counts, k) for k in (OWN_ROWS, OWN_COLS, LEFT_ROWS, RIGHT_ROWS, RIGHT_COLS)
    ]

    for comp in range(3):
        edge[0, comp, 0:8, :] = above_ref[comp, SLAB - 8 : SLAB, :]
        edge[0, comp, 8:32, 0:cols] = state_ref[comp, 0:24, :]
        edge[0, comp, 8:32, right] = rim_ref[comp, 0:24, :]
        edge[1, comp, 0:24, 0:cols] = state_ref[comp, rows - 24 : rows, :]
        edge[1, comp, 0:24, right] = rim_ref[comp, rows - 24 : rows, :]
        edge[1, comp, 24:32, :] = below_ref[comp, :, :]

    half_rows = error_ref.shape[0]
    error_ref[8 : half_rows - 8, :] = inner_ref[8 : half_rows - 8, :]

    def edge_error(side, carry):
        fields = [edge[side, c][4:28] for c in range(3)]
        start = pl.multiple_of(side * (half_rows - 8), 8)
        error_ref[pl.ds(start, 8), :] = error_rows(fields, halved)
        return carry

    lax.fori_loop(0, 2, edge_error, 0)

    def moved_rows(own, own_rim, slab_rows, slab_rim, counts):
        here, left, right_count = counts
        size = own.shape[0]
        aligned = roll_by(slab_rows, here)[0:size]
        lanes, ids = lane_ids(size), row_ids(size)
        body = jnp.where(row_ids(size, cols) < here, aligned, own)
        on_left = lanes >= LANES // 2
        side = jnp.where(on_left, roll_by(slab_rim, left)[0:size], roll_by(slab_rim, right_count)[0:size])
        taken = ids < jnp.where(on_left, left, right_count)
        return body, jnp.where(taken, side, own_rim)

    def roll_by(value, by):
        return pltpu.roll(value, by & (SLAB - 1), 0)

    def moved_cols(body, rim, here, right_count):
        lanes = lane_ids(rim.shape[0])
        first = jnp.where(lanes < here, pltpu.roll(rim, here, 1), body[:, 0:LANES])
        outer = jnp.where(lanes < right_count, pltpu.roll(body[:, cols - LANES : cols], right_count, 1), rim)
        return first, body[:, LANES:cols], jnp.where(lanes >= LANES // 2, rim, outer)

    for comp in range(3):
        own, own_rim = state_ref[comp, :, :], rim_ref[comp, :, :]
        body, side = moved_rows(
            own[top], own_rim[top], above_ref[comp, :, 0:cols], above_ref[comp, :, right], (rc, rc_left, rc_right)
        )
        for part, body, side in (
            (top, body, side),
            (slice(SLAB, rows), own[SLAB:rows], own_rim[SLAB:rows]),
        ):
            first, second, outer = moved_cols(body, side, cc, cc_right)
            moved_ref[comp, part, 0:LANES] = first
            moved_ref[comp, part, LANES:cols] = second
            at = slice(part.start + 8, part.stop + 8)
            wide[comp, at, 0:LANES] = first
            wide[comp, at, LANES:cols] = second
            wide[comp, at, right] = outer
        first, second, outer = moved_cols(
            above_ref[comp, SLAB - 8 : SLAB, 0:cols], above_ref[comp, SLAB - 8 : SLAB, right], cc_above, cc_above_right
        )
        wide[comp, 0:8, 0:LANES] = first
        wide[comp, 0:8, LANES:cols] = second
        wide[comp, 0:8, right] = outer
        body, side = moved_rows(
            below_ref[comp, :, 0:cols], below_ref[comp, :, right], own[slab], own_rim[slab],
            (rc_below, rc_below_left, rc_below_right),
        )
        first, second, outer = moved_cols(body, side, cc_below, cc_below_right)
        wide[comp, rows + 8 : rows + 16, 0:LANES] = first
        wide[comp, rows + 8 : rows + 16, LANES:cols] = second
        wide[comp, rows + 8 : rows + 16, right] = outer

    row_start = patch_pos[0, 0, 0] + 4
    base = pl.multiple_of(row_start // 8 * 8, 8)
    width = cols + LANES
    for comp in range(3):
        near = wide[comp, pl.ds(base, 80), :]
        near = pltpu.roll(near, (80 - (row_start - base)) % 80, 0)
        near = pltpu.roll(near, (width + 2 - patch_pos[0, 0, 1]) % width, 1)
        window[comp, :, :] = near[0:72, 0:LANES]

    fine_rows, fine_cols = 2 * patch_ext[0, 0, 0], 2 * patch_ext[0, 0, 1]

    def patch_block(block, carry):
        start = pl.multiple_of(16 * block, 8)
        cells = [window[c, pl.ds(start, 24), :] for c in range(3)]
        fine = patch_rows(cells)
        lanes, ids = lane_ids(16), row_ids(16)
        for a in range(2):
            inside = (2 * (ids + start) + a < fine_rows) & (lanes < fine_cols)
            for c in range(3):
                patch_ref[c, pl.ds(2 * start + a, 16, stride=2), :] = jnp.where(inside, fine[a][c], 0.0)
        return carry

    lax.fori_loop(0, PATCH // 16, patch_block, 0)


def around(axis, by):
    devices = lax.axis_size(axis)
    return [(i, (i + by) % devices) for i in range(devices)]


def per_device(state, row_count, col_count, patch_pos, patch_ext):
    rows, cols = state.shape[1], state.shape[2]
    width = cols + LANES
    first_tile = pl.BlockSpec((3, rows, LANES), lambda i: (0, 0, 0))
    last_tile = pl.BlockSpec((3, rows, LANES), lambda i: (0, 0, cols // LANES - 1))
    to_right, to_left = pl.pallas_call(
        pack_cols,
        grid=(1,),
        out_shape=(f32(3, rows // 2 + 8, LANES), f32(8, LANES)),
        in_specs=[SMEM, SMEM, last_tile, first_tile],
        out_specs=(VMEM, VMEM),
        name="pack_cols",
    )(row_count, col_count, state, state)
    from_left = lax.ppermute(to_right, "col", around("col", 1))
    from_right = lax.ppermute(to_left, "col", around("col", -1))
    rim, to_below, to_above = pl.pallas_call(
        pack_rows,
        out_shape=(f32(3, rows, LANES), f32(3, SLAB, width), f32(3, 8, width)),
        in_specs=[SMEM, SMEM, VMEM, VMEM, VMEM],
        out_specs=(VMEM, VMEM, VMEM),
        name="pack_rows",
    )(row_count, col_count, from_left, from_right, state)
    from_above = lax.ppermute(to_below, "row", around("row", 1))
    from_below = lax.ppermute(to_above, "row", around("row", -1))
    inner = pl.pallas_call(
        inner_error,
        out_shape=f32(rows // 2, cols // 2),
        in_specs=[VMEM, VMEM],
        out_specs=VMEM,
        scratch_shapes=[pltpu.VMEM((2, 16, LANES), jnp.float32)],
        cost_estimate=pl.CostEstimate(flops=30_000_000, bytes_accessed=600_000, transcendentals=0),
        name="inner_error",
    )(state, rim)
    return pl.pallas_call(
        finish,
        out_shape=(f32(rows // 2, cols // 2), f32(3, rows, cols), f32(3, 2 * PATCH, 2 * PATCH)),
        in_specs=[SMEM] * 4 + [VMEM] * 5,
        out_specs=(VMEM, VMEM, VMEM),
        scratch_shapes=[
            pltpu.VMEM((2, 3, 32, width), jnp.float32),
            pltpu.VMEM((3, rows + 16, width), jnp.float32),
            pltpu.VMEM((3, 72, LANES), jnp.float32),
            pltpu.VMEM((2, 16, LANES), jnp.float32),
        ],
        compiler_params=PARAMS,
        name="finish",
    )(row_count, col_count, patch_pos, patch_ext, state, rim, from_above, from_below, inner)


def solution(mesh):
    placed = (
        P(None, "row", "col"),
        P("row", "col"),
        P("row", "col"),
        P("row", "col", None),
        P("row", "col", None),
    )
    return jax.shard_map(
        per_device,
        mesh=mesh,
        in_specs=placed,
        out_specs=(P("row", "col"), P(None, "row", "col"), P(None, "row", "col")),
        check_vma=False,
    )
```

time: 237 us -> 30.3 us (0.13)
  local copies, waits for them, and re-layouts: 107 us -> 1.4 us
  other arithmetic: 56.4 us -> 0 us
  waiting for transfers between devices: 25.6 us -> 3.26 us
  starting transfers between devices: 25.7 us -> 7.73 us
  Pallas kernels: 0 us -> 15.7 us
  loops' own time: 14 us -> 0 us
  between operations: 7.44 us -> 1.97 us
    mul x3 -> x0, other arithmetic: 39.7 us -> none  [the longest x2 39.1 us: coarsen(): 0.25 * (shaped[:, :, 0, :, 0] + shaped[:, :, 1, :, 0] + shaped[:, :, 0, :...]
    broadcast_in_dim x12 -> x0, local copies, waits for them, and re-layouts: 37.7 us -> none  [refine_patch(): jnp.broadcast_to(region[:, :, None, :, None], (3, PATCH + 4, 2, PATCH + 4...]
    reshape x1 -> x0, local copies, waits for them, and re-layouts: 27.3 us -> none  [coarsen(): cells.reshape(cells.shape[0], cells.shape[1] // 2, 2, cells.shape[2] // 2...]
    another operation x3 -> x0, local copies, waits for them, and re-layouts: 26.6 us -> none  [the longest x1 26.6 us: coarsen(): cells.reshape(cells.shape[0], cells.shape[1] // 2, 2, cells.shape[2] // 2...]
    ppermute x18 -> x4, waiting for transfers between devices: 25.6 us -> 3.26 us  [the longest x1 1.72 us: per_device(): from_left = lax.ppermute(to_right, 'col', around('col', 1))]
    ppermute x18 -> x4, starting transfers between devices: 25.7 us -> 7.73 us  [the longest x1 3.04 us: per_device(): from_right = lax.ppermute(to_left, 'col', around('col', -1))]
    pallas_call x0 -> x4, Pallas kernels: none -> 15.7 us  [the longest x1 6.41 us: per_device(): pl.pallas_call(inner_error, out_shape=f32(rows // 2, cols // 2), in_specs...]
    another operation x3 -> x0, loops' own time: 14 us -> none  [by_blocks(): stacked = lax.map(one_block, jnp.arange(count, dtype=jnp.int32))]
  transfers between devices with their start and end apart: 18 -> 4, of which waited for: 9 -> 2; matrix products, arithmetic and copies ran while one was open for 50% -> 0% of each run, Pallas kernels for 0% -> 21%
where the time goes in v1:
time: 30.3 us; the launch traced here: 30.1 us
  Pallas kernels  15.7 us (52%)
  starting transfers between devices  7.73 us (26%)
  waiting for transfers between devices  3.26 us (11%)
  between operations  1.97 us (7%)
  local copies, waits for them, and re-layouts  1.4 us (5%)
    pallas_call x1, Pallas kernels, per_device(): pl.pallas_call(inner_error, out_shape=f32(rows // 2, cols // 2), in_specs...  6.41 us
    pallas_call x1, Pallas kernels, per_device(): pl.pallas_call(finish, out_shape=(f32(rows // 2, cols // 2), f32(3, rows,...  5.47 us
    ppermute x1, starting transfers between devices, per_device(): from_right = lax.ppermute(to_left, 'col', around('col', -1))  3.04 us
    ppermute x1, starting transfers between devices, per_device(): from_left = lax.ppermute(to_right, 'col', around('col', 1))  2.94 us
    pallas_call x1, Pallas kernels, per_device(): pl.pallas_call(pack_rows, out_shape=(f32(3, rows, LANES), f32(3, SLAB, wi...  2.04 us
    pallas_call x1, Pallas kernels, per_device(): pl.pallas_call(pack_cols, grid=(1,), out_shape=(f32(3, rows // 2 + 8, LAN...  1.8 us
    ppermute x1, starting transfers between devices, per_device(): from_below = lax.ppermute(to_above, 'row', around('row', -1))  1.74 us
    ppermute x1, waiting for transfers between devices, per_device(): from_left = lax.ppermute(to_right, 'col', around('col', 1))  1.72 us
  transfers between devices with their start and end apart: 4, of which 2 were waited for; matrix products, arithmetic and copies ran while one was open for 0% of the time, Pallas kernels for 21%

profile of v1, /device:TPU:0, one launch (start us, length us, event | category | flops | bytes accessed | tf_op | source)
XLA Modules:
  0.0 30.1 jit_solution(769651831799899385)
XLA Ops:
  1.9 1.8 %pack_cols.1 = (f32[3,72,128]{2,1,0:T(8,128)}, f32[8,128]{1,0:T(8,128)}) custom-call(s32[1,1]{1,0:T(1,128)S(6)} %copy.8.row_count, s32[1,1]{1,0:T(1,128)S(6)} %copy.9.col_count, f32[3,128,256]{2,1,0:T(8,128)} %state_ref.5, f32[3,128,256]{2,1,0:T(8,128)} %state_ref.5), custom_call_target="tpu_custom_call" | custom-call | tf_op jit(solution)/shard_map/pack_cols/pallas_call | solution.py:345
  3.7 2.9 %collective-permute-start = (f32[3,72,128]{2,1,0:T(8,128)}, f32[3,72,128]{2,1,0:T(8,128)S(1)}, u32[]{:S(2)}, u32[]{:S(2)}) collective-permute-start(f32[3,72,128]{2,1,0:T(8,128)} %get-tuple-element.8), channel_id=1, source_target_pairs={{0,1},{1,2},{2,3},{3,4},{4,5},{5,6},{6,7},{7,0},{8,9},{9,10},{10,1... | collective-permute-start | bytes 331784 | tf_op jit(solution)/shard_map/ppermute | solution.py:353
  6.7 3.0 %collective-permute-start.1 = (f32[8,128]{1,0:T(8,128)}, f32[8,128]{1,0:T(8,128)S(1)}, u32[]{:S(2)}, u32[]{:S(2)}) collective-permute-start(f32[8,128]{1,0:T(8,128)} %get-tuple-element.9), channel_id=1, source_target_pairs={{0,7},{1,0},{2,1},{3,2},{4,3},{5,4},{6,5},{7,6},{8,15},{9,8},{10,9... | collective-permute-start | bytes 12296 | tf_op jit(solution)/shard_map/ppermute | solution.py:354
  9.7 1.5 %collective-permute-done.1.right_ref = f32[8,128]{1,0:T(8,128)S(1)} collective-permute-done((f32[8,128]{1,0:T(8,128)}, f32[8,128]{1,0:T(8,128)S(1)}, u32[]{:S(2)}, u32[]{:S(2)}) %collective-permute-start.1) | collective-permute-done | bytes 4128 | tf_op jit(solution)/shard_map/ppermute | solution.py:354
  11.2 0.0 copy-start.6
  11.2 1.7 %collective-permute-done.left_ref = f32[3,72,128]{2,1,0:T(8,128)S(1)} collective-permute-done((f32[3,72,128]{2,1,0:T(8,128)}, f32[3,72,128]{2,1,0:T(8,128)S(1)}, u32[]{:S(2)}, u32[]{:S(2)}) %collective-permute-start) | collective-permute-done | bytes 110624 | tf_op jit(solution)/shard_map/ppermute | solution.py:353
  13.0 0.0 copy-done.6
  13.0 0.0 copy-start.5
  13.0 0.6 %copy-done.5 = f32[3,72,128]{2,1,0:T(8,128)} copy-done((f32[3,72,128]{2,1,0:T(8,128)}, f32[3,72,128]{2,1,0:T(8,128)S(1)}, u32[]{:S(2)}) %copy-start.5) | copy-done | bytes 110616
  13.6 2.0 %pack_rows.1 = (f32[3,128,128]{2,1,0:T(8,128)}, f32[3,64,384]{2,1,0:T(8,128)}, f32[3,8,384]{2,1,0:T(8,128)}) custom-call(s32[1,1]{1,0:T(1,128)S(6)} %copy.8.row_count, s32[1,1]{1,0:T(1,128)S(6)} %copy.9.col_count, f32[3,72,128]{2,1,0:T(8,128)} %copy-done.5, f32[8,128]{1,0:T(8,128)} %copy-done.6, f32[3,128,256]{2,1,0:T(8,128)} %state_ref.5), custom_call_target="tpu_custom_call" | custom-call | tf_op jit(solution)/shard_map/pack_rows/pallas_call | solution.py:355
  15.6 0.0 copy-start
  15.6 0.0 collective-permute-start.2
  15.6 1.7 %collective-permute-start.3 = (f32[3,8,384]{2,1,0:T(8,128)}, f32[3,8,384]{2,1,0:T(8,128)S(1)}, u32[]{:S(2)}, u32[]{:S(2)}) collective-permute-start(f32[3,8,384]{2,1,0:T(8,128)} %get-tuple-element.12), channel_id=1, source_target_pairs={{0,24},{8,0},{16,8},{24,16},{1,25},{9,1},{17,9},{25,17},{2,26},{10... | collective-permute-start | bytes 110600 | tf_op jit(solution)/shard_map/ppermute | solution.py:363
  17.4 0.0 copy-start.1
  17.4 6.4 %inner_error.1.inner_ref = f32[64,128]{1,0:T(8,128)} custom-call(f32[3,128,256]{2,1,0:T(8,128)} %state_ref.5, f32[3,128,128]{2,1,0:T(8,128)} %get-tuple-element.10.rim_ref), custom_call_target="tpu_custom_call" | custom-call | flops 30000000 | bytes 600000 | tf_op jit(solution)/shard_map/inner_error/pallas_call | solution.py:364
  23.8 0.0 collective-permute-done.3.below_ref
  23.8 0.0 collective-permute-done.2.above_ref
  23.8 0.0 copy-done
  23.8 0.0 copy-done.1
  23.8 0.0 copy-done.3
  23.8 0.0 copy-done.4
  23.8 0.0 copy-start.2
  23.9 0.7 %copy-done.2 = f32[64,128]{1,0:T(8,128)S(1)} copy-done((f32[64,128]{1,0:T(8,128)S(1)}, f32[64,128]{1,0:T(8,128)}, u32[]{:S(2)}) %copy-start.2) | copy-done | bytes 32792
  24.6 5.5 %finish.1 = (f32[64,128]{1,0:T(8,128)}, f32[3,128,256]{2,1,0:T(8,128)}, f32[3,128,128]{2,1,0:T(8,128)}) custom-call(s32[1,1]{1,0:T(1,128)S(6)} %copy.8.row_count, s32[1,1]{1,0:T(1,128)S(6)} %copy.9.col_count, s32[1,1,2]{2,1,0:T(1,128)S(1)} %copy-done.3, s32[1,1,2]{2,1,0:T(1,128)S(1)} %copy-done.4, f32[3,128,256]{2,1,0:T(8,128)S(1)} %copy-done, ...), custom_call_target="tpu_custom_call" | custom-call | tf_op jit(solution)/shard_map/finish/pallas_call | solution.py:373
  (2 shorter events, 0.0 us)
Async XLA Ops:
  3.7 9.2 %collective-permute-start = (f32[3,72,128]{2,1,0:T(8,128)}, f32[3,72,128]{2,1,0:T(8,128)S(1)}, u32[]{:S(2)}, u32[]{:S(2)}) collective-permute-start(f32[3,72,128]{2,1,0:T(8,128)} %get-tuple-element.8), channel_id=1, source_target_pairs={{0,1},{1,2},{2,3},{3,4},{4,5},{5,6},{6,7},{7,0},{8,9},{9,10},{10,1... | collective-permute-start | bytes 331784 | tf_op jit(solution)/shard_map/ppermute | solution.py:353
  6.7 4.6 %collective-permute-start.1 = (f32[8,128]{1,0:T(8,128)}, f32[8,128]{1,0:T(8,128)S(1)}, u32[]{:S(2)}, u32[]{:S(2)}) collective-permute-start(f32[8,128]{1,0:T(8,128)} %get-tuple-element.9), channel_id=1, source_target_pairs={{0,7},{1,0},{2,1},{3,2},{4,3},{5,4},{6,5},{7,6},{8,15},{9,8},{10,9... | collective-permute-start | bytes 12296 | tf_op jit(solution)/shard_map/ppermute | solution.py:354
  11.2 1.7 %copy-start.6 = (f32[8,128]{1,0:T(8,128)}, f32[8,128]{1,0:T(8,128)S(1)}, u32[]{:S(2)}) copy-start(f32[8,128]{1,0:T(8,128)S(1)} %collective-permute-done.1.right_ref) | copy-start | bytes 12292
  13.0 0.6 %copy-start.5 = (f32[3,72,128]{2,1,0:T(8,128)}, f32[3,72,128]{2,1,0:T(8,128)S(1)}, u32[]{:S(2)}) copy-start(f32[3,72,128]{2,1,0:T(8,128)S(1)} %collective-permute-done.left_ref) | copy-start | bytes 331780
  15.6 8.2 %copy-start = (f32[3,128,256]{2,1,0:T(8,128)S(1)}, f32[3,128,256]{2,1,0:T(8,128)}, u32[]{:S(2)}) copy-start(f32[3,128,256]{2,1,0:T(8,128)} %state_ref.5) | copy-start | bytes 1179652
  15.6 8.2 %collective-permute-start.2 = (f32[3,64,384]{2,1,0:T(8,128)}, f32[3,64,384]{2,1,0:T(8,128)S(1)}, u32[]{:S(2)}, u32[]{:S(2)}) collective-permute-start(f32[3,64,384]{2,1,0:T(8,128)} %get-tuple-element.11), channel_id=1, source_target_pairs={{0,8},{8,16},{16,24},{24,0},{1,9},{9,17},{17,25},{25,1},{2,10},{10... | collective-permute-start | bytes 884744 | tf_op jit(solution)/shard_map/ppermute | solution.py:362
  15.6 8.2 %collective-permute-start.3 = (f32[3,8,384]{2,1,0:T(8,128)}, f32[3,8,384]{2,1,0:T(8,128)S(1)}, u32[]{:S(2)}, u32[]{:S(2)}) collective-permute-start(f32[3,8,384]{2,1,0:T(8,128)} %get-tuple-element.12), channel_id=1, source_target_pairs={{0,24},{8,0},{16,8},{24,16},{1,25},{9,1},{17,9},{25,17},{2,26},{10... | collective-permute-start | bytes 110600 | tf_op jit(solution)/shard_map/ppermute | solution.py:363
  17.4 6.4 %copy-start.1 = (f32[3,128,128]{2,1,0:T(8,128)S(1)}, f32[3,128,128]{2,1,0:T(8,128)}, u32[]{:S(2)}) copy-start(f32[3,128,128]{2,1,0:T(8,128)} %get-tuple-element.10.rim_ref) | copy-start | bytes 589828
  17.4 6.4 %copy-start.3 = (s32[1,1,2]{2,1,0:T(1,128)S(1)}, s32[1,1,2]{2,1,0:T(1,128)}, u32[]{:S(2)}) copy-start(s32[1,1,2]{2,1,0:T(1,128)} %patch_pos.1) | copy-start | bytes 28
  17.4 6.4 %copy-start.4 = (s32[1,1,2]{2,1,0:T(1,128)S(1)}, s32[1,1,2]{2,1,0:T(1,128)}, u32[]{:S(2)}) copy-start(s32[1,1,2]{2,1,0:T(1,128)} %patch_ext.1) | copy-start | bytes 28
  23.8 0.8 %copy-start.2 = (f32[64,128]{1,0:T(8,128)S(1)}, f32[64,128]{1,0:T(8,128)}, u32[]{:S(2)}) copy-start(f32[64,128]{1,0:T(8,128)} %inner_error.1.inner_ref) | copy-start | bytes 98308

commit v2 on v1

--- a/solution.py
+++ b/solution.py
@@ -15,7 +15,6 @@
 RIGHT_ROWS, RIGHT_COLS, LEFT_ROWS, LEFT_COLS, OWN_ROWS, OWN_COLS = 6, 7, 8, 9, 10, 11
 
 VMEM = pl.BlockSpec(memory_space=pltpu.VMEM)
-SMEM = pl.BlockSpec(memory_space=pltpu.SMEM)
 PARAMS = pltpu.CompilerParams(vmem_limit_bytes=32 * 1024 * 1024)
 
 
@@ -66,57 +65,99 @@
     return [f - (0.5 * RATIO) * t for f, t in zip(fields, total)]
 
 
-def block_sum(field):
-    pair = field + roll(field, -1, 0)
-    return pair + roll(pair, -1, 1)
-
-
-def error_rows(fields, halved):
-    fine_two = spread_step(spread_step(fields, 1, 1), 1, 1)
-    coarse_one = spread_step([0.25 * block_sum(f) for f in fields], 2, 2)
-    total = None
-    for fine, coarse in zip(fine_two, coarse_one):
-        part = jnp.abs(0.25 * block_sum(fine) - coarse)
-        total = part if total is None else total + part
-    total = ERR_SCALE * total
-    halved[0] = total[4:20, 0:LANES]
-    halved[1] = total[4:20, LANES : 2 * LANES]
-    lanes = lane_ids(8)
-    even = (2 * lanes) % LANES
-    low = jnp.take_along_axis(halved[0, pl.ds(0, 8, stride=2), :], even, axis=1)
-    high = jnp.take_along_axis(halved[1, pl.ds(0, 8, stride=2), :], even, axis=1)
+def pair_change(near, far, near_terms, far_terms, axis):
+    inner = doubled_flux(near, far, near_terms, far_terms)
+    before = [roll(f, 1, axis) for f in far]
+    before_terms = [before[1 + axis] if c == 0 else roll(far_terms[c], 1, axis) for c in range(4)]
+    outer = doubled_flux(before, near, before_terms, near_terms)
+    near_change = [i - o for i, o in zip(inner, outer)]
+    far_change = [roll(o, -1, axis) - i for i, o in zip(inner, outer)]
+    return near_change, far_change
+
+
+def paired_step(phases):
+    terms = [[cell_terms(*phases[x][y]) for y in range(2)] for x in range(2)]
+    along_first = [
+        pair_change(phases[0][y], phases[1][y], terms[0][y][0], terms[1][y][0], 0) for y in range(2)
+    ]
+    along_second = [
+        pair_change(phases[x][0], phases[x][1], terms[x][0][1], terms[x][1][1], 1) for x in range(2)
+    ]
+    return [
+        [
+            [
+                phases[x][y][c] - (0.5 * RATIO) * (along_first[y][x][c] + along_second[x][y][c])
+                for c in range(3)
+            ]
+            for y in range(2)
+        ]
+        for x in range(2)
+    ]
+
+
+def block_mean(phases):
+    return [
+        0.25 * ((phases[0][0][c] + phases[1][0][c]) + (phases[0][1][c] + phases[1][1][c])) for c in range(3)
+    ]
+
+
+def coarse_error(phases):
+    fine = block_mean(paired_step(paired_step(phases)))
+    coarse = spread_step(block_mean(phases), 1, 1)
+    parts = [jnp.abs(f - c) for f, c in zip(fine, coarse)]
+    return ERR_SCALE * ((parts[0] + parts[1]) + parts[2])
+
+
+def every_other(first, second, parity):
+    lanes = lane_ids(first.shape[0])
+    pick = (2 * lanes + parity) % LANES
+    low = jnp.take_along_axis(first, pick, axis=1)
+    high = jnp.take_along_axis(second, pick, axis=1)
     return jnp.where(lanes < LANES // 2, low, high)
 
 
-def pack_cols(row_count, col_count, last_ref, first_ref, left_ref, right_ref):
-    rows = last_ref.shape[1]
-    half = rows // 2
-    rc = row_count[0, 0].astype(jnp.float32)
-    cc = col_count[0, 0].astype(jnp.float32)
-    lanes = lane_ids(half)
-    for comp in range(3):
-        upper = last_ref[comp, 0:half, :]
-        lower = roll(last_ref[comp, half:rows, :], LANES // 2, 1)
-        left_ref[comp, 0:half, :] = jnp.where(lanes >= LANES // 2, upper, lower)
-        left_ref[comp, half : half + 8, :] = jnp.where(lane_ids(8) == LEFT_ROWS, rc, cc)
-    lanes = lane_ids(rows)
-    packed = jnp.where(lanes == RIGHT_ROWS, rc, cc)
-    for comp in (2, 1, 0):
-        packed = jnp.where(lanes < 2 * comp + 2, roll(first_ref[comp], 2 * comp, 1), packed)
-    right_ref[...] = packed.T[0:8]
-
-
-def pack_rows(row_count, col_count, left_ref, right_ref, state_ref, rim_ref, down_ref, up_ref):
+def pack_cols(numbers_ref, state_ref, left_ref, right_ref, strip_ref):
     rows, cols = state_ref.shape[1], state_ref.shape[2]
     half = rows // 2
-    rc = row_count[0, 0].astype(jnp.float32)
-    cc = col_count[0, 0].astype(jnp.float32)
+    numbers = numbers_ref[...].astype(jnp.float32)
+    rc, cc = numbers[:, 0:1], numbers[:, 1:2]
+    lanes = lane_ids(half)
+    for comp in range(3):
+        upper = state_ref[comp, 0:half, cols - LANES : cols]
+        lower = roll(state_ref[comp, half:rows, cols - LANES : cols], LANES // 2, 1)
+        left_ref[comp * half : (comp + 1) * half, :] = jnp.where(lanes >= LANES // 2, upper, lower)
+    lanes = lane_ids(rows)
+    packed = None
+    for comp in range(3):
+        ends = jnp.where(lanes < LANES // 2, state_ref[comp, :, 0:LANES], state_ref[comp, :, cols - LANES : cols])
+        ends = roll(ends, 8 * comp + 4, 1)
+        packed = ends if packed is None else jnp.where(lanes >= 8 * comp, ends, packed)
+    strip_ref[0:24, :] = packed.T[0:24]
+    ids = row_ids(8)
+    spread = jnp.broadcast_to(numbers[:, 5:6], (8, LANES))
+    for k in range(5):
+        spread = jnp.where(ids == k, numbers[:, k : k + 1], spread)
+    strip_ref[24:32, :] = spread
+    counts = jnp.where(ids == 6, rc, cc)
+    for ref, base, at in ((left_ref, 3 * half, 2), (right_ref, 0, 4)):
+        ref[base : base + 8, :] = counts
+        for comp in range(3):
+            ref[base + 2 * comp : base + 2 * comp + 2, :] = strip_ref[8 * comp + at : 8 * comp + at + 2, :]
+
+
+def pack_rows(strip_ref, left_ref, right_ref, state_ref, rim_ref, down_ref, up_ref):
+    rows, cols = state_ref.shape[1], state_ref.shape[2]
+    half = rows // 2
+    rc, cc = strip_ref[24:25, :], strip_ref[25:26, :]
     right = jnp.concatenate([right_ref[...], jnp.zeros((LANES - 8, LANES), jnp.float32)], axis=0).T
     lanes = lane_ids(rows)
-    from_left = (lanes == LEFT_ROWS) | (lanes == LEFT_COLS)
-    counts = jnp.where(from_left, left_ref[0, half : half + 1, :], jnp.where(lanes == OWN_ROWS, rc, cc))
-    for comp in range(3):
-        packed = left_ref[comp, 0:half, :]
+    left_rc = left_ref[3 * half + 6 : 3 * half + 7, :]
+    left_cc = left_ref[3 * half + 7 : 3 * half + 8, :]
+    counts = jnp.where(lanes == OWN_ROWS, rc, cc)
+    counts = jnp.where(lanes == LEFT_COLS, left_cc, counts)
+    counts = jnp.where(lanes == LEFT_ROWS, left_rc, counts)
+    for comp in range(3):
+        packed = left_ref[comp * half : (comp + 1) * half, :]
         left = jnp.concatenate([packed, roll(packed, LANES // 2, 1)], axis=0)
         inner = right if comp == 0 else roll(right, -2 * comp, 1)
         inner = jnp.where(lanes < LEFT_ROWS, inner, counts)
@@ -128,21 +169,85 @@
         up_ref[comp, :, cols : cols + LANES] = rim[0:8]
 
 
-def inner_error(state_ref, rim_ref, error_ref, halved):
-    blocks = state_ref.shape[1] // 16
-
-    def one(block, carry):
-        start = pl.multiple_of(16 * block - 8, 8)
-        fields = [
-            jnp.concatenate(
-                [state_ref[c, pl.ds(start, 32), :][4:28], rim_ref[c, pl.ds(start, 32), :][4:28]], axis=1
+def inner_error(state_ref, error_ref, columns):
+    rows = state_ref.shape[1]
+    half = rows // 2
+    for comp in range(3):
+        first, second = state_ref[comp, :, 0:LANES], state_ref[comp, :, LANES : 2 * LANES]
+        for parity in range(2):
+            columns[comp, parity] = every_other(first, second, parity)
+    size = 24
+    for start in range(0, half - 2, size - 4):
+        start = min(start, half - size)
+        phases = [
+            [
+                [columns[c, y, pl.ds(2 * start + x, size, stride=2), :] for c in range(3)]
+                for y in range(2)
+            ]
+            for x in range(2)
+        ]
+        error = coarse_error(phases)
+        low = 0 if start == 0 else 2
+        error_ref[start + low : start + size, :] = error[low:size]
+
+
+def edge_phases(state_ref, above_ref, below_ref, left_ref, right_ref, strip_ref, near_rows, columns, strips):
+    rows, cols = state_ref.shape[1], state_ref.shape[2]
+    right = slice(cols, cols + LANES)
+    left_base = left_ref.shape[0] - 8
+    lanes = lane_ids(8)
+    packed_up, packed_down = None, None
+    for comp in range(3):
+        near_rows[comp, 0:2, :] = above_ref[comp, SLAB - 2 : SLAB, 0:cols]
+        near_rows[comp, 2:6, :] = state_ref[comp, 0:4, :]
+        near_rows[comp, 6:10, :] = state_ref[comp, rows - 4 : rows, :]
+        near_rows[comp, 10:12, :] = below_ref[comp, 0:2, 0:cols]
+        near_rows[comp, 12:16, :] = state_ref[comp, 0:4, :]
+        first, second = near_rows[comp, :, 0:LANES], near_rows[comp, :, LANES : 2 * LANES]
+        for parity in range(2):
+            columns[comp, parity] = every_other(first, second, parity)
+
+        def around_corner(ref, part):
+            rim = ref[comp, part, right]
+            start = jnp.where(lanes < LANES // 2, ref[comp, part, 0:LANES], rim)
+            end = jnp.where(lanes < LANES // 2, rim, ref[comp, part, cols - LANES : cols])
+            return jnp.where(
+                (lanes >= 12 * comp) & (lanes < 12 * comp + 6), roll(start, 12 * comp + 2, 1), roll(end, 12 * comp + 10, 1)
             )
-            for c in range(3)
-        ]
-        error_ref[pl.ds(pl.multiple_of(8 * block, 8), 8), :] = error_rows(fields, halved)
-        return carry
-
-    lax.fori_loop(1, blocks - 1, one, 0)
+
+        up, down = around_corner(above_ref, slice(SLAB - 8, SLAB)), around_corner(below_ref, slice(0, 8))
+        packed_up = up if comp == 0 else jnp.where(lanes >= 12 * comp, up, packed_up)
+        packed_down = down if comp == 0 else jnp.where(lanes >= 12 * comp, down, packed_down)
+    corners = jnp.concatenate([packed_down, jnp.ones((LANES - 16, LANES), jnp.float32), packed_up], axis=0).T
+    for comp in range(3):
+        strips[comp, 0, 0:2, :] = left_ref[left_base + 2 * comp : left_base + 2 * comp + 2, :]
+        strips[comp, 0, 2:6, :] = strip_ref[8 * comp + 4 : 8 * comp + 8, :]
+        strips[comp, 0, 6:10, :] = strip_ref[8 * comp : 8 * comp + 4, :]
+        strips[comp, 0, 10:12, :] = right_ref[2 * comp : 2 * comp + 2, :]
+        strips[comp, 0, 12:16, :] = strip_ref[8 * comp + 4 : 8 * comp + 8, :]
+        strips[comp, 1, 0:12, :] = corners[12 * comp : 12 * comp + 12, :]
+        strips[comp, 1, 12:16, :] = strip_ref[8 * comp + 4 : 8 * comp + 8, :]
+    phases = []
+    for x in range(2):
+        phases.append([])
+        for y in range(2):
+            cells = []
+            for comp, turned in ((0, 0), (1, 2), (2, 1)):
+                by_row = columns[comp, y, pl.ds(x, 8, stride=2), :]
+                own, outer = [strips[turned, k, pl.ds(x, 8, stride=2), :] for k in range(2)]
+                cells.append(jnp.concatenate([by_row, every_other(own, outer, y)], axis=0))
+            phases[-1].append(cells)
+    return phases
+
+
+def put_edges(error, edges):
+    half_rows = error.shape[0]
+    turned = jnp.concatenate([edges, jnp.zeros((LANES - 16, LANES), jnp.float32)], axis=0).T[0:half_rows]
+    lanes, ids = lane_ids(half_rows), row_ids(half_rows)
+    error = jnp.where(ids == 0, edges[1:2], jnp.where(ids == half_rows - 1, edges[4:5], error))
+    return jnp.where(
+        lanes == 0, roll(turned, -9, 1), jnp.where(lanes == LANES - 1, roll(turned, LANES - 13, 1), error)
+    )
 
 
 def minmod(lower_diff, upper_diff):
@@ -217,44 +322,32 @@
 
 
 def finish(
-    row_count, col_count, patch_pos, patch_ext, state_ref, rim_ref, above_ref, below_ref, inner_ref,
-    error_ref, moved_ref, patch_ref, edge, wide, window, halved,
+    state_ref, rim_ref, above_ref, below_ref, inner_ref, left_ref, right_ref,
+    strip_ref, error_ref, moved_ref, patch_ref, wide, window, near_rows, columns, strips,
 ):
     rows, cols = state_ref.shape[1], state_ref.shape[2]
     slab = slice(rows - SLAB, rows)
     top = slice(0, SLAB)
     right = slice(cols, cols + LANES)
-    last = slice(cols - LANES, cols)
 
     rim_counts = rim_ref[0, 0:8, :]
     above_counts = above_ref[0, 0:8, right]
     below_counts = below_ref[0, 0:8, right]
     get = lambda counts, lane: counts[0, lane].astype(jnp.int32)
-    rc, cc = row_count[0, 0], col_count[0, 0]
-    rc_left, rc_right, cc_right = [get(rim_counts, k) for k in (LEFT_ROWS, RIGHT_ROWS, RIGHT_COLS)]
+    rc, cc, rc_left, rc_right, cc_right = [
+        get(rim_counts, k) for k in (OWN_ROWS, OWN_COLS, LEFT_ROWS, RIGHT_ROWS, RIGHT_COLS)
+    ]
     cc_above, cc_above_right = [get(above_counts, k) for k in (OWN_COLS, RIGHT_COLS)]
     rc_below, cc_below, rc_below_left, rc_below_right, cc_below_right = [
         get(below_counts, k) for k in (OWN_ROWS, OWN_COLS, LEFT_ROWS, RIGHT_ROWS, RIGHT_COLS)
     ]
-
-    for comp in range(3):
-        edge[0, comp, 0:8, :] = above_ref[comp, SLAB - 8 : SLAB, :]
-        edge[0, comp, 8:32, 0:cols] = state_ref[comp, 0:24, :]
-        edge[0, comp, 8:32, right] = rim_ref[comp, 0:24, :]
-        edge[1, comp, 0:24, 0:cols] = state_ref[comp, rows - 24 : rows, :]
-        edge[1, comp, 0:24, right] = rim_ref[comp, rows - 24 : rows, :]
-        edge[1, comp, 24:32, :] = below_ref[comp, :, :]
-
-    half_rows = error_ref.shape[0]
-    error_ref[8 : half_rows - 8, :] = inner_ref[8 : half_rows - 8, :]
-
-    def edge_error(side, carry):
-        fields = [edge[side, c][4:28] for c in range(3)]
-        start = pl.multiple_of(side * (half_rows - 8), 8)
-        error_ref[pl.ds(start, 8), :] = error_rows(fields, halved)
-        return carry
-
-    lax.fori_loop(0, 2, edge_error, 0)
+    numbers = strip_ref[24:32, :]
+    pos_row, pos_col, ext_row, ext_col = [numbers[k, 0].astype(jnp.int32) for k in range(2, 6)]
+
+    edges = coarse_error(
+        edge_phases(state_ref, above_ref, below_ref, left_ref, right_ref, strip_ref, near_rows, columns, strips)
+    )
+    error_ref[...] = put_edges(inner_ref[...], edges)
 
     def moved_rows(own, own_rim, slab_rows, slab_rim, counts):
         here, left, right_count = counts
@@ -307,16 +400,16 @@
         wide[comp, rows + 8 : rows + 16, LANES:cols] = second
         wide[comp, rows + 8 : rows + 16, right] = outer
 
-    row_start = patch_pos[0, 0, 0] + 4
+    row_start = pos_row + 4
     base = pl.multiple_of(row_start // 8 * 8, 8)
     width = cols + LANES
     for comp in range(3):
         near = wide[comp, pl.ds(base, 80), :]
         near = pltpu.roll(near, (80 - (row_start - base)) % 80, 0)
-        near = pltpu.roll(near, (width + 2 - patch_pos[0, 0, 1]) % width, 1)
+        near = pltpu.roll(near, (width + 2 - pos_col) % width, 1)
         window[comp, :, :] = near[0:72, 0:LANES]
 
-    fine_rows, fine_cols = 2 * patch_ext[0, 0, 0], 2 * patch_ext[0, 0, 1]
+    fine_rows, fine_cols = 2 * ext_row, 2 * ext_col
 
     def patch_block(block, carry):
         start = pl.multiple_of(16 * block, 8)
@@ -329,7 +422,7 @@
                 patch_ref[c, pl.ds(2 * start + a, 16, stride=2), :] = jnp.where(inside, fine[a][c], 0.0)
         return carry
 
-    lax.fori_loop(0, PATCH // 16, patch_block, 0)
+    lax.fori_loop(0, PATCH // 16, patch_block, 0, unroll=True)
 
 
 def around(axis, by):
@@ -337,53 +430,61 @@
     return [(i, (i + by) % devices) for i in range(devices)]
 
 
+def in_vmem(value):
+    return pltpu.with_memory_space_constraint(value, pltpu.VMEM)
+
+
+def vmem(*shape):
+    return pltpu.VMEM(shape, jnp.float32)
+
+
 def per_device(state, row_count, col_count, patch_pos, patch_ext):
     rows, cols = state.shape[1], state.shape[2]
     width = cols + LANES
-    first_tile = pl.BlockSpec((3, rows, LANES), lambda i: (0, 0, 0))
-    last_tile = pl.BlockSpec((3, rows, LANES), lambda i: (0, 0, cols // LANES - 1))
-    to_right, to_left = pl.pallas_call(
+    half = rows // 2
+    numbers = jnp.concatenate([row_count, col_count, patch_pos[0], patch_ext[0]], axis=1)
+    to_right, to_left, strip = pl.pallas_call(
         pack_cols,
-        grid=(1,),
-        out_shape=(f32(3, rows // 2 + 8, LANES), f32(8, LANES)),
-        in_specs=[SMEM, SMEM, last_tile, first_tile],
-        out_specs=(VMEM, VMEM),
+        out_shape=(vmem(3 * half + 8, LANES), vmem(8, LANES), vmem(32, LANES)),
+        in_specs=[VMEM] * 2,
+        out_specs=(VMEM,) * 3,
         name="pack_cols",
-    )(row_count, col_count, state, state)
-    from_left = lax.ppermute(to_right, "col", around("col", 1))
-    from_right = lax.ppermute(to_left, "col", around("col", -1))
+    )(numbers, state)
+    from_left = in_vmem(lax.ppermute(to_right, "col", around("col", 1)))
+    from_right = in_vmem(lax.ppermute(to_left, "col", around("col", -1)))
+    inner = pl.pallas_call(
+        inner_error,
+        out_shape=vmem(half, cols // 2),
+        in_specs=[VMEM],
+        out_specs=VMEM,
+        scratch_shapes=[vmem(3, 2, rows, LANES)],
+        cost_estimate=pl.CostEstimate(flops=30_000_000, bytes_accessed=600_000, transcendentals=0),
+        name="inner_error",
+    )(state)
     rim, to_below, to_above = pl.pallas_call(
         pack_rows,
-        out_shape=(f32(3, rows, LANES), f32(3, SLAB, width), f32(3, 8, width)),
-        in_specs=[SMEM, SMEM, VMEM, VMEM, VMEM],
-        out_specs=(VMEM, VMEM, VMEM),
+        out_shape=(vmem(3, rows, LANES), vmem(3, SLAB, width), vmem(3, 8, width)),
+        in_specs=[VMEM] * 4,
+        out_specs=(VMEM,) * 3,
         name="pack_rows",
-    )(row_count, col_count, from_left, from_right, state)
-    from_above = lax.ppermute(to_below, "row", around("row", 1))
-    from_below = lax.ppermute(to_above, "row", around("row", -1))
-    inner = pl.pallas_call(
-        inner_error,
-        out_shape=f32(rows // 2, cols // 2),
-        in_specs=[VMEM, VMEM],
-        out_specs=VMEM,
-        scratch_shapes=[pltpu.VMEM((2, 16, LANES), jnp.float32)],
-        cost_estimate=pl.CostEstimate(flops=30_000_000, bytes_accessed=600_000, transcendentals=0),
-        name="inner_error",
-    )(state, rim)
+    )(strip, from_left, from_right, state)
+    from_above = in_vmem(lax.ppermute(to_below, "row", around("row", 1)))
+    from_below = in_vmem(lax.ppermute(to_above, "row", around("row", -1)))
     return pl.pallas_call(
         finish,
-        out_shape=(f32(rows // 2, cols // 2), f32(3, rows, cols), f32(3, 2 * PATCH, 2 * PATCH)),
-        in_specs=[SMEM] * 4 + [VMEM] * 5,
-        out_specs=(VMEM, VMEM, VMEM),
+        out_shape=(f32(half, cols // 2), f32(3, rows, cols), f32(3, 2 * PATCH, 2 * PATCH)),
+        in_specs=[VMEM] * 8,
+        out_specs=(VMEM,) * 3,
         scratch_shapes=[
-            pltpu.VMEM((2, 3, 32, width), jnp.float32),
-            pltpu.VMEM((3, rows + 16, width), jnp.float32),
-            pltpu.VMEM((3, 72, LANES), jnp.float32),
-            pltpu.VMEM((2, 16, LANES), jnp.float32),
+            vmem(3, rows + 16, width),
+            vmem(3, 72, LANES),
+            vmem(3, 16, cols),
+            vmem(3, 2, 16, LANES),
+            vmem(3, 2, 16, LANES),
         ],
         compiler_params=PARAMS,
         name="finish",
-    )(row_count, col_count, patch_pos, patch_ext, state, rim, from_above, from_below, inner)
+    )(state, rim, from_above, from_below, inner, from_left, from_right, strip)
 
 
 def solution(mesh):

time: 30.3 us -> 25.6 us (0.84)
  Pallas kernels: 15.7 us -> 9.11 us
  waiting for transfers between devices: 3.26 us -> 4.63 us
  other arithmetic: 0 us -> 0.59 us
    pallas_call x4, Pallas kernels: 15.7 us -> 9.11 us  [the longest x1 3.63 us: per_device(): pl.pallas_call(finish, out_shape=(f32(half, cols // 2), f32(3, rows, cols...]
    ppermute x4, waiting for transfers between devices: 3.26 us -> 4.63 us  [the longest x1 1.75 us: per_device(): from_above = in_vmem(lax.ppermute(to_below, 'row', around('row', 1)))]
    concatenate x0 -> x1, other arithmetic: none -> 0.59 us  [per_device(): jnp.concatenate([row_count, col_count, patch_pos[0], patch_ext[0]], axis=1)]
    unnamed x14 -> x10, local copies, waits for them, and re-layouts: 1.4 us -> 1.29 us
  transfers between devices with their start and end apart: 4 -> 4, of which waited for: 2 -> 3; matrix products, arithmetic and copies ran while one was open for 0% -> 0% of each run, Pallas kernels for 21% -> 12%
where the time goes in v2:
time: 25.6 us; the launch traced here: 25.4 us
  Pallas kernels  9.11 us (36%)
  starting transfers between devices  7.76 us (30%)
  waiting for transfers between devices  4.63 us (18%)
  between operations  1.98 us (8%)
  local copies, waits for them, and re-layouts  1.29 us (5%)
  other arithmetic  0.59 us (2%)
    pallas_call x1, Pallas kernels, per_device(): pl.pallas_call(finish, out_shape=(f32(half, cols // 2), f32(3, rows, cols...  3.63 us
    ppermute x1, starting transfers between devices, per_device(): from_right = in_vmem(lax.ppermute(to_left, 'col', around('col', -1)))  3.04 us
    pallas_call x1, Pallas kernels, per_device(): pl.pallas_call(inner_error, out_shape=vmem(half, cols // 2), in_specs=[VM...  3.02 us
    ppermute x1, starting transfers between devices, per_device(): from_left = in_vmem(lax.ppermute(to_right, 'col', around('col', 1)))  2.94 us
    ppermute x1, waiting for transfers between devices, per_device(): from_above = in_vmem(lax.ppermute(to_below, 'row', around('row', 1)))  1.75 us
    ppermute x1, starting transfers between devices, per_device(): from_below = in_vmem(lax.ppermute(to_above, 'row', around('row', -1)))  1.72 us
    ppermute x1, waiting for transfers between devices, per_device(): from_left = in_vmem(lax.ppermute(to_right, 'col', around('col', 1)))  1.55 us
    ppermute x1, waiting for transfers between devices, per_device(): from_right = in_vmem(lax.ppermute(to_left, 'col', around('col', -1)))  1.33 us
  transfers between devices with their start and end apart: 4, of which 3 were waited for; matrix products, arithmetic and copies ran while one was open for 0% of the time, Pallas kernels for 12%

profile of v2, /device:TPU:0, one launch (start us, length us, event | category | flops | bytes accessed | tf_op | source)
XLA Modules:
  0.0 25.4 jit_solution(125007433748461993)
XLA Ops:
  1.9 0.0 copy-start.3
  1.9 0.0 copy-start.4
  1.9 0.6 %copy-done.3 = s32[1,1,2]{2,1,0:T(1,128)S(1)} copy-done((s32[1,1,2]{2,1,0:T(1,128)S(1)}, s32[1,1,2]{2,1,0:T(1,128)}, u32[]{:S(2)}) %copy-start.3) | copy-done | bytes 32
  2.6 0.0 copy-done.4
  2.6 0.6 %pad_add_fusion.numbers_ref = s32[1,6]{1,0:T(1,128)} fusion(s32[1,2]{1,0:T(1,128)S(1)} %bitcast.2, s32[1,2]{1,0:T(1,128)S(1)} %bitcast.3, s32[1,1]{1,0:T(1,128)S(6)} %copy.9, s32[1,1]{1,0:T(1,128)S(6)} %copy.8), kind=kLoop, calls=%fused_computation | loop fusion | flops 18 | bytes 48 | tf_op jit(solution)/shard_map/concatenate | solution.py:445
  3.2 1.2 %pack_cols.1 = (f32[200,128]{1,0:T(8,128)S(1)}, f32[8,128]{1,0:T(8,128)S(1)}, f32[32,128]{1,0:T(8,128)S(1)}) custom-call(s32[1,6]{1,0:T(1,128)} %pad_add_fusion.numbers_ref, f32[3,128,256]{2,1,0:T(8,128)} %state_ref.7), custom_call_target="tpu_custom_call" | custom-call | tf_op jit(solution)/shard_map/pack_cols/pallas_call | solution.py:446
  4.4 0.0 copy-start.1
  4.4 0.6 %copy-done.1 = f32[32,128]{1,0:T(8,128)} copy-done((f32[32,128]{1,0:T(8,128)}, f32[32,128]{1,0:T(8,128)S(1)}, u32[]{:S(2)}) %copy-start.1) | copy-done | bytes 16408
  5.0 2.9 %collective-permute-start = (f32[200,128]{1,0:T(8,128)S(1)}, f32[200,128]{1,0:T(8,128)S(1)}, u32[]{:S(2)}, u32[]{:S(2)}) collective-permute-start(f32[200,128]{1,0:T(8,128)S(1)} %get-tuple-element.10), channel_id=1, source_target_pairs={{0,1},{1,2},{2,3},{3,4},{4,5},{5,6},{6,7},{7,0},{8,9},{9,10},{10,1... | collective-permute-start | bytes 307208 | tf_op jit(solution)/shard_map/ppermute | solution.py:453
  7.9 3.0 %collective-permute-start.1 = (f32[8,128]{1,0:T(8,128)S(1)}, f32[8,128]{1,0:T(8,128)S(1)}, u32[]{:S(2)}, u32[]{:S(2)}) collective-permute-start(f32[8,128]{1,0:T(8,128)S(1)} %get-tuple-element.11), channel_id=1, source_target_pairs={{0,7},{1,0},{2,1},{3,2},{4,3},{5,4},{6,5},{7,6},{8,15},{9,8},{10,9... | collective-permute-start | bytes 12296 | tf_op jit(solution)/shard_map/ppermute | solution.py:454
  11.0 1.3 %collective-permute-done.1.right_ref = f32[8,128]{1,0:T(8,128)S(1)} collective-permute-done((f32[8,128]{1,0:T(8,128)S(1)}, f32[8,128]{1,0:T(8,128)S(1)}, u32[]{:S(2)}, u32[]{:S(2)}) %collective-permute-start.1) | collective-permute-done | bytes 4128 | tf_op jit(solution)/shard_map/ppermute | solution.py:454
  12.3 1.5 %collective-permute-done.left_ref = f32[200,128]{1,0:T(8,128)S(1)} collective-permute-done((f32[200,128]{1,0:T(8,128)S(1)}, f32[200,128]{1,0:T(8,128)S(1)}, u32[]{:S(2)}, u32[]{:S(2)}) %collective-permute-start) | collective-permute-done | bytes 102432 | tf_op jit(solution)/shard_map/ppermute | solution.py:453
  13.9 0.0 copy-start
  13.9 1.3 %pack_rows.1 = (f32[3,128,128]{2,1,0:T(8,128)S(1)}, f32[3,64,384]{2,1,0:T(8,128)S(1)}, f32[3,8,384]{2,1,0:T(8,128)S(1)}) custom-call(f32[32,128]{1,0:T(8,128)} %copy-done.1, f32[200,128]{1,0:T(8,128)S(1)} %collective-permute-done.left_ref, f32[8,128]{1,0:T(8,128)S(1)} %collective-permute-done.1.right_ref, f32[3,128,256]{2,1,0:T(8,128)} %state_ref.7), custom_call_target="tpu_custom_call" | custom-call | tf_op jit(solution)/shard_map/pack_rows/pallas_call | solution.py:464
  15.1 0.1 collective-permute-start.2
  15.2 0.0 copy-start.2
  15.2 1.7 %collective-permute-start.3 = (f32[3,8,384]{2,1,0:T(8,128)S(1)}, f32[3,8,384]{2,1,0:T(8,128)S(1)}, u32[]{:S(2)}, u32[]{:S(2)}) collective-permute-start(f32[3,8,384]{2,1,0:T(8,128)S(1)} %get-tuple-element.14), channel_id=1, source_target_pairs={{0,24},{8,0},{16,8},{24,16},{1,25},{9,1},{17,9},{25,17},{2,26},{10... | collective-permute-start | bytes 110600 | tf_op jit(solution)/shard_map/ppermute | solution.py:472
  16.9 3.0 %inner_error.1.inner_ref = f32[64,128]{1,0:T(8,128)S(1)} custom-call(f32[3,128,256]{2,1,0:T(8,128)} %state_ref.7), custom_call_target="tpu_custom_call" | custom-call | flops 30000000 | bytes 600000 | tf_op jit(solution)/shard_map/inner_error/pallas_call | solution.py:455
  20.0 0.0 collective-permute-done.3.below_ref
  20.0 1.8 %collective-permute-done.2.above_ref = f32[3,64,384]{2,1,0:T(8,128)S(1)} collective-permute-done((f32[3,64,384]{2,1,0:T(8,128)S(1)}, f32[3,64,384]{2,1,0:T(8,128)S(1)}, u32[]{:S(2)}, u32[]{:S(2)}) %collective-permute-start.2) | collective-permute-done | bytes 294944 | tf_op jit(solution)/shard_map/ppermute | solution.py:471
  21.7 0.0 copy-done
  21.7 0.0 copy-done.2
  21.7 3.6 %finish.1 = (f32[64,128]{1,0:T(8,128)}, f32[3,128,256]{2,1,0:T(8,128)}, f32[3,128,128]{2,1,0:T(8,128)}) custom-call(f32[3,128,256]{2,1,0:T(8,128)S(1)} %copy-done, f32[3,128,128]{2,1,0:T(8,128)S(1)} %get-tuple-element.12.rim_ref, f32[3,64,384]{2,1,0:T(8,128)S(1)} %collective-permute-done.2.above_ref, f32[3,8,384]{2,1,0:T(8,128)S(1)} %collective-permute-done.3.below_ref, ...), custom_call_target="tpu_custom_call" | custom-call | tf_op jit(solution)/shard_map/finish/pallas_call | solution.py:473
Async XLA Ops:
  1.9 0.7 %copy-start.3 = (s32[1,1,2]{2,1,0:T(1,128)S(1)}, s32[1,1,2]{2,1,0:T(1,128)}, u32[]{:S(2)}) copy-start(s32[1,1,2]{2,1,0:T(1,128)} %param.9) | copy-start | bytes 28
  1.9 0.7 %copy-start.4 = (s32[1,1,2]{2,1,0:T(1,128)S(1)}, s32[1,1,2]{2,1,0:T(1,128)}, u32[]{:S(2)}) copy-start(s32[1,1,2]{2,1,0:T(1,128)} %param.8) | copy-start | bytes 28
  4.4 0.6 %copy-start.1 = (f32[32,128]{1,0:T(8,128)}, f32[32,128]{1,0:T(8,128)S(1)}, u32[]{:S(2)}) copy-start(f32[32,128]{1,0:T(8,128)S(1)} %get-tuple-element.9.strip_ref) | copy-start | bytes 49156
  5.0 8.9 %collective-permute-start = (f32[200,128]{1,0:T(8,128)S(1)}, f32[200,128]{1,0:T(8,128)S(1)}, u32[]{:S(2)}, u32[]{:S(2)}) collective-permute-start(f32[200,128]{1,0:T(8,128)S(1)} %get-tuple-element.10), channel_id=1, source_target_pairs={{0,1},{1,2},{2,3},{3,4},{4,5},{5,6},{6,7},{7,0},{8,9},{9,10},{10,1... | collective-permute-start | bytes 307208 | tf_op jit(solution)/shard_map/ppermute | solution.py:453
  7.9 4.4 %collective-permute-start.1 = (f32[8,128]{1,0:T(8,128)S(1)}, f32[8,128]{1,0:T(8,128)S(1)}, u32[]{:S(2)}, u32[]{:S(2)}) collective-permute-start(f32[8,128]{1,0:T(8,128)S(1)} %get-tuple-element.11), channel_id=1, source_target_pairs={{0,7},{1,0},{2,1},{3,2},{4,3},{5,4},{6,5},{7,6},{8,15},{9,8},{10,9... | collective-permute-start | bytes 12296 | tf_op jit(solution)/shard_map/ppermute | solution.py:454
  13.9 7.9 %copy-start = (f32[3,128,256]{2,1,0:T(8,128)S(1)}, f32[3,128,256]{2,1,0:T(8,128)}, u32[]{:S(2)}) copy-start(f32[3,128,256]{2,1,0:T(8,128)} %state_ref.7) | copy-start | bytes 1179652
  15.1 6.6 %collective-permute-start.2 = (f32[3,64,384]{2,1,0:T(8,128)S(1)}, f32[3,64,384]{2,1,0:T(8,128)S(1)}, u32[]{:S(2)}, u32[]{:S(2)}) collective-permute-start(f32[3,64,384]{2,1,0:T(8,128)S(1)} %get-tuple-element.13), channel_id=1, source_target_pairs={{0,8},{8,16},{16,24},{24,0},{1,9},{9,17},{17,25},{25,1},{2,10},{10... | collective-permute-start | bytes 884744 | tf_op jit(solution)/shard_map/ppermute | solution.py:471
  15.2 6.5 %copy-start.2 = (f32[32,128]{1,0:T(8,128)S(1)}, f32[32,128]{1,0:T(8,128)}, u32[]{:S(2)}) copy-start(f32[32,128]{1,0:T(8,128)} %copy-done.1) | copy-start | bytes 49156
  15.2 4.8 %collective-permute-start.3 = (f32[3,8,384]{2,1,0:T(8,128)S(1)}, f32[3,8,384]{2,1,0:T(8,128)S(1)}, u32[]{:S(2)}, u32[]{:S(2)}) collective-permute-start(f32[3,8,384]{2,1,0:T(8,128)S(1)} %get-tuple-element.14), channel_id=1, source_target_pairs={{0,24},{8,0},{16,8},{24,16},{1,25},{9,1},{17,9},{25,17},{2,26},{10... | collective-permute-start | bytes 110600 | tf_op jit(solution)/shard_map/ppermute | solution.py:472

commit v3 on v2

--- a/solution.py
+++ b/solution.py
@@ -116,11 +116,10 @@
     return jnp.where(lanes < LANES // 2, low, high)
 
 
-def pack_cols(numbers_ref, state_ref, left_ref, right_ref, strip_ref):
+def pack_cols(row_count, col_count, patch_pos, patch_ext, state_ref, left_ref, right_ref, strip_ref, slab_ref):
     rows, cols = state_ref.shape[1], state_ref.shape[2]
     half = rows // 2
-    numbers = numbers_ref[...].astype(jnp.float32)
-    rc, cc = numbers[:, 0:1], numbers[:, 1:2]
+    rc, cc = row_count[...].astype(jnp.float32), col_count[...].astype(jnp.float32)
     lanes = lane_ids(half)
     for comp in range(3):
         upper = state_ref[comp, 0:half, cols - LANES : cols]
@@ -134,18 +133,20 @@
         packed = ends if packed is None else jnp.where(lanes >= 8 * comp, ends, packed)
     strip_ref[0:24, :] = packed.T[0:24]
     ids = row_ids(8)
-    spread = jnp.broadcast_to(numbers[:, 5:6], (8, LANES))
-    for k in range(5):
-        spread = jnp.where(ids == k, numbers[:, k : k + 1], spread)
+    pos, ext = patch_pos[0].astype(jnp.float32), patch_ext[0].astype(jnp.float32)
+    spread = jnp.broadcast_to(ext[:, 1:2], (8, LANES))
+    for k, number in enumerate((rc, cc, pos[:, 0:1], pos[:, 1:2], ext[:, 0:1])):
+        spread = jnp.where(ids == k, number, spread)
     strip_ref[24:32, :] = spread
     counts = jnp.where(ids == 6, rc, cc)
     for ref, base, at in ((left_ref, 3 * half, 2), (right_ref, 0, 4)):
         ref[base : base + 8, :] = counts
         for comp in range(3):
             ref[base + 2 * comp : base + 2 * comp + 2, :] = strip_ref[8 * comp + at : 8 * comp + at + 2, :]
-
-
-def pack_rows(strip_ref, left_ref, right_ref, state_ref, rim_ref, down_ref, up_ref):
+    slab_ref[...] = state_ref[:, rows - SLAB : rows, :]
+
+
+def pack_rows(strip_ref, left_ref, right_ref, state_ref, rim_ref, down_ref, up_ref, edge_ref):
     rows, cols = state_ref.shape[1], state_ref.shape[2]
     half = rows // 2
     rc, cc = strip_ref[24:25, :], strip_ref[25:26, :]
@@ -163,10 +164,15 @@
         inner = jnp.where(lanes < LEFT_ROWS, inner, counts)
         rim = jnp.where(lanes >= LANES // 2, left, inner)
         rim_ref[comp] = rim
-        down_ref[comp, :, 0:cols] = state_ref[comp, rows - SLAB : rows, :]
-        down_ref[comp, :, cols : cols + LANES] = rim[rows - SLAB : rows]
+        down_ref[comp] = rim[rows - SLAB : rows]
         up_ref[comp, :, 0:cols] = state_ref[comp, 0:8, :]
         up_ref[comp, :, cols : cols + LANES] = rim[0:8]
+        edge_ref[comp, 0:2, :] = left_ref[3 * half + 2 * comp : 3 * half + 2 * comp + 2, :]
+        edge_ref[comp, 2:6, :] = strip_ref[8 * comp + 4 : 8 * comp + 8, :]
+        edge_ref[comp, 6:10, :] = strip_ref[8 * comp : 8 * comp + 4, :]
+        edge_ref[comp, 10:12, :] = right_ref[2 * comp : 2 * comp + 2, :]
+        edge_ref[comp, 12:16, :] = strip_ref[8 * comp + 4 : 8 * comp + 8, :]
+    edge_ref[3, 0:8, :] = strip_ref[24:32, :]
 
 
 def inner_error(state_ref, error_ref, columns):
@@ -191,14 +197,13 @@
         error_ref[start + low : start + size, :] = error[low:size]
 
 
-def edge_phases(state_ref, above_ref, below_ref, left_ref, right_ref, strip_ref, near_rows, columns, strips):
+def edge_phases(state_ref, slab_ref, above_ref, below_ref, edge_ref, near_rows, columns, corners_ref):
     rows, cols = state_ref.shape[1], state_ref.shape[2]
     right = slice(cols, cols + LANES)
-    left_base = left_ref.shape[0] - 8
     lanes = lane_ids(8)
     packed_up, packed_down = None, None
     for comp in range(3):
-        near_rows[comp, 0:2, :] = above_ref[comp, SLAB - 2 : SLAB, 0:cols]
+        near_rows[comp, 0:2, :] = slab_ref[comp, SLAB - 2 : SLAB, :]
         near_rows[comp, 2:6, :] = state_ref[comp, 0:4, :]
         near_rows[comp, 6:10, :] = state_ref[comp, rows - 4 : rows, :]
         near_rows[comp, 10:12, :] = below_ref[comp, 0:2, 0:cols]
@@ -207,26 +212,20 @@
         for parity in range(2):
             columns[comp, parity] = every_other(first, second, parity)
 
-        def around_corner(ref, part):
-            rim = ref[comp, part, right]
-            start = jnp.where(lanes < LANES // 2, ref[comp, part, 0:LANES], rim)
-            end = jnp.where(lanes < LANES // 2, rim, ref[comp, part, cols - LANES : cols])
-            return jnp.where(
-                (lanes >= 12 * comp) & (lanes < 12 * comp + 6), roll(start, 12 * comp + 2, 1), roll(end, 12 * comp + 10, 1)
-            )
-
-        up, down = around_corner(above_ref, slice(SLAB - 8, SLAB)), around_corner(below_ref, slice(0, 8))
+        def around_corner(body, rim):
+            start = jnp.where(lanes < LANES // 2, body[:, 0:LANES], rim)
+            end = jnp.where(lanes < LANES // 2, rim, body[:, cols - LANES : cols])
+            first_six = (lanes >= 12 * comp) & (lanes < 12 * comp + 6)
+            return jnp.where(first_six, roll(start, 12 * comp + 2, 1), roll(end, 12 * comp + 10, 1))
+
+        up = around_corner(slab_ref[comp, SLAB - 8 : SLAB, :], above_ref[comp, SLAB - 8 : SLAB, :])
+        down = around_corner(below_ref[comp, :, 0:cols], below_ref[comp, :, right])
         packed_up = up if comp == 0 else jnp.where(lanes >= 12 * comp, up, packed_up)
         packed_down = down if comp == 0 else jnp.where(lanes >= 12 * comp, down, packed_down)
     corners = jnp.concatenate([packed_down, jnp.ones((LANES - 16, LANES), jnp.float32), packed_up], axis=0).T
     for comp in range(3):
-        strips[comp, 0, 0:2, :] = left_ref[left_base + 2 * comp : left_base + 2 * comp + 2, :]
-        strips[comp, 0, 2:6, :] = strip_ref[8 * comp + 4 : 8 * comp + 8, :]
-        strips[comp, 0, 6:10, :] = strip_ref[8 * comp : 8 * comp + 4, :]
-        strips[comp, 0, 10:12, :] = right_ref[2 * comp : 2 * comp + 2, :]
-        strips[comp, 0, 12:16, :] = strip_ref[8 * comp + 4 : 8 * comp + 8, :]
-        strips[comp, 1, 0:12, :] = corners[12 * comp : 12 * comp + 12, :]
-        strips[comp, 1, 12:16, :] = strip_ref[8 * comp + 4 : 8 * comp + 8, :]
+        corners_ref[comp, 0:12, :] = corners[12 * comp : 12 * comp + 12, :]
+        corners_ref[comp, 12:16, :] = edge_ref[comp, 12:16, :]
     phases = []
     for x in range(2):
         phases.append([])
@@ -234,7 +233,7 @@
             cells = []
             for comp, turned in ((0, 0), (1, 2), (2, 1)):
                 by_row = columns[comp, y, pl.ds(x, 8, stride=2), :]
-                own, outer = [strips[turned, k, pl.ds(x, 8, stride=2), :] for k in range(2)]
+                own, outer = [ref[turned, pl.ds(x, 8, stride=2), :] for ref in (edge_ref, corners_ref)]
                 cells.append(jnp.concatenate([by_row, every_other(own, outer, y)], axis=0))
             phases[-1].append(cells)
     return phases
@@ -322,16 +321,16 @@
 
 
 def finish(
-    state_ref, rim_ref, above_ref, below_ref, inner_ref, left_ref, right_ref,
-    strip_ref, error_ref, moved_ref, patch_ref, wide, window, near_rows, columns, strips,
+    state_ref, rim_ref, slab_ref, above_ref, below_ref, inner_ref, edge_ref,
+    error_ref, moved_ref, patch_ref, wide, window, near_rows, columns, corners,
 ):
     rows, cols = state_ref.shape[1], state_ref.shape[2]
-    slab = slice(rows - SLAB, rows)
+    bottom = slice(rows - SLAB, rows)
     top = slice(0, SLAB)
     right = slice(cols, cols + LANES)
 
     rim_counts = rim_ref[0, 0:8, :]
-    above_counts = above_ref[0, 0:8, right]
+    above_counts = above_ref[0, 0:8, :]
     below_counts = below_ref[0, 0:8, right]
     get = lambda counts, lane: counts[0, lane].astype(jnp.int32)
     rc, cc, rc_left, rc_right, cc_right = [
@@ -341,11 +340,11 @@
     rc_below, cc_below, rc_below_left, rc_below_right, cc_below_right = [
         get(below_counts, k) for k in (OWN_ROWS, OWN_COLS, LEFT_ROWS, RIGHT_ROWS, RIGHT_COLS)
     ]
-    numbers = strip_ref[24:32, :]
+    numbers = edge_ref[3, 0:8, :]
     pos_row, pos_col, ext_row, ext_col = [numbers[k, 0].astype(jnp.int32) for k in range(2, 6)]
 
     edges = coarse_error(
-        edge_phases(state_ref, above_ref, below_ref, left_ref, right_ref, strip_ref, near_rows, columns, strips)
+        edge_phases(state_ref, slab_ref, above_ref, below_ref, edge_ref, near_rows, columns, corners)
     )
     error_ref[...] = put_edges(inner_ref[...], edges)
 
@@ -372,7 +371,7 @@
     for comp in range(3):
         own, own_rim = state_ref[comp, :, :], rim_ref[comp, :, :]
         body, side = moved_rows(
-            own[top], own_rim[top], above_ref[comp, :, 0:cols], above_ref[comp, :, right], (rc, rc_left, rc_right)
+            own[top], own_rim[top], slab_ref[comp, :, :], above_ref[comp, :, :], (rc, rc_left, rc_right)
         )
         for part, body, side in (
             (top, body, side),
@@ -386,13 +385,13 @@
             wide[comp, at, LANES:cols] = second
             wide[comp, at, right] = outer
         first, second, outer = moved_cols(
-            above_ref[comp, SLAB - 8 : SLAB, 0:cols], above_ref[comp, SLAB - 8 : SLAB, right], cc_above, cc_above_right
+            slab_ref[comp, SLAB - 8 : SLAB, :], above_ref[comp, SLAB - 8 : SLAB, :], cc_above, cc_above_right
         )
         wide[comp, 0:8, 0:LANES] = first
         wide[comp, 0:8, LANES:cols] = second
         wide[comp, 0:8, right] = outer
         body, side = moved_rows(
-            below_ref[comp, :, 0:cols], below_ref[comp, :, right], own[slab], own_rim[slab],
+            below_ref[comp, :, 0:cols], below_ref[comp, :, right], own[bottom], own_rim[bottom],
             (rc_below, rc_below_left, rc_below_right),
         )
         first, second, outer = moved_cols(body, side, cc_below, cc_below_right)
@@ -434,6 +433,10 @@
     return pltpu.with_memory_space_constraint(value, pltpu.VMEM)
 
 
+def in_hbm(value):
+    return pltpu.with_memory_space_constraint(value, pltpu.HBM)
+
+
 def vmem(*shape):
     return pltpu.VMEM(shape, jnp.float32)
 
@@ -442,16 +445,18 @@
     rows, cols = state.shape[1], state.shape[2]
     width = cols + LANES
     half = rows // 2
-    numbers = jnp.concatenate([row_count, col_count, patch_pos[0], patch_ext[0]], axis=1)
-    to_right, to_left, strip = pl.pallas_call(
+    patch_pos, patch_ext = in_hbm(patch_pos), in_hbm(patch_ext)
+    to_right, to_left, strip, slab = pl.pallas_call(
         pack_cols,
-        out_shape=(vmem(3 * half + 8, LANES), vmem(8, LANES), vmem(32, LANES)),
-        in_specs=[VMEM] * 2,
-        out_specs=(VMEM,) * 3,
+        out_shape=(vmem(3 * half + 8, LANES), vmem(8, LANES), vmem(32, LANES), vmem(3, SLAB, cols)),
+        in_specs=[VMEM] * 5,
+        out_specs=(VMEM,) * 4,
         name="pack_cols",
-    )(numbers, state)
+    )(row_count, col_count, patch_pos, patch_ext, state)
+    strip, here = in_vmem(strip), in_vmem(state)
     from_left = in_vmem(lax.ppermute(to_right, "col", around("col", 1)))
     from_right = in_vmem(lax.ppermute(to_left, "col", around("col", -1)))
+    slab_above = in_vmem(lax.ppermute(slab, "row", around("row", 1)))
     inner = pl.pallas_call(
         inner_error,
         out_shape=vmem(half, cols // 2),
@@ -460,31 +465,31 @@
         scratch_shapes=[vmem(3, 2, rows, LANES)],
         cost_estimate=pl.CostEstimate(flops=30_000_000, bytes_accessed=600_000, transcendentals=0),
         name="inner_error",
-    )(state)
-    rim, to_below, to_above = pl.pallas_call(
+    )(here)
+    rim, to_below, to_above, edge = pl.pallas_call(
         pack_rows,
-        out_shape=(vmem(3, rows, LANES), vmem(3, SLAB, width), vmem(3, 8, width)),
+        out_shape=(vmem(3, rows, LANES), vmem(3, SLAB, LANES), vmem(3, 8, width), vmem(4, 16, LANES)),
         in_specs=[VMEM] * 4,
-        out_specs=(VMEM,) * 3,
+        out_specs=(VMEM,) * 4,
         name="pack_rows",
-    )(strip, from_left, from_right, state)
+    )(strip, from_left, from_right, here)
     from_above = in_vmem(lax.ppermute(to_below, "row", around("row", 1)))
     from_below = in_vmem(lax.ppermute(to_above, "row", around("row", -1)))
     return pl.pallas_call(
         finish,
         out_shape=(f32(half, cols // 2), f32(3, rows, cols), f32(3, 2 * PATCH, 2 * PATCH)),
-        in_specs=[VMEM] * 8,
+        in_specs=[VMEM] * 7,
         out_specs=(VMEM,) * 3,
         scratch_shapes=[
             vmem(3, rows + 16, width),
             vmem(3, 72, LANES),
             vmem(3, 16, cols),
             vmem(3, 2, 16, LANES),
-            vmem(3, 2, 16, LANES),
+            vmem(3, 16, LANES),
         ],
         compiler_params=PARAMS,
         name="finish",
-    )(state, rim, from_above, from_below, inner, from_left, from_right, strip)
+    )(here, rim, slab_above, from_above, from_below, inner, edge)
 
 
 def solution(mesh):

time: 25.6 us -> 20.7 us (0.81)
  the two profiles are of different devices: /device:TPU:0 before, /device:TPU:1 now
where the time goes in v3:
time: 20.7 us; the launch traced here: 20.5 us
  starting transfers between devices  9.38 us (45%)
  Pallas kernels  7.05 us (34%)
  waiting for transfers between devices  2.11 us (10%)
  between operations  2 us (10%)
    pallas_call x1, Pallas kernels, per_device(): pl.pallas_call(finish, out_shape=(f32(half, cols // 2), f32(3, rows, cols...  3.63 us
    ppermute x1, starting transfers between devices, per_device(): from_right = in_vmem(lax.ppermute(to_left, 'col', around('col', -1)))  2.95 us
    ppermute x1, starting transfers between devices, per_device(): from_above = in_vmem(lax.ppermute(to_below, 'row', around('row', 1)))  2.26 us
    ppermute x1, starting transfers between devices, per_device(): from_left = in_vmem(lax.ppermute(to_right, 'col', around('col', 1)))  2.08 us
    ppermute x1, starting transfers between devices, per_device(): slab_above = in_vmem(lax.ppermute(slab, 'row', around('row', 1)))  2.08 us
    pallas_call x1, Pallas kernels, per_device(): pl.pallas_call(inner_error, out_shape=vmem(half, cols // 2), in_specs=[VM...  2.03 us
    ppermute x1, waiting for transfers between devices, per_device(): from_below = in_vmem(lax.ppermute(to_above, 'row', around('row', -1)))  1.34 us
    pallas_call x1, Pallas kernels, per_device(): pl.pallas_call(pack_cols, out_shape=(vmem(3 * half + 8, LANES), vmem(8, L...  1.21 us
  transfers between devices with their start and end apart: 5, of which 2 were waited for; matrix products, arithmetic and copies ran while one was open for 0% of the time, Pallas kernels for 11%

profile of v3, /device:TPU:1, one launch (start us, length us, event | category | flops | bytes accessed | tf_op | source)
XLA Modules:
  0.0 20.5 jit_solution(6758220008070497716)
XLA Ops:
  0.6 0.0 copy-start
  2.0 1.2 %pack_cols.1 = (f32[200,128]{1,0:T(8,128)S(1)}, f32[8,128]{1,0:T(8,128)S(1)}, f32[32,128]{1,0:T(8,128)S(1)}, f32[3,64,256]{2,1,0:T(8,128)S(1)}) custom-call(s32[1,1]{1,0:T(1,128)S(6)} %copy.8.row_count, s32[1,1]{1,0:T(1,128)S(6)} %copy.9.col_count, s32[1,1,2]{2,1,0:T(1,128)} %patch_pos.1, s32[1,1,2]{2,1,0:T(1,128)} %patch_ext.1, f32[3,128,256]{2,1,0:T(8,128)} %state_ref.7), custom_call_target="tpu_custom_call" | custom-call | tf_op jit(solution)/shard_map/pack_cols/pallas_call | solution.py:449
  3.2 2.1 %collective-permute-start = (f32[200,128]{1,0:T(8,128)S(1)}, f32[200,128]{1,0:T(8,128)S(1)}, u32[]{:S(2)}, u32[]{:S(2)}) collective-permute-start(f32[200,128]{1,0:T(8,128)S(1)} %get-tuple-element.12), channel_id=1, source_target_pairs={{0,1},{1,2},{2,3},{3,4},{4,5},{5,6},{6,7},{7,0},{8,9},{9,10},{10,1... | collective-permute-start | bytes 307208 | tf_op jit(solution)/shard_map/ppermute | solution.py:457
  5.3 2.1 %collective-permute-start.2 = (f32[3,64,256]{2,1,0:T(8,128)S(1)}, f32[3,64,256]{2,1,0:T(8,128)S(1)}, u32[]{:S(2)}, u32[]{:S(2)}) collective-permute-start(f32[3,64,256]{2,1,0:T(8,128)S(1)} %get-tuple-element.15), channel_id=1, source_target_pairs={{0,8},{8,16},{16,24},{24,0},{1,9},{9,17},{17,25},{25,1},{2,10},{10... | collective-permute-start | bytes 589832 | tf_op jit(solution)/shard_map/ppermute | solution.py:459
  7.4 3.0 %collective-permute-start.1 = (f32[8,128]{1,0:T(8,128)S(1)}, f32[8,128]{1,0:T(8,128)S(1)}, u32[]{:S(2)}, u32[]{:S(2)}) collective-permute-start(f32[8,128]{1,0:T(8,128)S(1)} %get-tuple-element.13), channel_id=1, source_target_pairs={{0,7},{1,0},{2,1},{3,2},{4,3},{5,4},{6,5},{7,6},{8,15},{9,8},{10,9... | collective-permute-start | bytes 12296 | tf_op jit(solution)/shard_map/ppermute | solution.py:458
  10.3 0.8 %collective-permute-done.1.right_ref = f32[8,128]{1,0:T(8,128)S(1)} collective-permute-done((f32[8,128]{1,0:T(8,128)S(1)}, f32[8,128]{1,0:T(8,128)S(1)}, u32[]{:S(2)}, u32[]{:S(2)}) %collective-permute-start.1) | collective-permute-done | bytes 4128 | tf_op jit(solution)/shard_map/ppermute | solution.py:458
  11.1 0.0 collective-permute-done.left_ref
  11.1 0.0 copy-done
  11.1 0.2 pack_rows.1
  11.3 2.3 %collective-permute-start.3 = (f32[3,64,128]{2,1,0:T(8,128)S(1)}, f32[3,64,128]{2,1,0:T(8,128)S(1)}, u32[]{:S(2)}, u32[]{:S(2)}) collective-permute-start(f32[3,64,128]{2,1,0:T(8,128)S(1)} %get-tuple-element.16), channel_id=1, source_target_pairs={{0,8},{8,16},{16,24},{24,0},{1,9},{9,17},{17,25},{25,1},{2,10},{10... | collective-permute-start | bytes 294920 | tf_op jit(solution)/shard_map/ppermute | solution.py:476
  13.5 0.0 collective-permute-start.4
  13.5 2.0 %inner_error.1.inner_ref = f32[64,128]{1,0:T(8,128)S(1)} custom-call(f32[3,128,256]{2,1,0:T(8,128)S(1)} %copy-done), custom_call_target="tpu_custom_call" | custom-call | flops 30000000 | bytes 600000 | tf_op jit(solution)/shard_map/inner_error/pallas_call | solution.py:460
  15.6 1.3 %collective-permute-done.4.below_ref = f32[3,8,384]{2,1,0:T(8,128)S(1)} collective-permute-done((f32[3,8,384]{2,1,0:T(8,128)S(1)}, f32[3,8,384]{2,1,0:T(8,128)S(1)}, u32[]{:S(2)}, u32[]{:S(2)}) %collective-permute-start.4) | collective-permute-done | bytes 36896 | tf_op jit(solution)/shard_map/ppermute | solution.py:477
  16.9 0.0 collective-permute-done.2.slab_ref
  16.9 0.0 collective-permute-done.3.above_ref
  16.9 3.6 %finish.1 = (f32[64,128]{1,0:T(8,128)}, f32[3,128,256]{2,1,0:T(8,128)}, f32[3,128,128]{2,1,0:T(8,128)}) custom-call(f32[3,128,256]{2,1,0:T(8,128)S(1)} %copy-done, f32[3,128,128]{2,1,0:T(8,128)S(1)} %get-tuple-element.14.rim_ref, f32[3,64,256]{2,1,0:T(8,128)S(1)} %collective-permute-done.2.slab_ref, f32[3,64,128]{2,1,0:T(8,128)S(1)} %collective-permute-done.3.above_ref, ...), custom_call_target="tpu_custom_call" | custom-call | tf_op jit(solution)/shard_map/finish/pallas_call | solution.py:478
Async XLA Ops:
  0.6 10.4 %copy-start = (f32[3,128,256]{2,1,0:T(8,128)S(1)}, f32[3,128,256]{2,1,0:T(8,128)}, u32[]{:S(2)}) copy-start(f32[3,128,256]{2,1,0:T(8,128)} %state_ref.7) | copy-start | bytes 1179652
  3.2 7.9 %collective-permute-start = (f32[200,128]{1,0:T(8,128)S(1)}, f32[200,128]{1,0:T(8,128)S(1)}, u32[]{:S(2)}, u32[]{:S(2)}) collective-permute-start(f32[200,128]{1,0:T(8,128)S(1)} %get-tuple-element.12), channel_id=1, source_target_pairs={{0,1},{1,2},{2,3},{3,4},{4,5},{5,6},{6,7},{7,0},{8,9},{9,10},{10,1... | collective-permute-start | bytes 307208 | tf_op jit(solution)/shard_map/ppermute | solution.py:457
  5.3 11.6 %collective-permute-start.2 = (f32[3,64,256]{2,1,0:T(8,128)S(1)}, f32[3,64,256]{2,1,0:T(8,128)S(1)}, u32[]{:S(2)}, u32[]{:S(2)}) collective-permute-start(f32[3,64,256]{2,1,0:T(8,128)S(1)} %get-tuple-element.15), channel_id=1, source_target_pairs={{0,8},{8,16},{16,24},{24,0},{1,9},{9,17},{17,25},{25,1},{2,10},{10... | collective-permute-start | bytes 589832 | tf_op jit(solution)/shard_map/ppermute | solution.py:459
  7.4 3.7 %collective-permute-start.1 = (f32[8,128]{1,0:T(8,128)S(1)}, f32[8,128]{1,0:T(8,128)S(1)}, u32[]{:S(2)}, u32[]{:S(2)}) collective-permute-start(f32[8,128]{1,0:T(8,128)S(1)} %get-tuple-element.13), channel_id=1, source_target_pairs={{0,7},{1,0},{2,1},{3,2},{4,3},{5,4},{6,5},{7,6},{8,15},{9,8},{10,9... | collective-permute-start | bytes 12296 | tf_op jit(solution)/shard_map/ppermute | solution.py:458
  11.3 5.7 %collective-permute-start.3 = (f32[3,64,128]{2,1,0:T(8,128)S(1)}, f32[3,64,128]{2,1,0:T(8,128)S(1)}, u32[]{:S(2)}, u32[]{:S(2)}) collective-permute-start(f32[3,64,128]{2,1,0:T(8,128)S(1)} %get-tuple-element.16), channel_id=1, source_target_pairs={{0,8},{8,16},{16,24},{24,0},{1,9},{9,17},{17,25},{25,1},{2,10},{10... | collective-permute-start | bytes 294920 | tf_op jit(solution)/shard_map/ppermute | solution.py:476
  13.5 3.4 %collective-permute-start.4 = (f32[3,8,384]{2,1,0:T(8,128)S(1)}, f32[3,8,384]{2,1,0:T(8,128)S(1)}, u32[]{:S(2)}, u32[]{:S(2)}) collective-permute-start(f32[3,8,384]{2,1,0:T(8,128)S(1)} %get-tuple-element.17), channel_id=1, source_target_pairs={{0,24},{8,0},{16,8},{24,16},{1,25},{9,1},{17,9},{25,17},{2,26},{10... | collective-permute-start | bytes 110600 | tf_op jit(solution)/shard_map/ppermute | solution.py:477

commit v4 on v3

v4 whole, which is shorter than its diff:
```python
import jax
import jax.numpy as jnp
from jax import lax
from jax.experimental import pallas as pl
from jax.experimental.pallas import tpu as pltpu
from jax.sharding import PartitionSpec as P

SLAB = 64
PATCH = 64
LANES = 128
PATCH_ROWS = 64

RATIO = 0.1
ERR_SCALE = 10.0

RIGHT_ROWS, RIGHT_COLS, LEFT_ROWS, OWN_ROWS, OWN_COLS = 6, 7, 8, 10, 11
DOWN_ROWS = 3 * SLAB // 2 + 8

VMEM = pl.BlockSpec(memory_space=pltpu.VMEM)
SMEM = pl.BlockSpec(memory_space=pltpu.SMEM)
ANY = pl.BlockSpec(memory_space=pl.ANY)
PARAMS = pltpu.CompilerParams(vmem_limit_bytes=32 * 1024 * 1024)


def f32(*shape):
    return jax.ShapeDtypeStruct(shape, jnp.float32)


def lane_ids(rows, width=LANES):
    return lax.broadcasted_iota(jnp.int32, (rows, width), 1)


def row_ids(rows, width=LANES):
    return lax.broadcasted_iota(jnp.int32, (rows, width), 0)


def roll(value, by, axis):
    return pltpu.roll(value, by % value.shape[axis], axis)


def cell_terms(depth, first, second):
    inverse_root = lax.rsqrt(depth)
    wave = depth * inverse_root
    inverse = inverse_root * inverse_root
    first_vel = first * inverse
    second_vel = second * inverse
    pressure = 0.5 * depth * depth
    cross = first * second_vel
    row_terms = (first, first * first_vel + pressure, cross, jnp.abs(first_vel) + wave)
    col_terms = (second, cross, second * second_vel + pressure, jnp.abs(second_vel) + wave)
    return row_terms, col_terms


def doubled_flux(left, right, left_terms, right_terms):
    speed = jnp.maximum(left_terms[3], right_terms[3])
    return [(left_terms[c] + right_terms[c]) - speed * (right[c] - left[c]) for c in range(3)]


def spread_step(fields, row_by, col_by):
    row_terms, col_terms = cell_terms(*fields)
    total = None
    for terms, by, axis in ((row_terms, row_by, 0), (col_terms, col_by, 1)):
        lower = [roll(f, by, axis) for f in fields]
        momentum = lower[1 + axis]
        lower_terms = [momentum if c == 0 else roll(terms[c], by, axis) for c in range(4)]
        flux = doubled_flux(lower, fields, lower_terms, terms)
        change = [roll(f, -by, axis) - f for f in flux]
        total = change if total is None else [t + c for t, c in zip(total, change)]
    return [f - (0.5 * RATIO) * t for f, t in zip(fields, total)]


def pair_change(near, far, near_terms, far_terms, axis):
    inner = doubled_flux(near, far, near_terms, far_terms)
    before = [roll(f, 1, axis) for f in far]
    before_terms = [before[1 + axis] if c == 0 else roll(far_terms[c], 1, axis) for c in range(4)]
    outer = doubled_flux(before, near, before_terms, near_terms)
    near_change = [i - o for i, o in zip(inner, outer)]
    far_change = [roll(o, -1, axis) - i for i, o in zip(inner, outer)]
    return near_change, far_change


def paired_step(phases):
    terms = [[cell_terms(*phases[x][y]) for y in range(2)] for x in range(2)]
    along_first = [
        pair_change(phases[0][y], phases[1][y], terms[0][y][0], terms[1][y][0], 0) for y in range(2)
    ]
    along_second = [
        pair_change(phases[x][0], phases[x][1], terms[x][0][1], terms[x][1][1], 1) for x in range(2)
    ]
    return [
        [
            [
                phases[x][y][c] - (0.5 * RATIO) * (along_first[y][x][c] + along_second[x][y][c])
                for c in range(3)
            ]
            for y in range(2)
        ]
        for x in range(2)
    ]


def block_mean(phases):
    return [
        0.25 * ((phases[0][0][c] + phases[1][0][c]) + (phases[0][1][c] + phases[1][1][c])) for c in range(3)
    ]


def coarse_error(phases):
    fine = block_mean(paired_step(paired_step(phases)))
    coarse = spread_step(block_mean(phases), 1, 1)
    parts = [jnp.abs(f - c) for f, c in zip(fine, coarse)]
    return ERR_SCALE * ((parts[0] + parts[1]) + parts[2])


def every_other(first, second, parity):
    lanes = lane_ids(first.shape[0])
    pick = (2 * lanes + parity) % LANES
    low = jnp.take_along_axis(first, pick, axis=1)
    high = jnp.take_along_axis(second, pick, axis=1)
    return jnp.where(lanes < LANES // 2, low, high)


def pack_cols(row_count, state_ref, left_ref, strip_ref, slab_ref):
    rows, cols = state_ref.shape[1], state_ref.shape[2]
    half = rows // 2
    rc = row_count[0, 0].astype(jnp.float32)
    lanes = lane_ids(half)
    for comp in range(3):
        upper = state_ref[comp, 0:half, cols - LANES : cols]
        lower = roll(state_ref[comp, half:rows, cols - LANES : cols], LANES // 2, 1)
        left_ref[comp * half : (comp + 1) * half, :] = jnp.where(lanes >= LANES // 2, upper, lower)
    lanes = lane_ids(rows)
    packed = None
    for comp in range(3):
        ends = jnp.where(lanes < LANES // 2, state_ref[comp, :, 0:LANES], state_ref[comp, :, cols - LANES : cols])
        ends = roll(ends, 8 * comp + 4, 1)
        packed = ends if packed is None else jnp.where(lanes >= 8 * comp, ends, packed)
    strip_ref[0:24, :] = packed.T[0:24]
    strip_ref[24:32, :] = jnp.full((8, LANES), rc)
    left_ref[3 * half : 3 * half + 8, :] = jnp.full((8, LANES), rc)
    for comp in range(3):
        left_ref[3 * half + 2 * comp : 3 * half + 2 * comp + 2, :] = strip_ref[8 * comp + 2 : 8 * comp + 4, :]
    slab_ref[...] = state_ref[:, rows - SLAB : rows, :]


def pack_right(col_count, strip_ref, right_ref, counts_ref):
    cc = col_count[0, 0].astype(jnp.float32)
    counts = jnp.where(row_ids(8) == 6, strip_ref[24:32, :], cc)
    counts_ref[...] = counts
    right_ref[...] = counts
    for comp in range(3):
        right_ref[2 * comp : 2 * comp + 2, :] = strip_ref[8 * comp + 4 : 8 * comp + 6, :]


def is_odd():
    return lax.axis_index("row") % 2 == 1


def pack_rows(counts_ref, strip_ref, left_ref, right_ref, state_ref, inner_ref, rim_ref, within_ref, across_ref, edge_ref):
    rows, cols = state_ref.shape[1], state_ref.shape[2]
    half = rows // 2
    rc, cc = counts_ref[6:7, :], counts_ref[7:8, :]
    right = jnp.concatenate([right_ref[...], jnp.zeros((LANES - 8, LANES), jnp.float32)], axis=0).T
    lanes = lane_ids(rows)
    left_rc = left_ref[3 * half + 6 : 3 * half + 7, :]
    counts = jnp.where(lanes == LEFT_ROWS, left_rc, jnp.where(lanes == OWN_ROWS, rc, cc))
    odd = is_odd()
    packed_half = SLAB // 2
    low = lane_ids(packed_half) < LANES // 2

    def put(at, down, up):
        size = down.shape[0]
        within_ref[at : at + size, :] = jnp.where(odd, up, down)
        across_ref[at : at + size, :] = jnp.where(odd, down, up)

    ups, downs = [], []
    for comp in range(3):
        packed = left_ref[comp * half : (comp + 1) * half, :]
        left = jnp.concatenate([packed, roll(packed, LANES // 2, 1)], axis=0)
        inner = right if comp == 0 else roll(right, -2 * comp, 1)
        inner = jnp.where(lanes < LEFT_ROWS, inner, counts)
        rim = jnp.where(lanes >= LANES // 2, left, inner)
        rim_ref[comp] = rim
        last = packed[half - SLAB : half]
        downs.append(jnp.where(low, last[0:packed_half], roll(last[packed_half:SLAB], LANES // 2, 1)))
        ups += [state_ref[comp, 0:8, LANES * t : LANES * (t + 1)] for t in range(cols // LANES)] + [rim[0:8]]
        edge_ref[comp, 0:2, :] = left_ref[3 * half + 2 * comp : 3 * half + 2 * comp + 2, :]
        edge_ref[comp, 2:6, :] = strip_ref[8 * comp + 4 : 8 * comp + 8, :]
        edge_ref[comp, 6:10, :] = strip_ref[8 * comp : 8 * comp + 4, :]
        edge_ref[comp, 10:12, :] = right_ref[2 * comp : 2 * comp + 2, :]
        edge_ref[comp, 12:16, :] = strip_ref[8 * comp + 4 : 8 * comp + 8, :]
    downs.append(jnp.where(row_ids(8) == 6, cc, right_ref[...]))
    down = jnp.concatenate(downs, axis=0)
    up = jnp.concatenate(ups, axis=0)
    size = up.shape[0]
    put(0, down[0:size], up)
    put(size, down[size:DOWN_ROWS], down[size:DOWN_ROWS])
    across_ref[DOWN_ROWS : DOWN_ROWS + 8, :] = jnp.zeros((8, LANES), jnp.float32)


def inner_error(pos_ref, ext_ref, state_ref, error_ref, numbers_ref, columns, pos, ext, sems):
    rows = state_ref.shape[1]
    half = rows // 2
    copies = [pltpu.make_async_copy(src, dst, sems.at[k]) for k, (src, dst) in enumerate(((pos_ref, pos), (ext_ref, ext)))]
    for copy in copies:
        copy.start()
    for comp in range(3):
        first, second = state_ref[comp, :, 0:LANES], state_ref[comp, :, LANES : 2 * LANES]
        for parity in range(2):
            columns[comp, parity] = every_other(first, second, parity)
    size = 24
    for start in range(0, half - 2, size - 4):
        start = min(start, half - size)
        phases = [
            [
                [columns[c, y, pl.ds(2 * start + x, size, stride=2), :] for c in range(3)]
                for y in range(2)
            ]
            for x in range(2)
        ]
        error = coarse_error(phases)
        low = 0 if start == 0 else 2
        error_ref[start + low : start + size, :] = error[low:size]
    for copy in copies:
        copy.wait()
    pair = [v[0].astype(jnp.float32) for v in (pos, ext)]
    numbers = jnp.broadcast_to(pair[1][:, 1:2], (8, LANES))
    for k, number in enumerate((pair[0][:, 0:1], pair[0][:, 1:2], pair[1][:, 0:1])):
        numbers = jnp.where(row_ids(8) == k, number, numbers)
    numbers_ref[...] = numbers


def edge_phases(state_ref, slab_ref, above_rim, below, edge_ref, near_rows, columns, corners_ref):
    rows, cols = state_ref.shape[1], state_ref.shape[2]
    right = slice(cols, cols + LANES)
    lanes = lane_ids(8)
    packed_up, packed_down = None, None
    for comp in range(3):
        near_rows[comp, 0:2, :] = slab_ref[comp, SLAB - 2 : SLAB, :]
        near_rows[comp, 2:6, :] = state_ref[comp, 0:4, :]
        near_rows[comp, 6:10, :] = state_ref[comp, rows - 4 : rows, :]
        near_rows[comp, 10:12, :] = below[comp, 0:2, 0:cols]
        near_rows[comp, 12:16, :] = state_ref[comp, 0:4, :]
        first, second = near_rows[comp, :, 0:LANES], near_rows[comp, :, LANES : 2 * LANES]
        for parity in range(2):
            columns[comp, parity] = every_other(first, second, parity)

        def around_corner(body, rim):
            start = jnp.where(lanes < LANES // 2, body[:, 0:LANES], rim)
            end = jnp.where(lanes < LANES // 2, rim, body[:, cols - LANES : cols])
            first_six = (lanes >= 12 * comp) & (lanes < 12 * comp + 6)
            return jnp.where(first_six, roll(start, 12 * comp + 2, 1), roll(end, 12 * comp + 10, 1))

        up = around_corner(slab_ref[comp, SLAB - 8 : SLAB, :], above_rim[comp, SLAB - 8 : SLAB, :])
        down = around_corner(below[comp, :, 0:cols], below[comp, :, right])
        packed_up = up if comp == 0 else jnp.where(lanes >= 12 * comp, up, packed_up)
        packed_down = down if comp == 0 else jnp.where(lanes >= 12 * comp, down, packed_down)
    corners = jnp.concatenate([packed_down, jnp.ones((LANES - 16, LANES), jnp.float32), packed_up], axis=0).T
    for comp in range(3):
        corners_ref[comp, 0:12, :] = corners[12 * comp : 12 * comp + 12, :]
        corners_ref[comp, 12:16, :] = edge_ref[comp, 12:16, :]
    phases = []
    for x in range(2):
        phases.append([])
        for y in range(2):
            cells = []
            for comp, turned in ((0, 0), (1, 2), (2, 1)):
                by_row = columns[comp, y, pl.ds(x, 8, stride=2), :]
                own, outer = [ref[turned, pl.ds(x, 8, stride=2), :] for ref in (edge_ref, corners_ref)]
                cells.append(jnp.concatenate([by_row, every_other(own, outer, y)], axis=0))
            phases[-1].append(cells)
    return phases


def put_edges(error, edges):
    half_rows = error.shape[0]
    turned = jnp.concatenate([edges, jnp.zeros((LANES - 16, LANES), jnp.float32)], axis=0).T[0:half_rows]
    lanes, ids = lane_ids(half_rows), row_ids(half_rows)
    error = jnp.where(ids == 0, edges[1:2], jnp.where(ids == half_rows - 1, edges[4:5], error))
    return jnp.where(
        lanes == 0, roll(turned, -9, 1), jnp.where(lanes == LANES - 1, roll(turned, LANES - 13, 1), error)
    )


def minmod(lower_diff, upper_diff):
    smaller, larger = jnp.minimum(lower_diff, upper_diff), jnp.maximum(lower_diff, upper_diff)
    return jnp.maximum(smaller, jnp.minimum(larger, 0.0))


def axis_terms(cells, axis):
    depth, normal, tangent = cells[0], cells[1 + axis], cells[2 - axis]
    inverse_root = lax.rsqrt(depth)
    velocity = normal * (inverse_root * inverse_root)
    along = normal * velocity + 0.5 * depth * depth
    beside = tangent * velocity
    speed = jnp.abs(velocity) + depth * inverse_root
    return (normal, along, beside, speed) if axis == 0 else (normal, beside, along, speed)


def paired_change(near, far, axis):
    down = lambda v: roll(v, 1, axis)
    up = lambda v: roll(v, -1, axis)
    inner = [f - n for n, f in zip(near, far)]
    outer = [n - down(f) for n, f in zip(near, far)]
    near_half = [0.5 * minmod(o, i) for o, i in zip(outer, inner)]
    far_half = [0.5 * minmod(i, up(o)) for o, i in zip(outer, inner)]
    near_hi = [n + s for n, s in zip(near, near_half)]
    near_lo = [n - s for n, s in zip(near, near_half)]
    far_hi = [down(f + s) for f, s in zip(far, far_half)]
    far_lo = [f - s for f, s in zip(far, far_half)]
    terms = lambda cells: axis_terms(cells, axis)
    inner_flux = doubled_flux(near_hi, far_lo, terms(near_hi), terms(far_lo))
    outer_flux = doubled_flux(far_hi, near_lo, terms(far_hi), terms(near_lo))
    near_change = [i - o for i, o in zip(inner_flux, outer_flux)]
    far_change = [up(o) - i for i, o in zip(inner_flux, outer_flux)]
    return near_change, far_change


def doubled_first_step(cells):
    all_terms = cell_terms(*cells)
    changes = []
    for axis in (0, 1):
        terms = all_terms[axis]
        lower = [roll(f, 1, axis) for f in cells]
        lower_terms = [lower[1 + axis] if c == 0 else roll(terms[c], 1, axis) for c in range(4)]
        flux = doubled_flux(lower, cells, lower_terms, terms)
        own = [2.0 * terms[c] for c in range(3)]
        changes.append(
            (
                [o - f for o, f in zip(own, flux)],
                [roll(f, -1, axis) - o for o, f in zip(own, flux)],
            )
        )
    rows, cols = changes
    return [
        [
            [cells[c] - (0.5 * RATIO) * (rows[a][c] + cols[b][c]) for c in range(3)]
            for b in range(2)
        ]
        for a in range(2)
    ]


def patch_rows(cells):
    half = doubled_first_step(cells)
    by_row = [paired_change(half[0][b], half[1][b], 0) for b in range(2)]
    by_col = [paired_change(half[a][0], half[a][1], 1) for a in range(2)]
    size = cells[0].shape[0] - 8
    lanes = lane_ids(size)
    result = []
    for a in range(2):
        fine = [
            [half[a][b][c] - (0.5 * RATIO) * (by_row[b][a][c] + by_col[a][b][c]) for c in range(3)]
            for b in range(2)
        ]
        parts = []
        for c in range(3):
            pick = lanes // 2 + 2
            even = jnp.take_along_axis(fine[0][c][4 : 4 + size], pick, axis=1)
            odd = jnp.take_along_axis(fine[1][c][4 : 4 + size], pick, axis=1)
            parts.append(jnp.where(lanes % 2 == 0, even, odd))
        result.append(parts)
    return result


def sliding(load, start, size):
    group, shift = start // 8, start % 8
    turn = (8 - shift) % 8
    parts = [pltpu.roll(load(group + k), turn, 0) for k in range(size // 8 + 1)]
    keep = row_ids(8, parts[0].shape[1]) < 8 - shift
    return [jnp.where(keep, parts[k], parts[k + 1]) for k in range(size // 8)]


def scalar(values, row, lane):
    return values[row, lane].astype(jnp.int32)


def slab_rows(ref, first, count, size):
    last = SLAB // 8 - 1
    load = lambda k: ref[pl.ds(pl.multiple_of(first + 8 * jnp.minimum(k, last), 8), 8), :]
    return sliding(load, SLAB - count, size)


def column_move(first_cols, last_cols, side, here, right_count):
    lanes = lane_ids(8)
    head = jnp.where(lanes < here, pltpu.roll(side, here, 1), first_cols)
    outer = jnp.where(lanes < right_count, pltpu.roll(last_cols, right_count, 1), side)
    return head, jnp.where(lanes >= LANES // 2, side, outer)


def move_rows(state_ref, rim_ref, slab_ref, wide_ref):
    rows, cols = state_ref.shape[1], state_ref.shape[2]
    counts = rim_ref[0, 0:8, :]
    rc, cc, cc_right = [scalar(counts, 0, k) for k in (OWN_ROWS, OWN_COLS, RIGHT_COLS)]
    for comp in range(3):
        bodies = slab_rows(slab_ref.at[comp], 0, rc, SLAB)
        for k in range(rows // 8):
            part, at = slice(8 * k, 8 * k + 8), slice(8 * k + 8, 8 * k + 16)
            body = state_ref[comp, part, :]
            if 8 * k < SLAB:
                body = jnp.where(row_ids(8, cols) + 8 * k < rc, bodies[k], body)
                wide_ref[comp, at, LANES : LANES + cols] = body
                continue
            head, outer = column_move(
                body[:, 0:LANES], body[:, cols - LANES : cols], rim_ref[comp, part, :], cc, cc_right
            )
            wide_ref[comp, at, 0:LANES] = outer
            wide_ref[comp, at, LANES : 2 * LANES] = head
            wide_ref[comp, at, 2 * LANES : LANES + cols] = body[:, LANES:cols]
            wide_ref[comp, at, LANES + cols : 2 * LANES + cols] = outer


def finish(
    state_ref, rim_ref, slab_ref, rows_ref, within_ref, across_ref, inner_ref, edge_ref, numbers_ref,
    error_out, moved_out, patch_out,
    wide, window, near_rows, columns, corners, above_rim, below, error, patch, sems,
):
    rows, cols = state_ref.shape[1], state_ref.shape[2]
    right = slice(cols, cols + LANES)
    inside_wide = slice(LANES, LANES + cols)
    on_left = lane_ids(8) >= LANES // 2
    copies = [
        pltpu.make_async_copy(rows_ref.at[:, SLAB + 8 : rows + 8, inside_wide], moved_out.at[:, SLAB:rows, :], sems.at[0])
    ]
    copies[-1].start()

    odd = is_odd()
    packed_half = SLAB // 2
    beside = jnp.where(odd, within_ref[DOWN_ROWS - 8 : DOWN_ROWS, :], across_ref[DOWN_ROWS - 8 : DOWN_ROWS, :])
    turned = jnp.concatenate([beside, jnp.zeros((LANES - 8, LANES), jnp.float32)], axis=0).T[rows - SLAB : rows]
    lanes = lane_ids(packed_half)
    tiles = cols // LANES + 1
    for comp in range(3):
        at = slice(comp * packed_half, (comp + 1) * packed_half)
        packed = jnp.where(odd, within_ref[at, :], across_ref[at, :])
        inner = turned if comp == 0 else roll(turned, -2 * comp, 1)
        upper = jnp.where(lanes >= LANES // 2, roll(packed, LANES // 2, 1), inner[0:packed_half])
        lower = jnp.where(lanes >= LANES // 2, packed, inner[packed_half:SLAB])
        above_rim[comp, 0:packed_half, :] = upper
        above_rim[comp, packed_half:SLAB, :] = lower
        for t in range(tiles):
            at = slice(8 * (comp * tiles + t), 8 * (comp * tiles + t) + 8)
            below[comp, :, LANES * t : LANES * (t + 1)] = jnp.where(odd, across_ref[at, :], within_ref[at, :])

    edges = coarse_error(
        edge_phases(state_ref, slab_ref, above_rim, below, edge_ref, near_rows, columns, corners)
    )
    error[...] = put_edges(inner_ref[...], edges)

    own_counts, below_counts, numbers = rim_ref[0, 0:8, :], below[0, :, right], numbers_ref[...]
    cc, rc_left, rc_right, cc_right = [
        scalar(own_counts, 0, k) for k in (OWN_COLS, LEFT_ROWS, RIGHT_ROWS, RIGHT_COLS)
    ]
    cc_above, cc_above_right = [scalar(beside, k, 0) for k in (6, 7)]
    rc_below, cc_below, rc_below_left, rc_below_right, cc_below_right = [
        scalar(below_counts, 0, k) for k in (OWN_ROWS, OWN_COLS, LEFT_ROWS, RIGHT_ROWS, RIGHT_COLS)
    ]
    pos_row, pos_col, ext_row, ext_col = [scalar(numbers, k, 0) for k in range(4)]

    def put(comp, at, body, side, here, right_count):
        tail = body[:, LANES:cols]
        head, outer = column_move(body[:, 0:LANES], tail[:, cols - 2 * LANES :], side, here, right_count)
        wide[comp, at : at + 8, 0:LANES] = outer
        wide[comp, at : at + 8, LANES : 2 * LANES] = head
        wide[comp, at : at + 8, 2 * LANES : LANES + cols] = tail
        wide[comp, at : at + 8, LANES + cols : 2 * LANES + cols] = outer

    def moved_rim(ref, first, left, right_count, size):
        from_left = slab_rows(ref, first, left, size)
        from_right = slab_rows(ref, first, right_count, size)
        return [jnp.where(on_left, a, b) for a, b in zip(from_left, from_right)]

    for comp in range(3):
        sides = moved_rim(above_rim.at[comp], 0, rc_left, rc_right, SLAB)
        for k in range(SLAB // 8):
            side = rim_ref[comp, 8 * k : 8 * k + 8, :]
            side = jnp.where(row_ids(8) + 8 * k < jnp.where(on_left, rc_left, rc_right), sides[k], side)
            put(comp, 8 * k + 8, rows_ref[comp, 8 * k + 8 : 8 * k + 16, inside_wide], side, cc, cc_right)
        wide[comp, SLAB + 8 : rows + 8, :] = rows_ref[comp, SLAB + 8 : rows + 8, :]
        put(comp, 0, slab_ref[comp, SLAB - 8 : SLAB, :], above_rim[comp, SLAB - 8 : SLAB, :], cc_above, cc_above_right)
        (body,) = slab_rows(state_ref.at[comp], rows - SLAB, rc_below, 8)
        (side,) = moved_rim(rim_ref.at[comp], rows - SLAB, rc_below_left, rc_below_right, 8)
        body = jnp.where(row_ids(8, cols) < rc_below, body, below[comp, :, 0:cols])
        side = jnp.where(
            row_ids(8) < jnp.where(on_left, rc_below_left, rc_below_right), side, below[comp, :, right]
        )
        put(comp, rows + 8, body, side, cc_below, cc_below_right)
    copies += [
        pltpu.make_async_copy(wide.at[:, 8 : SLAB + 8, inside_wide], moved_out.at[:, 0:SLAB, :], sems.at[1]),
        pltpu.make_async_copy(error, error_out, sems.at[2]),
    ]

    first_lane = pos_col + LANES - 2
    tile, shift = first_lane // LANES, first_lane % LANES
    turn = (LANES - shift) % LANES
    keep = lane_ids(8) < LANES - shift
    for comp in range(3):

        def load(k):
            group = pl.ds(pl.multiple_of(8 * k, 8), 8)
            near = wide[comp, group, pl.ds(pl.multiple_of(LANES * tile, LANES), LANES)]
            far = wide[comp, group, pl.ds(pl.multiple_of(LANES * tile + LANES, LANES), LANES)]
            return jnp.where(keep, pltpu.roll(near, turn, 1), pltpu.roll(far, turn, 1))

        for k, part in enumerate(sliding(load, pos_row + 4, 72)):
            window[comp, 8 * k : 8 * k + 8, :] = part

    fine_rows, fine_cols = 2 * ext_row, 2 * ext_col
    size = PATCH_ROWS
    for start in range(0, PATCH, size):
        cells = [window[c, start : start + size + 8, :] for c in range(3)]
        fine = patch_rows(cells)
        lanes, ids = lane_ids(size), row_ids(size)
        for a in range(2):
            inside = (2 * (ids + start) + a < fine_rows) & (lanes < fine_cols)
            for c in range(3):
                patch[c, pl.ds(2 * start + a, size, stride=2), :] = jnp.where(inside, fine[a][c], 0.0)
        part = pl.ds(2 * start, 2 * size)
        copies.append(
            pltpu.make_async_copy(patch.at[:, part, :], patch_out.at[:, part, :], sems.at[3 + start // size])
        )
        copies[-1].start()
    for copy in copies[1:3]:
        copy.start()
    for copy in copies:
        copy.wait()


def around(axis, by):
    devices = lax.axis_size(axis)
    return [(i, (i + by) % devices) for i in range(devices)]


def in_vmem(value):
    return pltpu.with_memory_space_constraint(value, pltpu.VMEM)


def in_hbm(value):
    return pltpu.with_memory_space_constraint(value, pltpu.HBM)


def vmem(*shape):
    return pltpu.VMEM(shape, jnp.float32)


def per_device(state, row_count, col_count, patch_pos, patch_ext):
    rows, cols = state.shape[1], state.shape[2]
    width = cols + LANES
    half = rows // 2
    here = in_vmem(state)
    to_right, strip, slab = pl.pallas_call(
        pack_cols,
        out_shape=(vmem(3 * half + 8, LANES), vmem(32, LANES), vmem(3, SLAB, cols)),
        in_specs=[SMEM, VMEM],
        out_specs=(VMEM,) * 3,
        name="pack_cols",
    )(row_count, here)
    strip = in_vmem(strip)
    to_left, counts = pl.pallas_call(
        pack_right, out_shape=(vmem(8, LANES), vmem(8, LANES)), in_specs=[SMEM, VMEM], out_specs=(VMEM,) * 2, name="pack_right"
    )(col_count, strip)
    from_left = in_vmem(lax.ppermute(to_right, "col", around("col", 1)))
    from_right = in_vmem(lax.ppermute(to_left, "col", around("col", -1)))
    slab_above = in_vmem(lax.ppermute(slab, "row", around("row", 1)))
    inner, numbers = pl.pallas_call(
        inner_error,
        out_shape=(vmem(half, cols // 2), vmem(8, LANES)),
        in_specs=[ANY, ANY, VMEM],
        out_specs=(VMEM,) * 2,
        scratch_shapes=[
            vmem(3, 2, rows, LANES),
            pltpu.VMEM(patch_pos.shape, jnp.int32),
            pltpu.VMEM(patch_ext.shape, jnp.int32),
            pltpu.SemaphoreType.DMA((2,)),
        ],
        cost_estimate=pl.CostEstimate(flops=30_000_000, bytes_accessed=600_000, transcendentals=0),
        name="inner_error",
    )(in_hbm(patch_pos), in_hbm(patch_ext), here)
    inner = in_vmem(inner)
    rim, within, across, edge = pl.pallas_call(
        pack_rows,
        out_shape=(vmem(3, rows, LANES), vmem(DOWN_ROWS, LANES), vmem(DOWN_ROWS + 8, LANES), vmem(3, 16, LANES)),
        in_specs=[VMEM] * 6,
        out_specs=(VMEM,) * 4,
        name="pack_rows",
    )(in_vmem(counts), strip, from_left, from_right, here, inner)
    rim = in_vmem(rim)
    devices = lax.axis_size("row")
    from_within = in_vmem(lax.ppermute(within, "row", [(i, i ^ 1) for i in range(devices)]))
    from_across = in_vmem(
        lax.ppermute(across, "row", [(i, (i + (1 if i % 2 else -1)) % devices) for i in range(devices)])
    )
    moved_rows = in_vmem(pl.pallas_call(
        move_rows,
        out_shape=vmem(3, rows + 16, width + LANES),
        in_specs=[VMEM] * 3,
        out_specs=VMEM,
        cost_estimate=pl.CostEstimate(flops=3_000_000, bytes_accessed=1_000_000, transcendentals=0),
        name="move_rows",
    )(here, rim, slab_above))
    return pl.pallas_call(
        finish,
        out_shape=(f32(half, cols // 2), f32(3, rows, cols), f32(3, 2 * PATCH, 2 * PATCH)),
        in_specs=[VMEM] * 9,
        out_specs=(ANY,) * 3,
        scratch_shapes=[
            vmem(3, rows + 16, width + LANES),
            vmem(3, 72, LANES),
            vmem(3, 16, cols),
            vmem(3, 2, 16, LANES),
            vmem(3, 16, LANES),
            vmem(3, SLAB, LANES),
            vmem(3, 8, width),
            vmem(half, cols // 2),
            vmem(3, 2 * PATCH, 2 * PATCH),
            pltpu.SemaphoreType.DMA((3 + PATCH // PATCH_ROWS,)),
        ],
        compiler_params=PARAMS,
        name="finish",
    )(here, rim, slab_above, moved_rows, from_within, from_across, inner, edge, numbers)


def solution(mesh):
    placed = (
        P(None, "row", "col"),
        P("row", "col"),
        P("row", "col"),
        P("row", "col", None),
        P("row", "col", None),
    )
    return jax.shard_map(
        per_device,
        mesh=mesh,
        in_specs=placed,
        out_specs=(P("row", "col"), P(None, "row", "col"), P(None, "row", "col")),
        check_vma=False,
    )
```

time: 20.7 us -> 19 us (0.918)
  Pallas kernels: 7.05 us -> 5.45 us
  starting transfers between devices: 9.38 us -> 8.08 us
  local copies, waits for them, and re-layouts: 0.01 us -> 0.99 us
    ppermute x2, starting transfers between devices: 2.26 us -> 1.13 us  [the longest x1 1.12 us: per_device(): lax.ppermute(across, 'row', [(i, (i + (1 if i % 2 else -1)) % devices) fo...]
    unnamed x2 -> x4, local copies, waits for them, and re-layouts: 0.01 us -> 0.99 us
    pallas_call x1, Pallas kernels: 3.63 us -> 2.68 us  [per_device(): pl.pallas_call(finish, out_shape=(f32(half, cols // 2), f32(3, rows, cols...]
    ppermute x2, waiting for transfers between devices: 1.35 us -> 2.28 us  [the longest x1 1.31 us: per_device(): lax.ppermute(across, 'row', [(i, (i + (1 if i % 2 else -1)) % devices) fo...]
    ppermute x1, starting transfers between devices: 2.08 us -> 1.21 us  [per_device(): from_left = in_vmem(lax.ppermute(to_right, 'col', around('col', 1)))]
    ppermute x1, waiting for transfers between devices: 0.75 us -> 0.01 us  [per_device(): from_right = in_vmem(lax.ppermute(to_left, 'col', around('col', -1)))]
    pallas_call x3 -> x5, Pallas kernels: 3.43 us -> 2.77 us  [the longest x1 2.13 us: per_device(): pl.pallas_call(inner_error, out_shape=(vmem(half, cols // 2), vmem(8, LAN...]
    ppermute x1, starting transfers between devices: 2.08 us -> 2.65 us  [per_device(): slab_above = in_vmem(lax.ppermute(slab, 'row', around('row', 1)))]
  transfers between devices with their start and end apart: 5 -> 5, of which waited for: 2 -> 2; matrix products, arithmetic and copies ran while one was open for 0% -> 0% of each run, Pallas kernels for 11% -> 14%
where the time goes in v4:
time: 19 us; the launch traced here: 18.8 us
  starting transfers between devices  8.08 us (43%)
  Pallas kernels  5.45 us (29%)
  waiting for transfers between devices  2.28 us (12%)
  between operations  1.99 us (10%)
  local copies, waits for them, and re-layouts  0.99 us (5%)
    ppermute x1, starting transfers between devices, per_device(): from_right = in_vmem(lax.ppermute(to_left, 'col', around('col', -1)))  3.09 us
    pallas_call x1, Pallas kernels, per_device(): pl.pallas_call(finish, out_shape=(f32(half, cols // 2), f32(3, rows, cols...  2.68 us
    ppermute x1, starting transfers between devices, per_device(): slab_above = in_vmem(lax.ppermute(slab, 'row', around('row', 1)))  2.65 us
    pallas_call x1, Pallas kernels, per_device(): pl.pallas_call(inner_error, out_shape=(vmem(half, cols // 2), vmem(8, LAN...  2.13 us
    ppermute x1, waiting for transfers between devices, per_device(): lax.ppermute(across, 'row', [(i, (i + (1 if i % 2 else -1)) % devices) fo...  1.31 us
    ppermute x1, starting transfers between devices, per_device(): from_left = in_vmem(lax.ppermute(to_right, 'col', around('col', 1)))  1.21 us
    ppermute x1, starting transfers between devices, per_device(): lax.ppermute(across, 'row', [(i, (i + (1 if i % 2 else -1)) % devices) fo...  1.12 us
    unnamed x4, local copies, waits for them, and re-layouts  0.99 us
  transfers between devices with their start and end apart: 5, of which 2 were waited for; matrix products, arithmetic and copies ran while one was open for 0% of the time, Pallas kernels for 14%

profile of v4, /device:TPU:1, one launch (start us, length us, event | category | flops | bytes accessed | tf_op | source)
XLA Modules:
  0.0 18.8 jit_solution(14444100629865941681)
XLA Ops:
  1.3 0.0 copy-start
  1.3 1.0 %copy-done = f32[3,128,256]{2,1,0:T(8,128)S(1)} copy-done((f32[3,128,256]{2,1,0:T(8,128)S(1)}, f32[3,128,256]{2,1,0:T(8,128)}, u32[]{:S(2)}) %copy-start) | copy-done | bytes 393240
  2.3 0.0 copy-start.1
  2.3 0.2 %pack_cols.1 = (f32[200,128]{1,0:T(8,128)S(1)}, f32[32,128]{1,0:T(8,128)S(1)}, f32[3,64,256]{2,1,0:T(8,128)S(1)}) custom-call(s32[1,1]{1,0:T(1,128)S(6)} %copy.8.row_count, f32[3,128,256]{2,1,0:T(8,128)S(1)} %copy-done), custom_call_target="tpu_custom_call" | custom-call | tf_op jit(solution)/shard_map/pack_cols/pallas_call | solution.py:551
  2.5 2.6 %collective-permute-start.2 = (f32[3,64,256]{2,1,0:T(8,128)S(1)}, f32[3,64,256]{2,1,0:T(8,128)S(1)}, u32[]{:S(2)}, u32[]{:S(2)}) collective-permute-start(f32[3,64,256]{2,1,0:T(8,128)S(1)} %get-tuple-element.20), channel_id=1, source_target_pairs={{0,8},{8,16},{16,24},{24,0},{1,9},{9,17},{17,25},{25,1},{2,10},{10... | collective-permute-start | bytes 589832 | tf_op jit(solution)/shard_map/ppermute | solution.py:564
  5.1 1.2 %collective-permute-start = (f32[200,128]{1,0:T(8,128)S(1)}, f32[200,128]{1,0:T(8,128)S(1)}, u32[]{:S(2)}, u32[]{:S(2)}) collective-permute-start(f32[200,128]{1,0:T(8,128)S(1)} %get-tuple-element.16), channel_id=1, source_target_pairs={{0,1},{1,2},{2,3},{3,4},{4,5},{5,6},{6,7},{7,0},{8,9},{9,10},{10,1... | collective-permute-start | bytes 307208 | tf_op jit(solution)/shard_map/ppermute | solution.py:562
  7.0 3.1 %collective-permute-start.1 = (f32[8,128]{1,0:T(8,128)S(1)}, f32[8,128]{1,0:T(8,128)S(1)}, u32[]{:S(2)}, u32[]{:S(2)}) collective-permute-start(f32[8,128]{1,0:T(8,128)S(1)} %get-tuple-element.17), channel_id=1, source_target_pairs={{0,7},{1,0},{2,1},{3,2},{4,3},{5,4},{6,5},{7,6},{8,15},{9,8},{10,9... | collective-permute-start | bytes 12296 | tf_op jit(solution)/shard_map/ppermute | solution.py:563
  10.1 0.0 copy-done.1
  10.1 2.1 %inner_error.1 = (f32[64,128]{1,0:T(8,128)S(1)}, f32[8,128]{1,0:T(8,128)S(1)}) custom-call(s32[1,1,2]{2,1,0:T(1,128)} %pos_ref.1, s32[1,1,2]{2,1,0:T(1,128)} %ext_ref.1, f32[3,128,256]{2,1,0:T(8,128)S(1)} %copy-done.1), custom_call_target="tpu_custom_call" | custom-call | flops 30000000 | bytes 600000 | tf_op jit(solution)/shard_map/inner_error/pallas_call | solution.py:565
  12.2 0.0 collective-permute-done.1.right_ref
  12.2 0.0 collective-permute-done.left_ref
  12.2 0.2 %pack_rows.1 = (f32[3,128,128]{2,1,0:T(8,128)S(1)}, f32[104,128]{1,0:T(8,128)S(1)}, f32[112,128]{1,0:T(8,128)S(1)}, f32[3,16,128]{2,1,0:T(8,128)S(1)}) custom-call(f32[8,128]{1,0:T(8,128)S(1)} %get-tuple-element.15.counts_ref, f32[32,128]{1,0:T(8,128)S(1)} %get-tuple-element.14.strip_ref, f32[200,128]{1,0:T(8,128)S(1)} %collective-permute-done.left_ref, ...), custom_call_target="tpu_custom_call" | custom-call | tf_op jit(solution)/shard_map/pack_rows/pallas_call | solution.py:580
  12.4 1.1 %collective-permute-start.4 = (f32[112,128]{1,0:T(8,128)S(1)}, f32[112,128]{1,0:T(8,128)S(1)}, u32[]{:S(2)}, u32[]{:S(2)}) collective-permute-start(f32[112,128]{1,0:T(8,128)S(1)} %get-tuple-element.22), channel_id=1, source_target_pairs={{0,24},{8,16},{16,8},{24,0},{1,25},{9,17},{17,9},{25,1},{2,26},{10... | collective-permute-start | bytes 172040 | tf_op jit(solution)/shard_map/ppermute | solution.py:591
  13.6 0.0 collective-permute-start.3
  13.6 0.0 collective-permute-done.2.slab_ref
  13.6 0.3 %move_rows.1.rows_ref = f32[3,144,512]{2,1,0:T(8,128)S(1)} custom-call(f32[3,128,256]{2,1,0:T(8,128)S(1)} %copy-done.1, f32[3,128,128]{2,1,0:T(8,128)S(1)} %get-tuple-element.19.rim_ref, f32[3,64,256]{2,1,0:T(8,128)S(1)} %collective-permute-done.2.slab_ref), custom_call_target="tpu_custom_call" | custom-call | flops 3000000 | bytes 1000000 | tf_op jit(solution)/shard_map/move_rows/pallas_call | solution.py:593
  13.8 1.0 %collective-permute-done.3.within_ref = f32[104,128]{1,0:T(8,128)S(1)} collective-permute-done((f32[104,128]{1,0:T(8,128)S(1)}, f32[104,128]{1,0:T(8,128)S(1)}, u32[]{:S(2)}, u32[]{:S(2)}) %collective-permute-start.3) | collective-permute-done | bytes 53280 | tf_op jit(solution)/shard_map/ppermute | solution.py:589
  14.8 1.3 %collective-permute-done.4.across_ref = f32[112,128]{1,0:T(8,128)S(1)} collective-permute-done((f32[112,128]{1,0:T(8,128)S(1)}, f32[112,128]{1,0:T(8,128)S(1)}, u32[]{:S(2)}, u32[]{:S(2)}) %collective-permute-start.4) | collective-permute-done | bytes 57376 | tf_op jit(solution)/shard_map/ppermute | solution.py:591
  16.1 2.7 %finish.1 = (f32[64,128]{1,0:T(8,128)}, f32[3,128,256]{2,1,0:T(8,128)}, f32[3,128,128]{2,1,0:T(8,128)}) custom-call(f32[3,128,256]{2,1,0:T(8,128)S(1)} %copy-done.1, f32[3,128,128]{2,1,0:T(8,128)S(1)} %get-tuple-element.19.rim_ref, f32[3,64,256]{2,1,0:T(8,128)S(1)} %collective-permute-done.2.slab_ref, f32[3,144,512]{2,1,0:T(8,128)S(1)} %move_rows.1.rows_ref, ...), custom_call_target="tpu_custom_call" | custom-call | tf_op jit(solution)/shard_map/finish/pallas_call | solution.py:601
  (1 shorter events, 0.0 us)
Async XLA Ops:
  1.3 1.0 %copy-start = (f32[3,128,256]{2,1,0:T(8,128)S(1)}, f32[3,128,256]{2,1,0:T(8,128)}, u32[]{:S(2)}) copy-start(f32[3,128,256]{2,1,0:T(8,128)} %state_ref.9) | copy-start | bytes 1179652
  2.3 7.8 %copy-start.1 = (f32[3,128,256]{2,1,0:T(8,128)S(1)}, f32[3,128,256]{2,1,0:T(8,128)}, u32[]{:S(2)}) copy-start(f32[3,128,256]{2,1,0:T(8,128)} %state_ref.9) | copy-start | bytes 1179652
  2.5 11.1 %collective-permute-start.2 = (f32[3,64,256]{2,1,0:T(8,128)S(1)}, f32[3,64,256]{2,1,0:T(8,128)S(1)}, u32[]{:S(2)}, u32[]{:S(2)}) collective-permute-start(f32[3,64,256]{2,1,0:T(8,128)S(1)} %get-tuple-element.20), channel_id=1, source_target_pairs={{0,8},{8,16},{16,24},{24,0},{1,9},{9,17},{17,25},{25,1},{2,10},{10... | collective-permute-start | bytes 589832 | tf_op jit(solution)/shard_map/ppermute | solution.py:564
  5.1 7.1 %collective-permute-start = (f32[200,128]{1,0:T(8,128)S(1)}, f32[200,128]{1,0:T(8,128)S(1)}, u32[]{:S(2)}, u32[]{:S(2)}) collective-permute-start(f32[200,128]{1,0:T(8,128)S(1)} %get-tuple-element.16), channel_id=1, source_target_pairs={{0,1},{1,2},{2,3},{3,4},{4,5},{5,6},{6,7},{7,0},{8,9},{9,10},{10,1... | collective-permute-start | bytes 307208 | tf_op jit(solution)/shard_map/ppermute | solution.py:562
  7.0 5.2 %collective-permute-start.1 = (f32[8,128]{1,0:T(8,128)S(1)}, f32[8,128]{1,0:T(8,128)S(1)}, u32[]{:S(2)}, u32[]{:S(2)}) collective-permute-start(f32[8,128]{1,0:T(8,128)S(1)} %get-tuple-element.17), channel_id=1, source_target_pairs={{0,7},{1,0},{2,1},{3,2},{4,3},{5,4},{6,5},{7,6},{8,15},{9,8},{10,9... | collective-permute-start | bytes 12296 | tf_op jit(solution)/shard_map/ppermute | solution.py:563
  12.4 3.7 %collective-permute-start.4 = (f32[112,128]{1,0:T(8,128)S(1)}, f32[112,128]{1,0:T(8,128)S(1)}, u32[]{:S(2)}, u32[]{:S(2)}) collective-permute-start(f32[112,128]{1,0:T(8,128)S(1)} %get-tuple-element.22), channel_id=1, source_target_pairs={{0,24},{8,16},{16,8},{24,0},{1,25},{9,17},{17,9},{25,1},{2,26},{10... | collective-permute-start | bytes 172040 | tf_op jit(solution)/shard_map/ppermute | solution.py:591
  13.6 1.2 %collective-permute-start.3 = (f32[104,128]{1,0:T(8,128)S(1)}, f32[104,128]{1,0:T(8,128)S(1)}, u32[]{:S(2)}, u32[]{:S(2)}) collective-permute-start(f32[104,128]{1,0:T(8,128)S(1)} %get-tuple-element.21), channel_id=1, source_target_pairs={{0,8},{8,0},{16,24},{24,16},{1,9},{9,1},{17,25},{25,17},{2,10},{10... | collective-permute-start | bytes 159752 | tf_op jit(solution)/shard_map/ppermute | solution.py:589

commit v5 on v4

--- a/solution.py
+++ b/solution.py
@@ -9,6 +9,7 @@
 PATCH = 64
 LANES = 128
 PATCH_ROWS = 64
+UPPER = 32
 
 RATIO = 0.1
 ERR_SCALE = 10.0
@@ -120,7 +121,11 @@
     return jnp.where(lanes < LANES // 2, low, high)
 
 
-def pack_cols(row_count, state_ref, left_ref, strip_ref, slab_ref):
+def blank(out_ref):
+    out_ref[...] = jnp.zeros(out_ref.shape, jnp.float32)
+
+
+def pack_cols(row_count, blank_ref, state_ref, left_ref, strip_ref, slab_ref):
     rows, cols = state_ref.shape[1], state_ref.shape[2]
     half = rows // 2
     rc = row_count[0, 0].astype(jnp.float32)
@@ -156,7 +161,7 @@
     return lax.axis_index("row") % 2 == 1
 
 
-def pack_rows(counts_ref, strip_ref, left_ref, right_ref, state_ref, inner_ref, rim_ref, within_ref, across_ref, edge_ref):
+def pack_rows(counts_ref, strip_ref, left_ref, right_ref, state_ref, upper_ref, rim_ref, within_ref, across_ref, edge_ref):
     rows, cols = state_ref.shape[1], state_ref.shape[2]
     half = rows // 2
     rc, cc = counts_ref[6:7, :], counts_ref[7:8, :]
@@ -198,29 +203,30 @@
     across_ref[DOWN_ROWS : DOWN_ROWS + 8, :] = jnp.zeros((8, LANES), jnp.float32)
 
 
-def inner_error(pos_ref, ext_ref, state_ref, error_ref, numbers_ref, columns, pos, ext, sems):
-    rows = state_ref.shape[1]
-    half = rows // 2
+def inner_error(state_ref, first, size, columns):
+    part = slice(2 * first, 2 * (first + size))
+    for comp in range(3):
+        left, right = state_ref[comp, part, 0:LANES], state_ref[comp, part, LANES : 2 * LANES]
+        for parity in range(2):
+            columns[comp, parity] = every_other(left, right, parity)
+    phases = [
+        [[columns[c, y, pl.ds(x, size, stride=2), :] for c in range(3)] for y in range(2)]
+        for x in range(2)
+    ]
+    return coarse_error(phases)
+
+
+def upper_error(state_ref, error_ref, columns):
+    rows = error_ref.shape[0]
+    error_ref[...] = inner_error(state_ref, 0, rows + 8, columns)[0:rows]
+
+
+def lower_error(pos_ref, ext_ref, state_ref, rim_ref, error_ref, numbers_ref, columns, pos, ext, sems):
     copies = [pltpu.make_async_copy(src, dst, sems.at[k]) for k, (src, dst) in enumerate(((pos_ref, pos), (ext_ref, ext)))]
     for copy in copies:
         copy.start()
-    for comp in range(3):
-        first, second = state_ref[comp, :, 0:LANES], state_ref[comp, :, LANES : 2 * LANES]
-        for parity in range(2):
-            columns[comp, parity] = every_other(first, second, parity)
-    size = 24
-    for start in range(0, half - 2, size - 4):
-        start = min(start, half - size)
-        phases = [
-            [
-                [columns[c, y, pl.ds(2 * start + x, size, stride=2), :] for c in range(3)]
-                for y in range(2)
-            ]
-            for x in range(2)
-        ]
-        error = coarse_error(phases)
-        low = 0 if start == 0 else 2
-        error_ref[start + low : start + size, :] = error[low:size]
+    rows = error_ref.shape[0]
+    error_ref[...] = inner_error(state_ref, state_ref.shape[1] // 2 - rows - 8, rows + 8, columns)[8 : rows + 8]
     for copy in copies:
         copy.wait()
     pair = [v[0].astype(jnp.float32) for v in (pos, ext)]
@@ -411,7 +417,7 @@
 
 
 def finish(
-    state_ref, rim_ref, slab_ref, rows_ref, within_ref, across_ref, inner_ref, edge_ref, numbers_ref,
+    state_ref, rim_ref, slab_ref, rows_ref, within_ref, across_ref, upper_ref, lower_ref, edge_ref, numbers_ref,
     error_out, moved_out, patch_out,
     wide, window, near_rows, columns, corners, above_rim, below, error, patch, sems,
 ):
@@ -445,7 +451,7 @@
     edges = coarse_error(
         edge_phases(state_ref, slab_ref, above_rim, below, edge_ref, near_rows, columns, corners)
     )
-    error[...] = put_edges(inner_ref[...], edges)
+    error[...] = put_edges(jnp.concatenate([upper_ref[...], lower_ref[...]], axis=0), edges)
 
     own_counts, below_counts, numbers = rim_ref[0, 0:8, :], below[0, :, right], numbers_ref[...]
     cc, rc_left, rc_right, cc_right = [
@@ -548,13 +554,20 @@
     width = cols + LANES
     half = rows // 2
     here = in_vmem(state)
+    ahead = pl.pallas_call(
+        blank,
+        out_shape=vmem(8, LANES),
+        out_specs=VMEM,
+        cost_estimate=pl.CostEstimate(flops=10_000_000_000, bytes_accessed=10_000_000, transcendentals=0),
+        name="ahead",
+    )()
     to_right, strip, slab = pl.pallas_call(
         pack_cols,
         out_shape=(vmem(3 * half + 8, LANES), vmem(32, LANES), vmem(3, SLAB, cols)),
-        in_specs=[SMEM, VMEM],
+        in_specs=[SMEM, VMEM, VMEM],
         out_specs=(VMEM,) * 3,
         name="pack_cols",
-    )(row_count, here)
+    )(row_count, in_vmem(ahead), here)
     strip = in_vmem(strip)
     to_left, counts = pl.pallas_call(
         pack_right, out_shape=(vmem(8, LANES), vmem(8, LANES)), in_specs=[SMEM, VMEM], out_specs=(VMEM,) * 2, name="pack_right"
@@ -562,29 +575,37 @@
     from_left = in_vmem(lax.ppermute(to_right, "col", around("col", 1)))
     from_right = in_vmem(lax.ppermute(to_left, "col", around("col", -1)))
     slab_above = in_vmem(lax.ppermute(slab, "row", around("row", 1)))
-    inner, numbers = pl.pallas_call(
-        inner_error,
-        out_shape=(vmem(half, cols // 2), vmem(8, LANES)),
-        in_specs=[ANY, ANY, VMEM],
-        out_specs=(VMEM,) * 2,
-        scratch_shapes=[
-            vmem(3, 2, rows, LANES),
-            pltpu.VMEM(patch_pos.shape, jnp.int32),
-            pltpu.VMEM(patch_ext.shape, jnp.int32),
-            pltpu.SemaphoreType.DMA((2,)),
-        ],
-        cost_estimate=pl.CostEstimate(flops=30_000_000, bytes_accessed=600_000, transcendentals=0),
-        name="inner_error",
-    )(in_hbm(patch_pos), in_hbm(patch_ext), here)
-    inner = in_vmem(inner)
+    upper = in_vmem(pl.pallas_call(
+        upper_error,
+        out_shape=vmem(UPPER, cols // 2),
+        in_specs=[VMEM],
+        out_specs=VMEM,
+        scratch_shapes=[vmem(3, 2, 2 * UPPER + 16, LANES)],
+        cost_estimate=pl.CostEstimate(flops=15_000_000, bytes_accessed=300_000, transcendentals=0),
+        name="upper_error",
+    )(here))
     rim, within, across, edge = pl.pallas_call(
         pack_rows,
         out_shape=(vmem(3, rows, LANES), vmem(DOWN_ROWS, LANES), vmem(DOWN_ROWS + 8, LANES), vmem(3, 16, LANES)),
         in_specs=[VMEM] * 6,
         out_specs=(VMEM,) * 4,
         name="pack_rows",
-    )(in_vmem(counts), strip, from_left, from_right, here, inner)
+    )(in_vmem(counts), strip, from_left, from_right, here, upper)
     rim = in_vmem(rim)
+    lower, numbers = pl.pallas_call(
+        lower_error,
+        out_shape=(vmem(half - UPPER, cols // 2), vmem(8, LANES)),
+        in_specs=[ANY, ANY, VMEM, VMEM],
+        out_specs=(VMEM,) * 2,
+        scratch_shapes=[
+            vmem(3, 2, 2 * (half - UPPER) + 16, LANES),
+            pltpu.VMEM(patch_pos.shape, jnp.int32),
+            pltpu.VMEM(patch_ext.shape, jnp.int32),
+            pltpu.SemaphoreType.DMA((2,)),
+        ],
+        cost_estimate=pl.CostEstimate(flops=15_000_000, bytes_accessed=300_000, transcendentals=0),
+        name="lower_error",
+    )(in_hbm(patch_pos), in_hbm(patch_ext), here, rim)
     devices = lax.axis_size("row")
     from_within = in_vmem(lax.ppermute(within, "row", [(i, i ^ 1) for i in range(devices)]))
     from_across = in_vmem(
@@ -601,7 +622,7 @@
     return pl.pallas_call(
         finish,
         out_shape=(f32(half, cols // 2), f32(3, rows, cols), f32(3, 2 * PATCH, 2 * PATCH)),
-        in_specs=[VMEM] * 9,
+        in_specs=[VMEM] * 10,
         out_specs=(ANY,) * 3,
         scratch_shapes=[
             vmem(3, rows + 16, width + LANES),
@@ -617,7 +638,7 @@
         ],
         compiler_params=PARAMS,
         name="finish",
-    )(here, rim, slab_above, moved_rows, from_within, from_across, inner, edge, numbers)
+    )(here, rim, slab_above, moved_rows, from_within, from_across, upper, lower, edge, numbers)
 
 
 def solution(mesh):

time: 19 us -> 17.8 us (0.937)
  the two profiles are of different devices: /device:TPU:1 before, /device:TPU:0 now
where the time goes in v5:
time: 17.8 us; the launch traced here: 17.6 us
  starting transfers between devices  8.5 us (48%)
  Pallas kernels  4.88 us (27%)
  between operations  2.05 us (12%)
  waiting for transfers between devices  1.88 us (11%)
  local copies, waits for them, and re-layouts  0.3 us (2%)
    ppermute x1, starting transfers between devices, per_device(): from_right = in_vmem(lax.ppermute(to_left, 'col', around('col', -1)))  3.1 us
    pallas_call x1, Pallas kernels, per_device(): pl.pallas_call(finish, out_shape=(f32(half, cols // 2), f32(3, rows, cols...  2.68 us
    ppermute x1, starting transfers between devices, per_device(): from_left = in_vmem(lax.ppermute(to_right, 'col', around('col', 1)))  2.55 us
    ppermute x1, starting transfers between devices, per_device(): lax.ppermute(across, 'row', [(i, (i + (1 if i % 2 else -1)) % devices) fo...  1.65 us
    ppermute x1, waiting for transfers between devices, per_device(): from_left = in_vmem(lax.ppermute(to_right, 'col', around('col', 1)))  0.87 us
    pallas_call x1, Pallas kernels, per_device(): pl.pallas_call(lower_error, out_shape=(vmem(half - UPPER, cols // 2), vme...  0.84 us
    pallas_call x1, Pallas kernels, per_device(): pl.pallas_call(upper_error, out_shape=vmem(UPPER, cols // 2), in_specs=[V...  0.73 us
    ppermute x1, starting transfers between devices, per_device(): lax.ppermute(within, 'row', [(i, i ^ 1) for i in range(devices)])  0.72 us
  transfers between devices with their start and end apart: 5, of which 3 were waited for; matrix products, arithmetic and copies ran while one was open for 0% of the time, Pallas kernels for 11%

profile of v5, /device:TPU:0, one launch (start us, length us, event | category | flops | bytes accessed | tf_op | source)
XLA Modules:
  0.0 17.6 jit_solution(3540874384433219701)
XLA Ops:
  0.6 0.0 copy-start
  1.3 0.3 %copy-done = f32[3,128,256]{2,1,0:T(8,128)S(1)} copy-done((f32[3,128,256]{2,1,0:T(8,128)S(1)}, f32[3,128,256]{2,1,0:T(8,128)}, u32[]{:S(2)}) %copy-start) | copy-done | bytes 393240
  1.6 0.2 %pack_cols.1 = (f32[200,128]{1,0:T(8,128)S(1)}, f32[32,128]{1,0:T(8,128)S(1)}, f32[3,64,256]{2,1,0:T(8,128)S(1)}) custom-call(s32[1,1]{1,0:T(1,128)S(6)} %copy.8.row_count, f32[8,128]{1,0:T(8,128)S(1)} %ahead.1.blank_ref, f32[3,128,256]{2,1,0:T(8,128)S(1)} %copy-done), custom_call_target="tpu_custom_call" | custom-call | tf_op jit(solution)/shard_map/pack_cols/pallas_call | solution.py:564
  1.8 0.5 %collective-permute-start.2 = (f32[3,64,256]{2,1,0:T(8,128)S(1)}, f32[3,64,256]{2,1,0:T(8,128)S(1)}, u32[]{:S(2)}, u32[]{:S(2)}) collective-permute-start(f32[3,64,256]{2,1,0:T(8,128)S(1)} %get-tuple-element.19), channel_id=1, source_target_pairs={{0,8},{8,16},{16,24},{24,0},{1,9},{9,17},{17,25},{25,1},{2,10},{10... | collective-permute-start | bytes 589832 | tf_op jit(solution)/shard_map/ppermute | solution.py:577
  2.3 2.6 %collective-permute-start = (f32[200,128]{1,0:T(8,128)S(1)}, f32[200,128]{1,0:T(8,128)S(1)}, u32[]{:S(2)}, u32[]{:S(2)}) collective-permute-start(f32[200,128]{1,0:T(8,128)S(1)} %get-tuple-element.16), channel_id=1, source_target_pairs={{0,1},{1,2},{2,3},{3,4},{4,5},{5,6},{6,7},{7,0},{8,9},{9,10},{10,1... | collective-permute-start | bytes 307208 | tf_op jit(solution)/shard_map/ppermute | solution.py:575
  5.5 3.1 %collective-permute-start.1 = (f32[8,128]{1,0:T(8,128)S(1)}, f32[8,128]{1,0:T(8,128)S(1)}, u32[]{:S(2)}, u32[]{:S(2)}) collective-permute-start(f32[8,128]{1,0:T(8,128)S(1)} %get-tuple-element.17), channel_id=1, source_target_pairs={{0,7},{1,0},{2,1},{3,2},{4,3},{5,4},{6,5},{7,6},{8,15},{9,8},{10,9... | collective-permute-start | bytes 12296 | tf_op jit(solution)/shard_map/ppermute | solution.py:576
  8.6 0.7 %upper_error.1.upper_ref = f32[32,128]{1,0:T(8,128)S(1)} custom-call(f32[3,128,256]{2,1,0:T(8,128)S(1)} %copy-done), custom_call_target="tpu_custom_call" | custom-call | flops 15000000 | bytes 300000 | tf_op jit(solution)/shard_map/upper_error/pallas_call | solution.py:578
  9.4 0.6 %collective-permute-done.1.right_ref = f32[8,128]{1,0:T(8,128)S(1)} collective-permute-done((f32[8,128]{1,0:T(8,128)S(1)}, f32[8,128]{1,0:T(8,128)S(1)}, u32[]{:S(2)}, u32[]{:S(2)}) %collective-permute-start.1) | collective-permute-done | bytes 4128 | tf_op jit(solution)/shard_map/ppermute | solution.py:576
  9.9 0.9 %collective-permute-done.left_ref = f32[200,128]{1,0:T(8,128)S(1)} collective-permute-done((f32[200,128]{1,0:T(8,128)S(1)}, f32[200,128]{1,0:T(8,128)S(1)}, u32[]{:S(2)}, u32[]{:S(2)}) %collective-permute-start) | collective-permute-done | bytes 102432 | tf_op jit(solution)/shard_map/ppermute | solution.py:575
  10.8 0.2 %pack_rows.1 = (f32[3,128,128]{2,1,0:T(8,128)S(1)}, f32[104,128]{1,0:T(8,128)S(1)}, f32[112,128]{1,0:T(8,128)S(1)}, f32[3,16,128]{2,1,0:T(8,128)S(1)}) custom-call(f32[8,128]{1,0:T(8,128)S(1)} %get-tuple-element.15.counts_ref, f32[32,128]{1,0:T(8,128)S(1)} %get-tuple-element.14.strip_ref, f32[200,128]{1,0:T(8,128)S(1)} %collective-permute-done.left_ref, ...), custom_call_target="tpu_custom_call" | custom-call | tf_op jit(solution)/shard_map/pack_rows/pallas_call | solution.py:587
  11.0 1.6 %collective-permute-start.4 = (f32[112,128]{1,0:T(8,128)S(1)}, f32[112,128]{1,0:T(8,128)S(1)}, u32[]{:S(2)}, u32[]{:S(2)}) collective-permute-start(f32[112,128]{1,0:T(8,128)S(1)} %get-tuple-element.21), channel_id=1, source_target_pairs={{0,24},{8,16},{16,8},{24,0},{1,25},{9,17},{17,9},{25,1},{2,26},{10... | collective-permute-start | bytes 172040 | tf_op jit(solution)/shard_map/ppermute | solution.py:612
  12.7 0.7 %collective-permute-start.3 = (f32[104,128]{1,0:T(8,128)S(1)}, f32[104,128]{1,0:T(8,128)S(1)}, u32[]{:S(2)}, u32[]{:S(2)}) collective-permute-start(f32[104,128]{1,0:T(8,128)S(1)} %get-tuple-element.20), channel_id=1, source_target_pairs={{0,8},{8,0},{16,24},{24,16},{1,9},{9,1},{17,25},{25,17},{2,10},{10... | collective-permute-start | bytes 159752 | tf_op jit(solution)/shard_map/ppermute | solution.py:610
  13.4 0.8 %lower_error.1 = (f32[32,128]{1,0:T(8,128)S(1)}, f32[8,128]{1,0:T(8,128)S(1)}) custom-call(s32[1,1,2]{2,1,0:T(1,128)} %pos_ref.1, s32[1,1,2]{2,1,0:T(1,128)} %ext_ref.1, f32[3,128,256]{2,1,0:T(8,128)S(1)} %copy-done, f32[3,128,128]{2,1,0:T(8,128)S(1)} %get-tuple-element.18.rim_ref), custom_call_target="tpu_custom_call" | custom-call | flops 15000000 | bytes 300000 | tf_op jit(solution)/shard_map/lower_error/pallas_call | solution.py:595
  14.2 0.0 collective-permute-done.2.slab_ref
  14.2 0.3 %move_rows.1.rows_ref = f32[3,144,512]{2,1,0:T(8,128)S(1)} custom-call(f32[3,128,256]{2,1,0:T(8,128)S(1)} %copy-done, f32[3,128,128]{2,1,0:T(8,128)S(1)} %get-tuple-element.18.rim_ref, f32[3,64,256]{2,1,0:T(8,128)S(1)} %collective-permute-done.2.slab_ref), custom_call_target="tpu_custom_call" | custom-call | flops 3000000 | bytes 1000000 | tf_op jit(solution)/shard_map/move_rows/pallas_call | solution.py:614
  14.5 0.0 collective-permute-done.3.within_ref
  14.5 0.4 %collective-permute-done.4.across_ref = f32[112,128]{1,0:T(8,128)S(1)} collective-permute-done((f32[112,128]{1,0:T(8,128)S(1)}, f32[112,128]{1,0:T(8,128)S(1)}, u32[]{:S(2)}, u32[]{:S(2)}) %collective-permute-start.4) | collective-permute-done | bytes 57376 | tf_op jit(solution)/shard_map/ppermute | solution.py:612
  14.9 2.7 %finish.1 = (f32[64,128]{1,0:T(8,128)}, f32[3,128,256]{2,1,0:T(8,128)}, f32[3,128,128]{2,1,0:T(8,128)}) custom-call(f32[3,128,256]{2,1,0:T(8,128)S(1)} %copy-done, f32[3,128,128]{2,1,0:T(8,128)S(1)} %get-tuple-element.18.rim_ref, f32[3,64,256]{2,1,0:T(8,128)S(1)} %collective-permute-done.2.slab_ref, f32[3,144,512]{2,1,0:T(8,128)S(1)} %move_rows.1.rows_ref, ...), custom_call_target="tpu_custom_call" | custom-call | tf_op jit(solution)/shard_map/finish/pallas_call | solution.py:622
  (2 shorter events, 0.0 us)
Async XLA Ops:
  0.6 1.0 %copy-start = (f32[3,128,256]{2,1,0:T(8,128)S(1)}, f32[3,128,256]{2,1,0:T(8,128)}, u32[]{:S(2)}) copy-start(f32[3,128,256]{2,1,0:T(8,128)} %state_ref.11) | copy-start | bytes 1179652
  1.8 12.4 %collective-permute-start.2 = (f32[3,64,256]{2,1,0:T(8,128)S(1)}, f32[3,64,256]{2,1,0:T(8,128)S(1)}, u32[]{:S(2)}, u32[]{:S(2)}) collective-permute-start(f32[3,64,256]{2,1,0:T(8,128)S(1)} %get-tuple-element.19), channel_id=1, source_target_pairs={{0,8},{8,16},{16,24},{24,0},{1,9},{9,17},{17,25},{25,1},{2,10},{10... | collective-permute-start | bytes 589832 | tf_op jit(solution)/shard_map/ppermute | solution.py:577
  2.3 8.5 %collective-permute-start = (f32[200,128]{1,0:T(8,128)S(1)}, f32[200,128]{1,0:T(8,128)S(1)}, u32[]{:S(2)}, u32[]{:S(2)}) collective-permute-start(f32[200,128]{1,0:T(8,128)S(1)} %get-tuple-element.16), channel_id=1, source_target_pairs={{0,1},{1,2},{2,3},{3,4},{4,5},{5,6},{6,7},{7,0},{8,9},{9,10},{10,1... | collective-permute-start | bytes 307208 | tf_op jit(solution)/shard_map/ppermute | solution.py:575
  5.5 4.4 %collective-permute-start.1 = (f32[8,128]{1,0:T(8,128)S(1)}, f32[8,128]{1,0:T(8,128)S(1)}, u32[]{:S(2)}, u32[]{:S(2)}) collective-permute-start(f32[8,128]{1,0:T(8,128)S(1)} %get-tuple-element.17), channel_id=1, source_target_pairs={{0,7},{1,0},{2,1},{3,2},{4,3},{5,4},{6,5},{7,6},{8,15},{9,8},{10,9... | collective-permute-start | bytes 12296 | tf_op jit(solution)/shard_map/ppermute | solution.py:576
  11.0 3.9 %collective-permute-start.4 = (f32[112,128]{1,0:T(8,128)S(1)}, f32[112,128]{1,0:T(8,128)S(1)}, u32[]{:S(2)}, u32[]{:S(2)}) collective-permute-start(f32[112,128]{1,0:T(8,128)S(1)} %get-tuple-element.21), channel_id=1, source_target_pairs={{0,24},{8,16},{16,8},{24,0},{1,25},{9,17},{17,9},{25,1},{2,26},{10... | collective-permute-start | bytes 172040 | tf_op jit(solution)/shard_map/ppermute | solution.py:612
  12.7 1.9 %collective-permute-start.3 = (f32[104,128]{1,0:T(8,128)S(1)}, f32[104,128]{1,0:T(8,128)S(1)}, u32[]{:S(2)}, u32[]{:S(2)}) collective-permute-start(f32[104,128]{1,0:T(8,128)S(1)} %get-tuple-element.20), channel_id=1, source_target_pairs={{0,8},{8,0},{16,24},{24,16},{1,9},{9,1},{17,25},{25,17},{2,10},{10... | collective-permute-start | bytes 159752 | tf_op jit(solution)/shard_map/ppermute | solution.py:610

commit v6 on v5

--- a/solution.py
+++ b/solution.py
@@ -522,10 +522,9 @@
             for c in range(3):
                 patch[c, pl.ds(2 * start + a, size, stride=2), :] = jnp.where(inside, fine[a][c], 0.0)
         part = pl.ds(2 * start, 2 * size)
-        copies.append(
-            pltpu.make_async_copy(patch.at[:, part, :], patch_out.at[:, part, :], sems.at[3 + start // size])
-        )
-        copies[-1].start()
+        for c in range(3):
+            copies.append(pltpu.make_async_copy(patch.at[c, part, :], patch_out.at[c, part, :], sems.at[3 + c]))
+            copies[-1].start()
     for copy in copies[1:3]:
         copy.start()
     for copy in copies:
@@ -589,6 +588,7 @@
         out_shape=(vmem(3, rows, LANES), vmem(DOWN_ROWS, LANES), vmem(DOWN_ROWS + 8, LANES), vmem(3, 16, LANES)),
         in_specs=[VMEM] * 6,
         out_specs=(VMEM,) * 4,
+        cost_estimate=pl.CostEstimate(flops=3_000_000_000, bytes_accessed=600_000, transcendentals=0),
         name="pack_rows",
     )(in_vmem(counts), strip, from_left, from_right, here, upper)
     rim = in_vmem(rim)
@@ -634,7 +634,7 @@
             vmem(3, 8, width),
             vmem(half, cols // 2),
             vmem(3, 2 * PATCH, 2 * PATCH),
-            pltpu.SemaphoreType.DMA((3 + PATCH // PATCH_ROWS,)),
+            pltpu.SemaphoreType.DMA((6,)),
         ],
         compiler_params=PARAMS,
         name="finish",

time: 17.8 us -> 17.6 us (0.989)
  starting transfers between devices: 8.5 us -> 7.76 us
  waiting for transfers between devices: 1.88 us -> 2.46 us
    ppermute x1, starting transfers between devices: 1.65 us -> 0.37 us  [per_device(): lax.ppermute(across, 'row', [(i, (i + (1 if i % 2 else -1)) % devices) fo...]
    ppermute x1, starting transfers between devices: 0.72 us -> 1.33 us  [per_device(): lax.ppermute(within, 'row', [(i, i ^ 1) for i in range(devices)])]
    ppermute x1, starting transfers between devices: 0.47 us -> 0.01 us  [per_device(): slab_above = in_vmem(lax.ppermute(slab, 'row', around('row', 1)))]
    ppermute x1, waiting for transfers between devices: 0.41 us -> 0.85 us  [per_device(): lax.ppermute(across, 'row', [(i, (i + (1 if i % 2 else -1)) % devices) fo...]
    ppermute x1, starting transfers between devices: 2.55 us -> 2.96 us  [per_device(): from_left = in_vmem(lax.ppermute(to_right, 'col', around('col', 1)))]
  transfers between devices with their start and end apart: 5 -> 5, of which waited for: 3 -> 4; matrix products, arithmetic and copies ran while one was open for 0% -> 0% of each run, Pallas kernels for 11% -> 12%
where the time goes in v6:
time: 17.6 us; the launch traced here: 17.5 us
  starting transfers between devices  7.76 us (44%)
  Pallas kernels  4.9 us (28%)
  waiting for transfers between devices  2.46 us (14%)
  between operations  2.04 us (12%)
  local copies, waits for them, and re-layouts  0.3 us (2%)
    ppermute x1, starting transfers between devices, per_device(): from_right = in_vmem(lax.ppermute(to_left, 'col', around('col', -1)))  3.1 us
    ppermute x1, starting transfers between devices, per_device(): from_left = in_vmem(lax.ppermute(to_right, 'col', around('col', 1)))  2.96 us
    pallas_call x1, Pallas kernels, per_device(): pl.pallas_call(finish, out_shape=(f32(half, cols // 2), f32(3, rows, cols...  2.7 us
    ppermute x1, starting transfers between devices, per_device(): lax.ppermute(within, 'row', [(i, i ^ 1) for i in range(devices)])  1.33 us
    ppermute x1, waiting for transfers between devices, per_device(): from_left = in_vmem(lax.ppermute(to_right, 'col', around('col', 1)))  0.87 us
    ppermute x1, waiting for transfers between devices, per_device(): lax.ppermute(across, 'row', [(i, (i + (1 if i % 2 else -1)) % devices) fo...  0.85 us
    pallas_call x1, Pallas kernels, per_device(): pl.pallas_call(lower_error, out_shape=(vmem(half - UPPER, cols // 2), vme...  0.84 us
    pallas_call x1, Pallas kernels, per_device(): pl.pallas_call(upper_error, out_shape=vmem(UPPER, cols // 2), in_specs=[V...  0.73 us
  transfers between devices with their start and end apart: 5, of which 4 were waited for; matrix products, arithmetic and copies ran while one was open for 0% of the time, Pallas kernels for 12%

profile of v6, /device:TPU:0, one launch (start us, length us, event | category | flops | bytes accessed | tf_op | source)
XLA Modules:
  0.0 17.5 jit_solution(6090624703954042016)
XLA Ops:
  0.6 0.0 copy-start
  1.3 0.3 %copy-done = f32[3,128,256]{2,1,0:T(8,128)S(1)} copy-done((f32[3,128,256]{2,1,0:T(8,128)S(1)}, f32[3,128,256]{2,1,0:T(8,128)}, u32[]{:S(2)}) %copy-start) | copy-done | bytes 393240
  1.6 0.2 %pack_cols.1 = (f32[200,128]{1,0:T(8,128)S(1)}, f32[32,128]{1,0:T(8,128)S(1)}, f32[3,64,256]{2,1,0:T(8,128)S(1)}) custom-call(s32[1,1]{1,0:T(1,128)S(6)} %copy.8.row_count, f32[8,128]{1,0:T(8,128)S(1)} %ahead.1.blank_ref, f32[3,128,256]{2,1,0:T(8,128)S(1)} %copy-done), custom_call_target="tpu_custom_call" | custom-call | tf_op jit(solution)/shard_map/pack_cols/pallas_call | solution.py:563
  1.8 3.0 %collective-permute-start = (f32[200,128]{1,0:T(8,128)S(1)}, f32[200,128]{1,0:T(8,128)S(1)}, u32[]{:S(2)}, u32[]{:S(2)}) collective-permute-start(f32[200,128]{1,0:T(8,128)S(1)} %get-tuple-element.16), channel_id=1, source_target_pairs={{0,1},{1,2},{2,3},{3,4},{4,5},{5,6},{6,7},{7,0},{8,9},{9,10},{10,1... | collective-permute-start | bytes 307208 | tf_op jit(solution)/shard_map/ppermute | solution.py:574
  5.5 3.1 %collective-permute-start.1 = (f32[8,128]{1,0:T(8,128)S(1)}, f32[8,128]{1,0:T(8,128)S(1)}, u32[]{:S(2)}, u32[]{:S(2)}) collective-permute-start(f32[8,128]{1,0:T(8,128)S(1)} %get-tuple-element.17), channel_id=1, source_target_pairs={{0,7},{1,0},{2,1},{3,2},{4,3},{5,4},{6,5},{7,6},{8,15},{9,8},{10,9... | collective-permute-start | bytes 12296 | tf_op jit(solution)/shard_map/ppermute | solution.py:575
  8.6 0.0 collective-permute-start.2
  8.6 0.7 %upper_error.1.upper_ref = f32[32,128]{1,0:T(8,128)S(1)} custom-call(f32[3,128,256]{2,1,0:T(8,128)S(1)} %copy-done), custom_call_target="tpu_custom_call" | custom-call | flops 15000000 | bytes 300000 | tf_op jit(solution)/shard_map/upper_error/pallas_call | solution.py:577
  9.3 0.6 %collective-permute-done.1.right_ref = f32[8,128]{1,0:T(8,128)S(1)} collective-permute-done((f32[8,128]{1,0:T(8,128)S(1)}, f32[8,128]{1,0:T(8,128)S(1)}, u32[]{:S(2)}, u32[]{:S(2)}) %collective-permute-start.1) | collective-permute-done | bytes 4128 | tf_op jit(solution)/shard_map/ppermute | solution.py:575
  9.9 0.9 %collective-permute-done.left_ref = f32[200,128]{1,0:T(8,128)S(1)} collective-permute-done((f32[200,128]{1,0:T(8,128)S(1)}, f32[200,128]{1,0:T(8,128)S(1)}, u32[]{:S(2)}, u32[]{:S(2)}) %collective-permute-start) | collective-permute-done | bytes 102432 | tf_op jit(solution)/shard_map/ppermute | solution.py:574
  10.8 0.2 %pack_rows.1 = (f32[3,128,128]{2,1,0:T(8,128)S(1)}, f32[104,128]{1,0:T(8,128)S(1)}, f32[112,128]{1,0:T(8,128)S(1)}, f32[3,16,128]{2,1,0:T(8,128)S(1)}) custom-call(f32[8,128]{1,0:T(8,128)S(1)} %get-tuple-element.15.counts_ref, f32[32,128]{1,0:T(8,128)S(1)} %get-tuple-element.14.strip_ref, f32[200,128]{1,0:T(8,128)S(1)} %collective-permute-done.left_ref, ...), custom_call_target="tpu_custom_call" | custom-call | flops 3000000000 | bytes 600000 | tf_op jit(solution)/shard_map/pack_rows/pallas_call | solution.py:586
  10.9 0.4 %collective-permute-start.4 = (f32[112,128]{1,0:T(8,128)S(1)}, f32[112,128]{1,0:T(8,128)S(1)}, u32[]{:S(2)}, u32[]{:S(2)}) collective-permute-start(f32[112,128]{1,0:T(8,128)S(1)} %get-tuple-element.21), channel_id=1, source_target_pairs={{0,24},{8,16},{16,8},{24,0},{1,25},{9,17},{17,9},{25,1},{2,26},{10... | collective-permute-start | bytes 172040 | tf_op jit(solution)/shard_map/ppermute | solution.py:612
  11.3 1.3 %collective-permute-start.3 = (f32[104,128]{1,0:T(8,128)S(1)}, f32[104,128]{1,0:T(8,128)S(1)}, u32[]{:S(2)}, u32[]{:S(2)}) collective-permute-start(f32[104,128]{1,0:T(8,128)S(1)} %get-tuple-element.20), channel_id=1, source_target_pairs={{0,8},{8,0},{16,24},{24,16},{1,9},{9,1},{17,25},{25,17},{2,10},{10... | collective-permute-start | bytes 159752 | tf_op jit(solution)/shard_map/ppermute | solution.py:610
  12.6 0.8 %lower_error.1 = (f32[32,128]{1,0:T(8,128)S(1)}, f32[8,128]{1,0:T(8,128)S(1)}) custom-call(s32[1,1,2]{2,1,0:T(1,128)} %pos_ref.1, s32[1,1,2]{2,1,0:T(1,128)} %ext_ref.1, f32[3,128,256]{2,1,0:T(8,128)S(1)} %copy-done, f32[3,128,128]{2,1,0:T(8,128)S(1)} %get-tuple-element.18.rim_ref), custom_call_target="tpu_custom_call" | custom-call | flops 15000000 | bytes 300000 | tf_op jit(solution)/shard_map/lower_error/pallas_call | solution.py:595
  13.5 0.2 collective-permute-done.2.slab_ref
  13.6 0.3 %move_rows.1.rows_ref = f32[3,144,512]{2,1,0:T(8,128)S(1)} custom-call(f32[3,128,256]{2,1,0:T(8,128)S(1)} %copy-done, f32[3,128,128]{2,1,0:T(8,128)S(1)} %get-tuple-element.18.rim_ref, f32[3,64,256]{2,1,0:T(8,128)S(1)} %collective-permute-done.2.slab_ref), custom_call_target="tpu_custom_call" | custom-call | flops 3000000 | bytes 1000000 | tf_op jit(solution)/shard_map/move_rows/pallas_call | solution.py:614
  13.9 0.0 collective-permute-done.3.within_ref
  13.9 0.8 %collective-permute-done.4.across_ref = f32[112,128]{1,0:T(8,128)S(1)} collective-permute-done((f32[112,128]{1,0:T(8,128)S(1)}, f32[112,128]{1,0:T(8,128)S(1)}, u32[]{:S(2)}, u32[]{:S(2)}) %collective-permute-start.4) | collective-permute-done | bytes 57376 | tf_op jit(solution)/shard_map/ppermute | solution.py:612
  14.8 2.7 %finish.1 = (f32[64,128]{1,0:T(8,128)}, f32[3,128,256]{2,1,0:T(8,128)}, f32[3,128,128]{2,1,0:T(8,128)}) custom-call(f32[3,128,256]{2,1,0:T(8,128)S(1)} %copy-done, f32[3,128,128]{2,1,0:T(8,128)S(1)} %get-tuple-element.18.rim_ref, f32[3,64,256]{2,1,0:T(8,128)S(1)} %collective-permute-done.2.slab_ref, f32[3,144,512]{2,1,0:T(8,128)S(1)} %move_rows.1.rows_ref, ...), custom_call_target="tpu_custom_call" | custom-call | tf_op jit(solution)/shard_map/finish/pallas_call | solution.py:622
  (2 shorter events, 0.0 us)
Async XLA Ops:
  0.6 1.0 %copy-start = (f32[3,128,256]{2,1,0:T(8,128)S(1)}, f32[3,128,256]{2,1,0:T(8,128)}, u32[]{:S(2)}) copy-start(f32[3,128,256]{2,1,0:T(8,128)} %state_ref.11) | copy-start | bytes 1179652
  1.8 8.9 %collective-permute-start = (f32[200,128]{1,0:T(8,128)S(1)}, f32[200,128]{1,0:T(8,128)S(1)}, u32[]{:S(2)}, u32[]{:S(2)}) collective-permute-start(f32[200,128]{1,0:T(8,128)S(1)} %get-tuple-element.16), channel_id=1, source_target_pairs={{0,1},{1,2},{2,3},{3,4},{4,5},{5,6},{6,7},{7,0},{8,9},{9,10},{10,1... | collective-permute-start | bytes 307208 | tf_op jit(solution)/shard_map/ppermute | solution.py:574
  5.5 4.4 %collective-permute-start.1 = (f32[8,128]{1,0:T(8,128)S(1)}, f32[8,128]{1,0:T(8,128)S(1)}, u32[]{:S(2)}, u32[]{:S(2)}) collective-permute-start(f32[8,128]{1,0:T(8,128)S(1)} %get-tuple-element.17), channel_id=1, source_target_pairs={{0,7},{1,0},{2,1},{3,2},{4,3},{5,4},{6,5},{7,6},{8,15},{9,8},{10,9... | collective-permute-start | bytes 12296 | tf_op jit(solution)/shard_map/ppermute | solution.py:575
  8.6 5.1 %collective-permute-start.2 = (f32[3,64,256]{2,1,0:T(8,128)S(1)}, f32[3,64,256]{2,1,0:T(8,128)S(1)}, u32[]{:S(2)}, u32[]{:S(2)}) collective-permute-start(f32[3,64,256]{2,1,0:T(8,128)S(1)} %get-tuple-element.19), channel_id=1, source_target_pairs={{0,8},{8,16},{16,24},{24,0},{1,9},{9,17},{17,25},{25,1},{2,10},{10... | collective-permute-start | bytes 589832 | tf_op jit(solution)/shard_map/ppermute | solution.py:576
  10.9 3.8 %collective-permute-start.4 = (f32[112,128]{1,0:T(8,128)S(1)}, f32[112,128]{1,0:T(8,128)S(1)}, u32[]{:S(2)}, u32[]{:S(2)}) collective-permute-start(f32[112,128]{1,0:T(8,128)S(1)} %get-tuple-element.21), channel_id=1, source_target_pairs={{0,24},{8,16},{16,8},{24,0},{1,25},{9,17},{17,9},{25,1},{2,26},{10... | collective-permute-start | bytes 172040 | tf_op jit(solution)/shard_map/ppermute | solution.py:612
  11.3 2.6 %collective-permute-start.3 = (f32[104,128]{1,0:T(8,128)S(1)}, f32[104,128]{1,0:T(8,128)S(1)}, u32[]{:S(2)}, u32[]{:S(2)}) collective-permute-start(f32[104,128]{1,0:T(8,128)S(1)} %get-tuple-element.20), channel_id=1, source_target_pairs={{0,8},{8,0},{16,24},{24,16},{1,9},{9,1},{17,25},{25,17},{2,10},{10... | collective-permute-start | bytes 159752 | tf_op jit(solution)/shard_map/ppermute | solution.py:610

commit v7 on v6

--- a/solution.py
+++ b/solution.py
@@ -242,14 +242,14 @@
     lanes = lane_ids(8)
     packed_up, packed_down = None, None
     for comp in range(3):
-        near_rows[comp, 0:2, :] = slab_ref[comp, SLAB - 2 : SLAB, :]
-        near_rows[comp, 2:6, :] = state_ref[comp, 0:4, :]
-        near_rows[comp, 6:10, :] = state_ref[comp, rows - 4 : rows, :]
-        near_rows[comp, 10:12, :] = below[comp, 0:2, 0:cols]
-        near_rows[comp, 12:16, :] = state_ref[comp, 0:4, :]
-        first, second = near_rows[comp, :, 0:LANES], near_rows[comp, :, LANES : 2 * LANES]
+        near_rows[comp][0:2, :] = slab_ref[comp, SLAB - 2 : SLAB, :]
+        near_rows[comp][2:6, :] = state_ref[comp, 0:4, :]
+        near_rows[comp][6:10, :] = state_ref[comp, rows - 4 : rows, :]
+        near_rows[comp][10:12, :] = below[comp][0:2, 0:cols]
+        near_rows[comp][12:16, :] = state_ref[comp, 0:4, :]
+        first, second = near_rows[comp][:, 0:LANES], near_rows[comp][:, LANES : 2 * LANES]
         for parity in range(2):
-            columns[comp, parity] = every_other(first, second, parity)
+            columns[comp][parity] = every_other(first, second, parity)
 
         def around_corner(body, rim):
             start = jnp.where(lanes < LANES // 2, body[:, 0:LANES], rim)
@@ -257,22 +257,23 @@
             first_six = (lanes >= 12 * comp) & (lanes < 12 * comp + 6)
             return jnp.where(first_six, roll(start, 12 * comp + 2, 1), roll(end, 12 * comp + 10, 1))
 
-        up = around_corner(slab_ref[comp, SLAB - 8 : SLAB, :], above_rim[comp, SLAB - 8 : SLAB, :])
-        down = around_corner(below[comp, :, 0:cols], below[comp, :, right])
+        up = around_corner(slab_ref[comp, SLAB - 8 : SLAB, :], above_rim[comp][SLAB - 8 : SLAB, :])
+        down = around_corner(below[comp][:, 0:cols], below[comp][:, right])
         packed_up = up if comp == 0 else jnp.where(lanes >= 12 * comp, up, packed_up)
         packed_down = down if comp == 0 else jnp.where(lanes >= 12 * comp, down, packed_down)
     corners = jnp.concatenate([packed_down, jnp.ones((LANES - 16, LANES), jnp.float32), packed_up], axis=0).T
     for comp in range(3):
-        corners_ref[comp, 0:12, :] = corners[12 * comp : 12 * comp + 12, :]
-        corners_ref[comp, 12:16, :] = edge_ref[comp, 12:16, :]
+        corners_ref[comp][0:12, :] = corners[12 * comp : 12 * comp + 12, :]
+        corners_ref[comp][12:16, :] = edge_ref[comp, 12:16, :]
     phases = []
     for x in range(2):
         phases.append([])
         for y in range(2):
             cells = []
             for comp, turned in ((0, 0), (1, 2), (2, 1)):
-                by_row = columns[comp, y, pl.ds(x, 8, stride=2), :]
-                own, outer = [ref[turned, pl.ds(x, 8, stride=2), :] for ref in (edge_ref, corners_ref)]
+                by_row = columns[comp][y, pl.ds(x, 8, stride=2), :]
+                own = edge_ref[turned, pl.ds(x, 8, stride=2), :]
+                outer = corners_ref[turned][pl.ds(x, 8, stride=2), :]
                 cells.append(jnp.concatenate([by_row, every_other(own, outer, y)], axis=0))
             phases[-1].append(cells)
     return phases
@@ -419,7 +420,7 @@
 def finish(
     state_ref, rim_ref, slab_ref, rows_ref, within_ref, across_ref, upper_ref, lower_ref, edge_ref, numbers_ref,
     error_out, moved_out, patch_out,
-    wide, window, near_rows, columns, corners, above_rim, below, error, patch, sems,
+    wide, window, near_rows, columns, corners, above_rim, below, patch, error, sems,
 ):
     rows, cols = state_ref.shape[1], state_ref.shape[2]
     right = slice(cols, cols + LANES)
@@ -442,18 +443,18 @@
         inner = turned if comp == 0 else roll(turned, -2 * comp, 1)
         upper = jnp.where(lanes >= LANES // 2, roll(packed, LANES // 2, 1), inner[0:packed_half])
         lower = jnp.where(lanes >= LANES // 2, packed, inner[packed_half:SLAB])
-        above_rim[comp, 0:packed_half, :] = upper
-        above_rim[comp, packed_half:SLAB, :] = lower
+        above_rim[comp][0:packed_half, :] = upper
+        above_rim[comp][packed_half:SLAB, :] = lower
         for t in range(tiles):
             at = slice(8 * (comp * tiles + t), 8 * (comp * tiles + t) + 8)
-            below[comp, :, LANES * t : LANES * (t + 1)] = jnp.where(odd, across_ref[at, :], within_ref[at, :])
+            below[comp][:, LANES * t : LANES * (t + 1)] = jnp.where(odd, across_ref[at, :], within_ref[at, :])
 
     edges = coarse_error(
         edge_phases(state_ref, slab_ref, above_rim, below, edge_ref, near_rows, columns, corners)
     )
     error[...] = put_edges(jnp.concatenate([upper_ref[...], lower_ref[...]], axis=0), edges)
 
-    own_counts, below_counts, numbers = rim_ref[0, 0:8, :], below[0, :, right], numbers_ref[...]
+    own_counts, below_counts, numbers = rim_ref[0, 0:8, :], below[0][:, right], numbers_ref[...]
     cc, rc_left, rc_right, cc_right = [
         scalar(own_counts, 0, k) for k in (OWN_COLS, LEFT_ROWS, RIGHT_ROWS, RIGHT_COLS)
     ]
@@ -466,10 +467,10 @@
     def put(comp, at, body, side, here, right_count):
         tail = body[:, LANES:cols]
         head, outer = column_move(body[:, 0:LANES], tail[:, cols - 2 * LANES :], side, here, right_count)
-        wide[comp, at : at + 8, 0:LANES] = outer
-        wide[comp, at : at + 8, LANES : 2 * LANES] = head
-        wide[comp, at : at + 8, 2 * LANES : LANES + cols] = tail
-        wide[comp, at : at + 8, LANES + cols : 2 * LANES + cols] = outer
+        wide[comp][at : at + 8, 0:LANES] = outer
+        wide[comp][at : at + 8, LANES : 2 * LANES] = head
+        wide[comp][at : at + 8, 2 * LANES : LANES + cols] = tail
+        wide[comp][at : at + 8, LANES + cols : 2 * LANES + cols] = outer
 
     def moved_rim(ref, first, left, right_count, size):
         from_left = slab_rows(ref, first, left, size)
@@ -477,23 +478,24 @@
         return [jnp.where(on_left, a, b) for a, b in zip(from_left, from_right)]
 
     for comp in range(3):
-        sides = moved_rim(above_rim.at[comp], 0, rc_left, rc_right, SLAB)
+        sides = moved_rim(above_rim[comp], 0, rc_left, rc_right, SLAB)
         for k in range(SLAB // 8):
             side = rim_ref[comp, 8 * k : 8 * k + 8, :]
             side = jnp.where(row_ids(8) + 8 * k < jnp.where(on_left, rc_left, rc_right), sides[k], side)
             put(comp, 8 * k + 8, rows_ref[comp, 8 * k + 8 : 8 * k + 16, inside_wide], side, cc, cc_right)
-        wide[comp, SLAB + 8 : rows + 8, :] = rows_ref[comp, SLAB + 8 : rows + 8, :]
-        put(comp, 0, slab_ref[comp, SLAB - 8 : SLAB, :], above_rim[comp, SLAB - 8 : SLAB, :], cc_above, cc_above_right)
+        wide[comp][SLAB + 8 : rows + 8, :] = rows_ref[comp, SLAB + 8 : rows + 8, :]
+        put(comp, 0, slab_ref[comp, SLAB - 8 : SLAB, :], above_rim[comp][SLAB - 8 : SLAB, :], cc_above, cc_above_right)
         (body,) = slab_rows(state_ref.at[comp], rows - SLAB, rc_below, 8)
         (side,) = moved_rim(rim_ref.at[comp], rows - SLAB, rc_below_left, rc_below_right, 8)
-        body = jnp.where(row_ids(8, cols) < rc_below, body, below[comp, :, 0:cols])
+        body = jnp.where(row_ids(8, cols) < rc_below, body, below[comp][:, 0:cols])
         side = jnp.where(
-            row_ids(8) < jnp.where(on_left, rc_below_left, rc_below_right), side, below[comp, :, right]
+            row_ids(8) < jnp.where(on_left, rc_below_left, rc_below_right), side, below[comp][:, right]
         )
         put(comp, rows + 8, body, side, cc_below, cc_below_right)
+    copies.append(pltpu.make_async_copy(error, error_out, sems.at[1]))
     copies += [
-        pltpu.make_async_copy(wide.at[:, 8 : SLAB + 8, inside_wide], moved_out.at[:, 0:SLAB, :], sems.at[1]),
-        pltpu.make_async_copy(error, error_out, sems.at[2]),
+        pltpu.make_async_copy(wide[c].at[8 : SLAB + 8, inside_wide], moved_out.at[c, 0:SLAB, :], sems.at[2 + c])
+        for c in range(3)
     ]
 
     first_lane = pos_col + LANES - 2
@@ -504,28 +506,28 @@
 
         def load(k):
             group = pl.ds(pl.multiple_of(8 * k, 8), 8)
-            near = wide[comp, group, pl.ds(pl.multiple_of(LANES * tile, LANES), LANES)]
-            far = wide[comp, group, pl.ds(pl.multiple_of(LANES * tile + LANES, LANES), LANES)]
+            near = wide[comp][group, pl.ds(pl.multiple_of(LANES * tile, LANES), LANES)]
+            far = wide[comp][group, pl.ds(pl.multiple_of(LANES * tile + LANES, LANES), LANES)]
             return jnp.where(keep, pltpu.roll(near, turn, 1), pltpu.roll(far, turn, 1))
 
         for k, part in enumerate(sliding(load, pos_row + 4, 72)):
-            window[comp, 8 * k : 8 * k + 8, :] = part
+            window[comp][8 * k : 8 * k + 8, :] = part
 
     fine_rows, fine_cols = 2 * ext_row, 2 * ext_col
     size = PATCH_ROWS
     for start in range(0, PATCH, size):
-        cells = [window[c, start : start + size + 8, :] for c in range(3)]
+        cells = [window[c][start : start + size + 8, :] for c in range(3)]
         fine = patch_rows(cells)
         lanes, ids = lane_ids(size), row_ids(size)
         for a in range(2):
             inside = (2 * (ids + start) + a < fine_rows) & (lanes < fine_cols)
             for c in range(3):
-                patch[c, pl.ds(2 * start + a, size, stride=2), :] = jnp.where(inside, fine[a][c], 0.0)
+                patch[c][pl.ds(2 * start + a, size, stride=2), :] = jnp.where(inside, fine[a][c], 0.0)
         part = pl.ds(2 * start, 2 * size)
         for c in range(3):
-            copies.append(pltpu.make_async_copy(patch.at[c, part, :], patch_out.at[c, part, :], sems.at[3 + c]))
+            copies.append(pltpu.make_async_copy(patch[c].at[part, :], patch_out.at[c, part, :], sems.at[5 + c]))
             copies[-1].start()
-    for copy in copies[1:3]:
+    for copy in copies[1:5]:
         copy.start()
     for copy in copies:
         copy.wait()
@@ -625,16 +627,16 @@
         in_specs=[VMEM] * 10,
         out_specs=(ANY,) * 3,
         scratch_shapes=[
-            vmem(3, rows + 16, width + LANES),
-            vmem(3, 72, LANES),
-            vmem(3, 16, cols),
-            vmem(3, 2, 16, LANES),
-            vmem(3, 16, LANES),
-            vmem(3, SLAB, LANES),
-            vmem(3, 8, width),
+            [vmem(rows + 16, width + LANES)] * 3,
+            [vmem(72, LANES)] * 3,
+            [vmem(16, cols)] * 3,
+            [vmem(2, 16, LANES)] * 3,
+            [vmem(16, LANES)] * 3,
+            [vmem(SLAB, LANES)] * 3,
+            [vmem(8, width)] * 3,
+            [vmem(2 * PATCH, 2 * PATCH)] * 3,
             vmem(half, cols // 2),
-            vmem(3, 2 * PATCH, 2 * PATCH),
-            pltpu.SemaphoreType.DMA((6,)),
+            pltpu.SemaphoreType.DMA((8,)),
         ],
         compiler_params=PARAMS,
         name="finish",

time: 17.6 us -> 17.5 us (level)
  no operation moved by 1% of the time
where the time goes in v7:
time: 17.5 us; the launch traced here: 17.4 us
  starting transfers between devices  7.76 us (44%)
  Pallas kernels  4.82 us (28%)
  waiting for transfers between devices  2.46 us (14%)
  between operations  2.04 us (12%)
  local copies, waits for them, and re-layouts  0.3 us (2%)
    ppermute x1, starting transfers between devices, per_device(): from_right = in_vmem(lax.ppermute(to_left, 'col', around('col', -1)))  3.1 us
    ppermute x1, starting transfers between devices, per_device(): from_left = in_vmem(lax.ppermute(to_right, 'col', around('col', 1)))  2.96 us
    pallas_call x1, Pallas kernels, per_device(): pl.pallas_call(finish, out_shape=(f32(half, cols // 2), f32(3, rows, cols...  2.61 us
    ppermute x1, starting transfers between devices, per_device(): lax.ppermute(within, 'row', [(i, i ^ 1) for i in range(devices)])  1.33 us
    ppermute x1, waiting for transfers between devices, per_device(): from_left = in_vmem(lax.ppermute(to_right, 'col', around('col', 1)))  0.87 us
    ppermute x1, waiting for transfers between devices, per_device(): lax.ppermute(across, 'row', [(i, (i + (1 if i % 2 else -1)) % devices) fo...  0.85 us
    pallas_call x1, Pallas kernels, per_device(): pl.pallas_call(lower_error, out_shape=(vmem(half - UPPER, cols // 2), vme...  0.84 us
    pallas_call x1, Pallas kernels, per_device(): pl.pallas_call(upper_error, out_shape=vmem(UPPER, cols // 2), in_specs=[V...  0.73 us
  transfers between devices with their start and end apart: 5, of which 4 were waited for; matrix products, arithmetic and copies ran while one was open for 0% of the time, Pallas kernels for 12%

profile of v7, /device:TPU:0, one launch (start us, length us, event | category | flops | bytes accessed | tf_op | source)
XLA Modules:
  0.0 17.4 jit_solution(15333823277383591154)
XLA Ops:
  0.6 0.0 copy-start
  1.3 0.3 %copy-done = f32[3,128,256]{2,1,0:T(8,128)S(1)} copy-done((f32[3,128,256]{2,1,0:T(8,128)S(1)}, f32[3,128,256]{2,1,0:T(8,128)}, u32[]{:S(2)}) %copy-start) | copy-done | bytes 393240
  1.6 0.2 %pack_cols.1 = (f32[200,128]{1,0:T(8,128)S(1)}, f32[32,128]{1,0:T(8,128)S(1)}, f32[3,64,256]{2,1,0:T(8,128)S(1)}) custom-call(s32[1,1]{1,0:T(1,128)S(6)} %copy.8.row_count, f32[8,128]{1,0:T(8,128)S(1)} %ahead.1.blank_ref, f32[3,128,256]{2,1,0:T(8,128)S(1)} %copy-done), custom_call_target="tpu_custom_call" | custom-call | tf_op jit(solution)/shard_map/pack_cols/pallas_call | solution.py:565
  1.8 3.0 %collective-permute-start = (f32[200,128]{1,0:T(8,128)S(1)}, f32[200,128]{1,0:T(8,128)S(1)}, u32[]{:S(2)}, u32[]{:S(2)}) collective-permute-start(f32[200,128]{1,0:T(8,128)S(1)} %get-tuple-element.16), channel_id=1, source_target_pairs={{0,1},{1,2},{2,3},{3,4},{4,5},{5,6},{6,7},{7,0},{8,9},{9,10},{10,1... | collective-permute-start | bytes 307208 | tf_op jit(solution)/shard_map/ppermute | solution.py:576
  5.5 3.1 %collective-permute-start.1 = (f32[8,128]{1,0:T(8,128)S(1)}, f32[8,128]{1,0:T(8,128)S(1)}, u32[]{:S(2)}, u32[]{:S(2)}) collective-permute-start(f32[8,128]{1,0:T(8,128)S(1)} %get-tuple-element.17), channel_id=1, source_target_pairs={{0,7},{1,0},{2,1},{3,2},{4,3},{5,4},{6,5},{7,6},{8,15},{9,8},{10,9... | collective-permute-start | bytes 12296 | tf_op jit(solution)/shard_map/ppermute | solution.py:577
  8.6 0.0 collective-permute-start.2
  8.6 0.7 %upper_error.1.upper_ref = f32[32,128]{1,0:T(8,128)S(1)} custom-call(f32[3,128,256]{2,1,0:T(8,128)S(1)} %copy-done), custom_call_target="tpu_custom_call" | custom-call | flops 15000000 | bytes 300000 | tf_op jit(solution)/shard_map/upper_error/pallas_call | solution.py:579
  9.3 0.6 %collective-permute-done.1.right_ref = f32[8,128]{1,0:T(8,128)S(1)} collective-permute-done((f32[8,128]{1,0:T(8,128)S(1)}, f32[8,128]{1,0:T(8,128)S(1)}, u32[]{:S(2)}, u32[]{:S(2)}) %collective-permute-start.1) | collective-permute-done | bytes 4128 | tf_op jit(solution)/shard_map/ppermute | solution.py:577
  9.9 0.9 %collective-permute-done.left_ref = f32[200,128]{1,0:T(8,128)S(1)} collective-permute-done((f32[200,128]{1,0:T(8,128)S(1)}, f32[200,128]{1,0:T(8,128)S(1)}, u32[]{:S(2)}, u32[]{:S(2)}) %collective-permute-start) | collective-permute-done | bytes 102432 | tf_op jit(solution)/shard_map/ppermute | solution.py:576
  10.8 0.2 %pack_rows.1 = (f32[3,128,128]{2,1,0:T(8,128)S(1)}, f32[104,128]{1,0:T(8,128)S(1)}, f32[112,128]{1,0:T(8,128)S(1)}, f32[3,16,128]{2,1,0:T(8,128)S(1)}) custom-call(f32[8,128]{1,0:T(8,128)S(1)} %get-tuple-element.15.counts_ref, f32[32,128]{1,0:T(8,128)S(1)} %get-tuple-element.14.strip_ref, f32[200,128]{1,0:T(8,128)S(1)} %collective-permute-done.left_ref, ...), custom_call_target="tpu_custom_call" | custom-call | flops 3000000000 | bytes 600000 | tf_op jit(solution)/shard_map/pack_rows/pallas_call | solution.py:588
  10.9 0.4 %collective-permute-start.4 = (f32[112,128]{1,0:T(8,128)S(1)}, f32[112,128]{1,0:T(8,128)S(1)}, u32[]{:S(2)}, u32[]{:S(2)}) collective-permute-start(f32[112,128]{1,0:T(8,128)S(1)} %get-tuple-element.21), channel_id=1, source_target_pairs={{0,24},{8,16},{16,8},{24,0},{1,25},{9,17},{17,9},{25,1},{2,26},{10... | collective-permute-start | bytes 172040 | tf_op jit(solution)/shard_map/ppermute | solution.py:614
  11.3 1.3 %collective-permute-start.3 = (f32[104,128]{1,0:T(8,128)S(1)}, f32[104,128]{1,0:T(8,128)S(1)}, u32[]{:S(2)}, u32[]{:S(2)}) collective-permute-start(f32[104,128]{1,0:T(8,128)S(1)} %get-tuple-element.20), channel_id=1, source_target_pairs={{0,8},{8,0},{16,24},{24,16},{1,9},{9,1},{17,25},{25,17},{2,10},{10... | collective-permute-start | bytes 159752 | tf_op jit(solution)/shard_map/ppermute | solution.py:612
  12.6 0.8 %lower_error.1 = (f32[32,128]{1,0:T(8,128)S(1)}, f32[8,128]{1,0:T(8,128)S(1)}) custom-call(s32[1,1,2]{2,1,0:T(1,128)} %pos_ref.1, s32[1,1,2]{2,1,0:T(1,128)} %ext_ref.1, f32[3,128,256]{2,1,0:T(8,128)S(1)} %copy-done, f32[3,128,128]{2,1,0:T(8,128)S(1)} %get-tuple-element.18.rim_ref), custom_call_target="tpu_custom_call" | custom-call | flops 15000000 | bytes 300000 | tf_op jit(solution)/shard_map/lower_error/pallas_call | solution.py:597
  13.5 0.2 collective-permute-done.2.slab_ref
  13.6 0.3 %move_rows.1.rows_ref = f32[3,144,512]{2,1,0:T(8,128)S(1)} custom-call(f32[3,128,256]{2,1,0:T(8,128)S(1)} %copy-done, f32[3,128,128]{2,1,0:T(8,128)S(1)} %get-tuple-element.18.rim_ref, f32[3,64,256]{2,1,0:T(8,128)S(1)} %collective-permute-done.2.slab_ref), custom_call_target="tpu_custom_call" | custom-call | flops 3000000 | bytes 1000000 | tf_op jit(solution)/shard_map/move_rows/pallas_call | solution.py:616
  13.9 0.0 collective-permute-done.3.within_ref
  13.9 0.8 %collective-permute-done.4.across_ref = f32[112,128]{1,0:T(8,128)S(1)} collective-permute-done((f32[112,128]{1,0:T(8,128)S(1)}, f32[112,128]{1,0:T(8,128)S(1)}, u32[]{:S(2)}, u32[]{:S(2)}) %collective-permute-start.4) | collective-permute-done | bytes 57376 | tf_op jit(solution)/shard_map/ppermute | solution.py:614
  14.8 2.6 %finish.1 = (f32[64,128]{1,0:T(8,128)}, f32[3,128,256]{2,1,0:T(8,128)}, f32[3,128,128]{2,1,0:T(8,128)}) custom-call(f32[3,128,256]{2,1,0:T(8,128)S(1)} %copy-done, f32[3,128,128]{2,1,0:T(8,128)S(1)} %get-tuple-element.18.rim_ref, f32[3,64,256]{2,1,0:T(8,128)S(1)} %collective-permute-done.2.slab_ref, f32[3,144,512]{2,1,0:T(8,128)S(1)} %move_rows.1.rows_ref, ...), custom_call_target="tpu_custom_call" | custom-call | tf_op jit(solution)/shard_map/finish/pallas_call | solution.py:624
  (2 shorter events, 0.0 us)
Async XLA Ops:
  0.6 1.0 %copy-start = (f32[3,128,256]{2,1,0:T(8,128)S(1)}, f32[3,128,256]{2,1,0:T(8,128)}, u32[]{:S(2)}) copy-start(f32[3,128,256]{2,1,0:T(8,128)} %state_ref.11) | copy-start | bytes 1179652
  1.8 8.9 %collective-permute-start = (f32[200,128]{1,0:T(8,128)S(1)}, f32[200,128]{1,0:T(8,128)S(1)}, u32[]{:S(2)}, u32[]{:S(2)}) collective-permute-start(f32[200,128]{1,0:T(8,128)S(1)} %get-tuple-element.16), channel_id=1, source_target_pairs={{0,1},{1,2},{2,3},{3,4},{4,5},{5,6},{6,7},{7,0},{8,9},{9,10},{10,1... | collective-permute-start | bytes 307208 | tf_op jit(solution)/shard_map/ppermute | solution.py:576
  5.5 4.4 %collective-permute-start.1 = (f32[8,128]{1,0:T(8,128)S(1)}, f32[8,128]{1,0:T(8,128)S(1)}, u32[]{:S(2)}, u32[]{:S(2)}) collective-permute-start(f32[8,128]{1,0:T(8,128)S(1)} %get-tuple-element.17), channel_id=1, source_target_pairs={{0,7},{1,0},{2,1},{3,2},{4,3},{5,4},{6,5},{7,6},{8,15},{9,8},{10,9... | collective-permute-start | bytes 12296 | tf_op jit(solution)/shard_map/ppermute | solution.py:577
  8.6 5.1 %collective-permute-start.2 = (f32[3,64,256]{2,1,0:T(8,128)S(1)}, f32[3,64,256]{2,1,0:T(8,128)S(1)}, u32[]{:S(2)}, u32[]{:S(2)}) collective-permute-start(f32[3,64,256]{2,1,0:T(8,128)S(1)} %get-tuple-element.19), channel_id=1, source_target_pairs={{0,8},{8,16},{16,24},{24,0},{1,9},{9,17},{17,25},{25,1},{2,10},{10... | collective-permute-start | bytes 589832 | tf_op jit(solution)/shard_map/ppermute | solution.py:578
  10.9 3.8 %collective-permute-start.4 = (f32[112,128]{1,0:T(8,128)S(1)}, f32[112,128]{1,0:T(8,128)S(1)}, u32[]{:S(2)}, u32[]{:S(2)}) collective-permute-start(f32[112,128]{1,0:T(8,128)S(1)} %get-tuple-element.21), channel_id=1, source_target_pairs={{0,24},{8,16},{16,8},{24,0},{1,25},{9,17},{17,9},{25,1},{2,26},{10... | collective-permute-start | bytes 172040 | tf_op jit(solution)/shard_map/ppermute | solution.py:614
  11.3 2.6 %collective-permute-start.3 = (f32[104,128]{1,0:T(8,128)S(1)}, f32[104,128]{1,0:T(8,128)S(1)}, u32[]{:S(2)}, u32[]{:S(2)}) collective-permute-start(f32[104,128]{1,0:T(8,128)S(1)} %get-tuple-element.20), channel_id=1, source_target_pairs={{0,8},{8,0},{16,24},{24,16},{1,9},{9,1},{17,25},{25,17},{2,10},{10... | collective-permute-start | bytes 159752 | tf_op jit(solution)/shard_map/ppermute | solution.py:612

commit v8 on v7

--- a/solution.py
+++ b/solution.py
@@ -8,7 +8,6 @@
 SLAB = 64
 PATCH = 64
 LANES = 128
-PATCH_ROWS = 64
 UPPER = 32
 
 RATIO = 0.1
@@ -348,11 +347,10 @@
     ]
 
 
-def patch_rows(cells):
+def patch_rows(cells, size):
     half = doubled_first_step(cells)
     by_row = [paired_change(half[0][b], half[1][b], 0) for b in range(2)]
     by_col = [paired_change(half[a][0], half[a][1], 1) for a in range(2)]
-    size = cells[0].shape[0] - 8
     lanes = lane_ids(size)
     result = []
     for a in range(2):
@@ -363,8 +361,8 @@
         parts = []
         for c in range(3):
             pick = lanes // 2 + 2
-            even = jnp.take_along_axis(fine[0][c][4 : 4 + size], pick, axis=1)
-            odd = jnp.take_along_axis(fine[1][c][4 : 4 + size], pick, axis=1)
+            even = jnp.take_along_axis(fine[0][c][0:size], pick, axis=1)
+            odd = jnp.take_along_axis(fine[1][c][0:size], pick, axis=1)
             parts.append(jnp.where(lanes % 2 == 0, even, odd))
         result.append(parts)
     return result
@@ -505,28 +503,27 @@
     for comp in range(3):
 
         def load(k):
-            group = pl.ds(pl.multiple_of(8 * k, 8), 8)
+            group = pl.ds(pl.multiple_of(8 * jnp.minimum(k, rows // 8 + 1), 8), 8)
             near = wide[comp][group, pl.ds(pl.multiple_of(LANES * tile, LANES), LANES)]
             far = wide[comp][group, pl.ds(pl.multiple_of(LANES * tile + LANES, LANES), LANES)]
             return jnp.where(keep, pltpu.roll(near, turn, 1), pltpu.roll(far, turn, 1))
 
-        for k, part in enumerate(sliding(load, pos_row + 4, 72)):
+        parts = sliding(load, pos_row + 8, PATCH + 8)
+        (above,) = sliding(load, pos_row, 8)
+        parts[-1] = jnp.where(row_ids(8) < 4, parts[-1], above)
+        for k, part in enumerate(parts):
             window[comp][8 * k : 8 * k + 8, :] = part
 
     fine_rows, fine_cols = 2 * ext_row, 2 * ext_col
-    size = PATCH_ROWS
-    for start in range(0, PATCH, size):
-        cells = [window[c][start : start + size + 8, :] for c in range(3)]
-        fine = patch_rows(cells)
-        lanes, ids = lane_ids(size), row_ids(size)
-        for a in range(2):
-            inside = (2 * (ids + start) + a < fine_rows) & (lanes < fine_cols)
-            for c in range(3):
-                patch[c][pl.ds(2 * start + a, size, stride=2), :] = jnp.where(inside, fine[a][c], 0.0)
-        part = pl.ds(2 * start, 2 * size)
+    fine = patch_rows([window[c][...] for c in range(3)], PATCH)
+    lanes, ids = lane_ids(PATCH), row_ids(PATCH)
+    for a in range(2):
+        inside = (2 * ids + a < fine_rows) & (lanes < fine_cols)
         for c in range(3):
-            copies.append(pltpu.make_async_copy(patch[c].at[part, :], patch_out.at[c, part, :], sems.at[5 + c]))
-            copies[-1].start()
+            patch[c][pl.ds(a, PATCH, stride=2), :] = jnp.where(inside, fine[a][c], 0.0)
+    for c in range(3):
+        copies.append(pltpu.make_async_copy(patch[c], patch_out.at[c], sems.at[5 + c]))
+        copies[-1].start()
     for copy in copies[1:5]:
         copy.start()
     for copy in copies:
@@ -628,7 +625,7 @@
         out_specs=(ANY,) * 3,
         scratch_shapes=[
             [vmem(rows + 16, width + LANES)] * 3,
-            [vmem(72, LANES)] * 3,
+            [vmem(PATCH + 8, LANES)] * 3,
             [vmem(16, cols)] * 3,
             [vmem(2, 16, LANES)] * 3,
             [vmem(16, LANES)] * 3,

time: 17.5 us -> 17.5 us (level)
  no operation moved by 1% of the time
where the time goes in v8:
time: 17.5 us; the launch traced here: 17.3 us
  starting transfers between devices  7.76 us (44%)
  Pallas kernels  4.73 us (27%)
  waiting for transfers between devices  2.46 us (14%)
  between operations  2.04 us (12%)
  local copies, waits for them, and re-layouts  0.3 us (2%)
    ppermute x1, starting transfers between devices, per_device(): from_right = in_vmem(lax.ppermute(to_left, 'col', around('col', -1)))  3.1 us
    ppermute x1, starting transfers between devices, per_device(): from_left = in_vmem(lax.ppermute(to_right, 'col', around('col', 1)))  2.96 us
    pallas_call x1, Pallas kernels, per_device(): pl.pallas_call(finish, out_shape=(f32(half, cols // 2), f32(3, rows, cols...  2.52 us
    ppermute x1, starting transfers between devices, per_device(): lax.ppermute(within, 'row', [(i, i ^ 1) for i in range(devices)])  1.33 us
    ppermute x1, waiting for transfers between devices, per_device(): from_left = in_vmem(lax.ppermute(to_right, 'col', around('col', 1)))  0.87 us
    ppermute x1, waiting for transfers between devices, per_device(): lax.ppermute(across, 'row', [(i, (i + (1 if i % 2 else -1)) % devices) fo...  0.85 us
    pallas_call x1, Pallas kernels, per_device(): pl.pallas_call(lower_error, out_shape=(vmem(half - UPPER, cols // 2), vme...  0.84 us
    pallas_call x1, Pallas kernels, per_device(): pl.pallas_call(upper_error, out_shape=vmem(UPPER, cols // 2), in_specs=[V...  0.73 us
  transfers between devices with their start and end apart: 5, of which 4 were waited for; matrix products, arithmetic and copies ran while one was open for 0% of the time, Pallas kernels for 12%

profile of v8, /device:TPU:0, one launch (start us, length us, event | category | flops | bytes accessed | tf_op | source)
XLA Modules:
  0.0 17.3 jit_solution(14184265226952313375)
XLA Ops:
  0.6 0.0 copy-start
  1.3 0.3 %copy-done = f32[3,128,256]{2,1,0:T(8,128)S(1)} copy-done((f32[3,128,256]{2,1,0:T(8,128)S(1)}, f32[3,128,256]{2,1,0:T(8,128)}, u32[]{:S(2)}) %copy-start) | copy-done | bytes 393240
  1.6 0.2 %pack_cols.1 = (f32[200,128]{1,0:T(8,128)S(1)}, f32[32,128]{1,0:T(8,128)S(1)}, f32[3,64,256]{2,1,0:T(8,128)S(1)}) custom-call(s32[1,1]{1,0:T(1,128)S(6)} %copy.8.row_count, f32[8,128]{1,0:T(8,128)S(1)} %ahead.1.blank_ref, f32[3,128,256]{2,1,0:T(8,128)S(1)} %copy-done), custom_call_target="tpu_custom_call" | custom-call | tf_op jit(solution)/shard_map/pack_cols/pallas_call | solution.py:562
  1.8 3.0 %collective-permute-start = (f32[200,128]{1,0:T(8,128)S(1)}, f32[200,128]{1,0:T(8,128)S(1)}, u32[]{:S(2)}, u32[]{:S(2)}) collective-permute-start(f32[200,128]{1,0:T(8,128)S(1)} %get-tuple-element.16), channel_id=1, source_target_pairs={{0,1},{1,2},{2,3},{3,4},{4,5},{5,6},{6,7},{7,0},{8,9},{9,10},{10,1... | collective-permute-start | bytes 307208 | tf_op jit(solution)/shard_map/ppermute | solution.py:573
  5.5 3.1 %collective-permute-start.1 = (f32[8,128]{1,0:T(8,128)S(1)}, f32[8,128]{1,0:T(8,128)S(1)}, u32[]{:S(2)}, u32[]{:S(2)}) collective-permute-start(f32[8,128]{1,0:T(8,128)S(1)} %get-tuple-element.17), channel_id=1, source_target_pairs={{0,7},{1,0},{2,1},{3,2},{4,3},{5,4},{6,5},{7,6},{8,15},{9,8},{10,9... | collective-permute-start | bytes 12296 | tf_op jit(solution)/shard_map/ppermute | solution.py:574
  8.6 0.0 collective-permute-start.2
  8.6 0.7 %upper_error.1.upper_ref = f32[32,128]{1,0:T(8,128)S(1)} custom-call(f32[3,128,256]{2,1,0:T(8,128)S(1)} %copy-done), custom_call_target="tpu_custom_call" | custom-call | flops 15000000 | bytes 300000 | tf_op jit(solution)/shard_map/upper_error/pallas_call | solution.py:576
  9.3 0.6 %collective-permute-done.1.right_ref = f32[8,128]{1,0:T(8,128)S(1)} collective-permute-done((f32[8,128]{1,0:T(8,128)S(1)}, f32[8,128]{1,0:T(8,128)S(1)}, u32[]{:S(2)}, u32[]{:S(2)}) %collective-permute-start.1) | collective-permute-done | bytes 4128 | tf_op jit(solution)/shard_map/ppermute | solution.py:574
  9.9 0.9 %collective-permute-done.left_ref = f32[200,128]{1,0:T(8,128)S(1)} collective-permute-done((f32[200,128]{1,0:T(8,128)S(1)}, f32[200,128]{1,0:T(8,128)S(1)}, u32[]{:S(2)}, u32[]{:S(2)}) %collective-permute-start) | collective-permute-done | bytes 102432 | tf_op jit(solution)/shard_map/ppermute | solution.py:573
  10.8 0.2 %pack_rows.1 = (f32[3,128,128]{2,1,0:T(8,128)S(1)}, f32[104,128]{1,0:T(8,128)S(1)}, f32[112,128]{1,0:T(8,128)S(1)}, f32[3,16,128]{2,1,0:T(8,128)S(1)}) custom-call(f32[8,128]{1,0:T(8,128)S(1)} %get-tuple-element.15.counts_ref, f32[32,128]{1,0:T(8,128)S(1)} %get-tuple-element.14.strip_ref, f32[200,128]{1,0:T(8,128)S(1)} %collective-permute-done.left_ref, ...), custom_call_target="tpu_custom_call" | custom-call | flops 3000000000 | bytes 600000 | tf_op jit(solution)/shard_map/pack_rows/pallas_call | solution.py:585
  10.9 0.4 %collective-permute-start.4 = (f32[112,128]{1,0:T(8,128)S(1)}, f32[112,128]{1,0:T(8,128)S(1)}, u32[]{:S(2)}, u32[]{:S(2)}) collective-permute-start(f32[112,128]{1,0:T(8,128)S(1)} %get-tuple-element.21), channel_id=1, source_target_pairs={{0,24},{8,16},{16,8},{24,0},{1,25},{9,17},{17,9},{25,1},{2,26},{10... | collective-permute-start | bytes 172040 | tf_op jit(solution)/shard_map/ppermute | solution.py:611
  11.3 1.3 %collective-permute-start.3 = (f32[104,128]{1,0:T(8,128)S(1)}, f32[104,128]{1,0:T(8,128)S(1)}, u32[]{:S(2)}, u32[]{:S(2)}) collective-permute-start(f32[104,128]{1,0:T(8,128)S(1)} %get-tuple-element.20), channel_id=1, source_target_pairs={{0,8},{8,0},{16,24},{24,16},{1,9},{9,1},{17,25},{25,17},{2,10},{10... | collective-permute-start | bytes 159752 | tf_op jit(solution)/shard_map/ppermute | solution.py:609
  12.6 0.8 %lower_error.1 = (f32[32,128]{1,0:T(8,128)S(1)}, f32[8,128]{1,0:T(8,128)S(1)}) custom-call(s32[1,1,2]{2,1,0:T(1,128)} %pos_ref.1, s32[1,1,2]{2,1,0:T(1,128)} %ext_ref.1, f32[3,128,256]{2,1,0:T(8,128)S(1)} %copy-done, f32[3,128,128]{2,1,0:T(8,128)S(1)} %get-tuple-element.18.rim_ref), custom_call_target="tpu_custom_call" | custom-call | flops 15000000 | bytes 300000 | tf_op jit(solution)/shard_map/lower_error/pallas_call | solution.py:594
  13.5 0.2 collective-permute-done.2.slab_ref
  13.6 0.3 %move_rows.1.rows_ref = f32[3,144,512]{2,1,0:T(8,128)S(1)} custom-call(f32[3,128,256]{2,1,0:T(8,128)S(1)} %copy-done, f32[3,128,128]{2,1,0:T(8,128)S(1)} %get-tuple-element.18.rim_ref, f32[3,64,256]{2,1,0:T(8,128)S(1)} %collective-permute-done.2.slab_ref), custom_call_target="tpu_custom_call" | custom-call | flops 3000000 | bytes 1000000 | tf_op jit(solution)/shard_map/move_rows/pallas_call | solution.py:613
  13.9 0.0 collective-permute-done.3.within_ref
  13.9 0.8 %collective-permute-done.4.across_ref = f32[112,128]{1,0:T(8,128)S(1)} collective-permute-done((f32[112,128]{1,0:T(8,128)S(1)}, f32[112,128]{1,0:T(8,128)S(1)}, u32[]{:S(2)}, u32[]{:S(2)}) %collective-permute-start.4) | collective-permute-done | bytes 57376 | tf_op jit(solution)/shard_map/ppermute | solution.py:611
  14.8 2.5 %finish.1 = (f32[64,128]{1,0:T(8,128)}, f32[3,128,256]{2,1,0:T(8,128)}, f32[3,128,128]{2,1,0:T(8,128)}) custom-call(f32[3,128,256]{2,1,0:T(8,128)S(1)} %copy-done, f32[3,128,128]{2,1,0:T(8,128)S(1)} %get-tuple-element.18.rim_ref, f32[3,64,256]{2,1,0:T(8,128)S(1)} %collective-permute-done.2.slab_ref, f32[3,144,512]{2,1,0:T(8,128)S(1)} %move_rows.1.rows_ref, ...), custom_call_target="tpu_custom_call" | custom-call | tf_op jit(solution)/shard_map/finish/pallas_call | solution.py:621
  (2 shorter events, 0.0 us)
Async XLA Ops:
  0.6 1.0 %copy-start = (f32[3,128,256]{2,1,0:T(8,128)S(1)}, f32[3,128,256]{2,1,0:T(8,128)}, u32[]{:S(2)}) copy-start(f32[3,128,256]{2,1,0:T(8,128)} %state_ref.11) | copy-start | bytes 1179652
  1.8 8.9 %collective-permute-start = (f32[200,128]{1,0:T(8,128)S(1)}, f32[200,128]{1,0:T(8,128)S(1)}, u32[]{:S(2)}, u32[]{:S(2)}) collective-permute-start(f32[200,128]{1,0:T(8,128)S(1)} %get-tuple-element.16), channel_id=1, source_target_pairs={{0,1},{1,2},{2,3},{3,4},{4,5},{5,6},{6,7},{7,0},{8,9},{9,10},{10,1... | collective-permute-start | bytes 307208 | tf_op jit(solution)/shard_map/ppermute | solution.py:573
  5.5 4.4 %collective-permute-start.1 = (f32[8,128]{1,0:T(8,128)S(1)}, f32[8,128]{1,0:T(8,128)S(1)}, u32[]{:S(2)}, u32[]{:S(2)}) collective-permute-start(f32[8,128]{1,0:T(8,128)S(1)} %get-tuple-element.17), channel_id=1, source_target_pairs={{0,7},{1,0},{2,1},{3,2},{4,3},{5,4},{6,5},{7,6},{8,15},{9,8},{10,9... | collective-permute-start | bytes 12296 | tf_op jit(solution)/shard_map/ppermute | solution.py:574
  8.6 5.1 %collective-permute-start.2 = (f32[3,64,256]{2,1,0:T(8,128)S(1)}, f32[3,64,256]{2,1,0:T(8,128)S(1)}, u32[]{:S(2)}, u32[]{:S(2)}) collective-permute-start(f32[3,64,256]{2,1,0:T(8,128)S(1)} %get-tuple-element.19), channel_id=1, source_target_pairs={{0,8},{8,16},{16,24},{24,0},{1,9},{9,17},{17,25},{25,1},{2,10},{10... | collective-permute-start | bytes 589832 | tf_op jit(solution)/shard_map/ppermute | solution.py:575
  10.9 3.8 %collective-permute-start.4 = (f32[112,128]{1,0:T(8,128)S(1)}, f32[112,128]{1,0:T(8,128)S(1)}, u32[]{:S(2)}, u32[]{:S(2)}) collective-permute-start(f32[112,128]{1,0:T(8,128)S(1)} %get-tuple-element.21), channel_id=1, source_target_pairs={{0,24},{8,16},{16,8},{24,0},{1,25},{9,17},{17,9},{25,1},{2,26},{10... | collective-permute-start | bytes 172040 | tf_op jit(solution)/shard_map/ppermute | solution.py:611
  11.3 2.6 %collective-permute-start.3 = (f32[104,128]{1,0:T(8,128)S(1)}, f32[104,128]{1,0:T(8,128)S(1)}, u32[]{:S(2)}, u32[]{:S(2)}) collective-permute-start(f32[104,128]{1,0:T(8,128)S(1)} %get-tuple-element.20), channel_id=1, source_target_pairs={{0,8},{8,0},{16,24},{24,16},{1,9},{9,1},{17,25},{25,17},{2,10},{10... | collective-permute-start | bytes 159752 | tf_op jit(solution)/shard_map/ppermute | solution.py:609

commit v9 on v8

--- a/solution.py
+++ b/solution.py
@@ -193,13 +193,14 @@
         edge_ref[comp, 6:10, :] = strip_ref[8 * comp : 8 * comp + 4, :]
         edge_ref[comp, 10:12, :] = right_ref[2 * comp : 2 * comp + 2, :]
         edge_ref[comp, 12:16, :] = strip_ref[8 * comp + 4 : 8 * comp + 8, :]
-    downs.append(jnp.where(row_ids(8) == 6, cc, right_ref[...]))
+    last_row = jnp.where(lane_ids(8) < LANES // 2, cc, right_ref[7:8, :])
+    downs.append(jnp.where(row_ids(8) >= 6, last_row, right_ref[...]))
     down = jnp.concatenate(downs, axis=0)
     up = jnp.concatenate(ups, axis=0)
     size = up.shape[0]
     put(0, down[0:size], up)
-    put(size, down[size:DOWN_ROWS], down[size:DOWN_ROWS])
-    across_ref[DOWN_ROWS : DOWN_ROWS + 8, :] = jnp.zeros((8, LANES), jnp.float32)
+    across_ref[size:DOWN_ROWS, :] = down[size:DOWN_ROWS]
+    within_ref[size : DOWN_ROWS - 1, :] = down[size : DOWN_ROWS - 1]
 
 
 def inner_error(state_ref, first, size, columns):
@@ -431,8 +432,8 @@
 
     odd = is_odd()
     packed_half = SLAB // 2
-    beside = jnp.where(odd, within_ref[DOWN_ROWS - 8 : DOWN_ROWS, :], across_ref[DOWN_ROWS - 8 : DOWN_ROWS, :])
-    turned = jnp.concatenate([beside, jnp.zeros((LANES - 8, LANES), jnp.float32)], axis=0).T[rows - SLAB : rows]
+    beside = jnp.where(odd, within_ref[DOWN_ROWS - 8 : DOWN_ROWS - 1, :], across_ref[DOWN_ROWS - 8 : DOWN_ROWS - 1, :])
+    turned = jnp.concatenate([beside, jnp.zeros((LANES - 7, LANES), jnp.float32)], axis=0).T[rows - SLAB : rows]
     lanes = lane_ids(packed_half)
     tiles = cols // LANES + 1
     for comp in range(3):
@@ -456,7 +457,7 @@
     cc, rc_left, rc_right, cc_right = [
         scalar(own_counts, 0, k) for k in (OWN_COLS, LEFT_ROWS, RIGHT_ROWS, RIGHT_COLS)
     ]
-    cc_above, cc_above_right = [scalar(beside, k, 0) for k in (6, 7)]
+    cc_above, cc_above_right = [scalar(beside, 6, k) for k in (0, LANES - 1)]
     rc_below, cc_below, rc_below_left, rc_below_right, cc_below_right = [
         scalar(below_counts, 0, k) for k in (OWN_ROWS, OWN_COLS, LEFT_ROWS, RIGHT_ROWS, RIGHT_COLS)
     ]
@@ -584,7 +585,7 @@
     )(here))
     rim, within, across, edge = pl.pallas_call(
         pack_rows,
-        out_shape=(vmem(3, rows, LANES), vmem(DOWN_ROWS, LANES), vmem(DOWN_ROWS + 8, LANES), vmem(3, 16, LANES)),
+        out_shape=(vmem(3, rows, LANES), vmem(DOWN_ROWS - 1, LANES), vmem(DOWN_ROWS, LANES), vmem(3, 16, LANES)),
         in_specs=[VMEM] * 6,
         out_specs=(VMEM,) * 4,
         cost_estimate=pl.CostEstimate(flops=3_000_000_000, bytes_accessed=600_000, transcendentals=0),

time: 17.5 us -> 17.4 us (level)
  no operation moved by 1% of the time
where the time goes in v9:
time: 17.4 us; the launch traced here: 17.3 us
  starting transfers between devices  7.76 us (45%)
  Pallas kernels  4.78 us (27%)
  waiting for transfers between devices  2.38 us (14%)
  between operations  2.04 us (12%)
  local copies, waits for them, and re-layouts  0.3 us (2%)
    ppermute x1, starting transfers between devices, per_device(): from_right = in_vmem(lax.ppermute(to_left, 'col', around('col', -1)))  3.1 us
    ppermute x1, starting transfers between devices, per_device(): from_left = in_vmem(lax.ppermute(to_right, 'col', around('col', 1)))  2.96 us
    pallas_call x1, Pallas kernels, per_device(): pl.pallas_call(finish, out_shape=(f32(half, cols // 2), f32(3, rows, cols...  2.57 us
    ppermute x1, starting transfers between devices, per_device(): lax.ppermute(within, 'row', [(i, i ^ 1) for i in range(devices)])  1.33 us
    ppermute x1, waiting for transfers between devices, per_device(): from_left = in_vmem(lax.ppermute(to_right, 'col', around('col', 1)))  0.87 us
    pallas_call x1, Pallas kernels, per_device(): pl.pallas_call(lower_error, out_shape=(vmem(half - UPPER, cols // 2), vme...  0.84 us
    ppermute x1, waiting for transfers between devices, per_device(): lax.ppermute(across, 'row', [(i, (i + (1 if i % 2 else -1)) % devices) fo...  0.76 us
    pallas_call x1, Pallas kernels, per_device(): pl.pallas_call(upper_error, out_shape=vmem(UPPER, cols // 2), in_specs=[V...  0.73 us
  transfers between devices with their start and end apart: 5, of which 4 were waited for; matrix products, arithmetic and copies ran while one was open for 0% of the time, Pallas kernels for 12%

profile of v9, /device:TPU:0, one launch (start us, length us, event | category | flops | bytes accessed | tf_op | source)
XLA Modules:
  0.0 17.3 jit_solution(6095389715642301005)
XLA Ops:
  0.6 0.0 copy-start
  1.3 0.3 %copy-done = f32[3,128,256]{2,1,0:T(8,128)S(1)} copy-done((f32[3,128,256]{2,1,0:T(8,128)S(1)}, f32[3,128,256]{2,1,0:T(8,128)}, u32[]{:S(2)}) %copy-start) | copy-done | bytes 393240
  1.6 0.2 %pack_cols.1 = (f32[200,128]{1,0:T(8,128)S(1)}, f32[32,128]{1,0:T(8,128)S(1)}, f32[3,64,256]{2,1,0:T(8,128)S(1)}) custom-call(s32[1,1]{1,0:T(1,128)S(6)} %copy.8.row_count, f32[8,128]{1,0:T(8,128)S(1)} %ahead.1.blank_ref, f32[3,128,256]{2,1,0:T(8,128)S(1)} %copy-done), custom_call_target="tpu_custom_call" | custom-call | tf_op jit(solution)/shard_map/pack_cols/pallas_call | solution.py:563
  1.8 3.0 %collective-permute-start = (f32[200,128]{1,0:T(8,128)S(1)}, f32[200,128]{1,0:T(8,128)S(1)}, u32[]{:S(2)}, u32[]{:S(2)}) collective-permute-start(f32[200,128]{1,0:T(8,128)S(1)} %get-tuple-element.16), channel_id=1, source_target_pairs={{0,1},{1,2},{2,3},{3,4},{4,5},{5,6},{6,7},{7,0},{8,9},{9,10},{10,1... | collective-permute-start | bytes 307208 | tf_op jit(solution)/shard_map/ppermute | solution.py:574
  5.5 3.1 %collective-permute-start.1 = (f32[8,128]{1,0:T(8,128)S(1)}, f32[8,128]{1,0:T(8,128)S(1)}, u32[]{:S(2)}, u32[]{:S(2)}) collective-permute-start(f32[8,128]{1,0:T(8,128)S(1)} %get-tuple-element.17), channel_id=1, source_target_pairs={{0,7},{1,0},{2,1},{3,2},{4,3},{5,4},{6,5},{7,6},{8,15},{9,8},{10,9... | collective-permute-start | bytes 12296 | tf_op jit(solution)/shard_map/ppermute | solution.py:575
  8.6 0.0 collective-permute-start.2
  8.6 0.7 %upper_error.1.upper_ref = f32[32,128]{1,0:T(8,128)S(1)} custom-call(f32[3,128,256]{2,1,0:T(8,128)S(1)} %copy-done), custom_call_target="tpu_custom_call" | custom-call | flops 15000000 | bytes 300000 | tf_op jit(solution)/shard_map/upper_error/pallas_call | solution.py:577
  9.3 0.6 %collective-permute-done.1.right_ref = f32[8,128]{1,0:T(8,128)S(1)} collective-permute-done((f32[8,128]{1,0:T(8,128)S(1)}, f32[8,128]{1,0:T(8,128)S(1)}, u32[]{:S(2)}, u32[]{:S(2)}) %collective-permute-start.1) | collective-permute-done | bytes 4128 | tf_op jit(solution)/shard_map/ppermute | solution.py:575
  9.9 0.9 %collective-permute-done.left_ref = f32[200,128]{1,0:T(8,128)S(1)} collective-permute-done((f32[200,128]{1,0:T(8,128)S(1)}, f32[200,128]{1,0:T(8,128)S(1)}, u32[]{:S(2)}, u32[]{:S(2)}) %collective-permute-start) | collective-permute-done | bytes 102432 | tf_op jit(solution)/shard_map/ppermute | solution.py:574
  10.8 0.2 %pack_rows.1 = (f32[3,128,128]{2,1,0:T(8,128)S(1)}, f32[103,128]{1,0:T(8,128)S(1)}, f32[104,128]{1,0:T(8,128)S(1)}, f32[3,16,128]{2,1,0:T(8,128)S(1)}) custom-call(f32[8,128]{1,0:T(8,128)S(1)} %get-tuple-element.15.counts_ref, f32[32,128]{1,0:T(8,128)S(1)} %get-tuple-element.14.strip_ref, f32[200,128]{1,0:T(8,128)S(1)} %collective-permute-done.left_ref, ...), custom_call_target="tpu_custom_call" | custom-call | flops 3000000000 | bytes 600000 | tf_op jit(solution)/shard_map/pack_rows/pallas_call | solution.py:586
  10.9 0.4 %collective-permute-start.4 = (f32[104,128]{1,0:T(8,128)S(1)}, f32[104,128]{1,0:T(8,128)S(1)}, u32[]{:S(2)}, u32[]{:S(2)}) collective-permute-start(f32[104,128]{1,0:T(8,128)S(1)} %get-tuple-element.21), channel_id=1, source_target_pairs={{0,24},{8,16},{16,8},{24,0},{1,25},{9,17},{17,9},{25,1},{2,26},{10... | collective-permute-start | bytes 159752 | tf_op jit(solution)/shard_map/ppermute | solution.py:612
  11.3 1.3 %collective-permute-start.3 = (f32[103,128]{1,0:T(8,128)S(1)}, f32[103,128]{1,0:T(8,128)S(1)}, u32[]{:S(2)}, u32[]{:S(2)}) collective-permute-start(f32[103,128]{1,0:T(8,128)S(1)} %get-tuple-element.20), channel_id=1, source_target_pairs={{0,8},{8,0},{16,24},{24,16},{1,9},{9,1},{17,25},{25,17},{2,10},{10... | collective-permute-start | bytes 158216 | tf_op jit(solution)/shard_map/ppermute | solution.py:610
  12.6 0.8 %lower_error.1 = (f32[32,128]{1,0:T(8,128)S(1)}, f32[8,128]{1,0:T(8,128)S(1)}) custom-call(s32[1,1,2]{2,1,0:T(1,128)} %pos_ref.1, s32[1,1,2]{2,1,0:T(1,128)} %ext_ref.1, f32[3,128,256]{2,1,0:T(8,128)S(1)} %copy-done, f32[3,128,128]{2,1,0:T(8,128)S(1)} %get-tuple-element.18.rim_ref), custom_call_target="tpu_custom_call" | custom-call | flops 15000000 | bytes 300000 | tf_op jit(solution)/shard_map/lower_error/pallas_call | solution.py:595
  13.5 0.2 collective-permute-done.2.slab_ref
  13.6 0.3 %move_rows.1.rows_ref = f32[3,144,512]{2,1,0:T(8,128)S(1)} custom-call(f32[3,128,256]{2,1,0:T(8,128)S(1)} %copy-done, f32[3,128,128]{2,1,0:T(8,128)S(1)} %get-tuple-element.18.rim_ref, f32[3,64,256]{2,1,0:T(8,128)S(1)} %collective-permute-done.2.slab_ref), custom_call_target="tpu_custom_call" | custom-call | flops 3000000 | bytes 1000000 | tf_op jit(solution)/shard_map/move_rows/pallas_call | solution.py:614
  13.9 0.0 collective-permute-done.3.within_ref
  13.9 0.8 %collective-permute-done.4.across_ref = f32[104,128]{1,0:T(8,128)S(1)} collective-permute-done((f32[104,128]{1,0:T(8,128)S(1)}, f32[104,128]{1,0:T(8,128)S(1)}, u32[]{:S(2)}, u32[]{:S(2)}) %collective-permute-start.4) | collective-permute-done | bytes 53280 | tf_op jit(solution)/shard_map/ppermute | solution.py:612
  14.7 2.6 %finish.1 = (f32[64,128]{1,0:T(8,128)}, f32[3,128,256]{2,1,0:T(8,128)}, f32[3,128,128]{2,1,0:T(8,128)}) custom-call(f32[3,128,256]{2,1,0:T(8,128)S(1)} %copy-done, f32[3,128,128]{2,1,0:T(8,128)S(1)} %get-tuple-element.18.rim_ref, f32[3,64,256]{2,1,0:T(8,128)S(1)} %collective-permute-done.2.slab_ref, f32[3,144,512]{2,1,0:T(8,128)S(1)} %move_rows.1.rows_ref, ...), custom_call_target="tpu_custom_call" | custom-call | tf_op jit(solution)/shard_map/finish/pallas_call | solution.py:622
  (2 shorter events, 0.0 us)
Async XLA Ops:
  0.6 1.0 %copy-start = (f32[3,128,256]{2,1,0:T(8,128)S(1)}, f32[3,128,256]{2,1,0:T(8,128)}, u32[]{:S(2)}) copy-start(f32[3,128,256]{2,1,0:T(8,128)} %state_ref.11) | copy-start | bytes 1179652
  1.8 8.9 %collective-permute-start = (f32[200,128]{1,0:T(8,128)S(1)}, f32[200,128]{1,0:T(8,128)S(1)}, u32[]{:S(2)}, u32[]{:S(2)}) collective-permute-start(f32[200,128]{1,0:T(8,128)S(1)} %get-tuple-element.16), channel_id=1, source_target_pairs={{0,1},{1,2},{2,3},{3,4},{4,5},{5,6},{6,7},{7,0},{8,9},{9,10},{10,1... | collective-permute-start | bytes 307208 | tf_op jit(solution)/shard_map/ppermute | solution.py:574
  5.5 4.4 %collective-permute-start.1 = (f32[8,128]{1,0:T(8,128)S(1)}, f32[8,128]{1,0:T(8,128)S(1)}, u32[]{:S(2)}, u32[]{:S(2)}) collective-permute-start(f32[8,128]{1,0:T(8,128)S(1)} %get-tuple-element.17), channel_id=1, source_target_pairs={{0,7},{1,0},{2,1},{3,2},{4,3},{5,4},{6,5},{7,6},{8,15},{9,8},{10,9... | collective-permute-start | bytes 12296 | tf_op jit(solution)/shard_map/ppermute | solution.py:575
  8.6 5.1 %collective-permute-start.2 = (f32[3,64,256]{2,1,0:T(8,128)S(1)}, f32[3,64,256]{2,1,0:T(8,128)S(1)}, u32[]{:S(2)}, u32[]{:S(2)}) collective-permute-start(f32[3,64,256]{2,1,0:T(8,128)S(1)} %get-tuple-element.19), channel_id=1, source_target_pairs={{0,8},{8,16},{16,24},{24,0},{1,9},{9,17},{17,25},{25,1},{2,10},{10... | collective-permute-start | bytes 589832 | tf_op jit(solution)/shard_map/ppermute | solution.py:576
  10.9 3.7 %collective-permute-start.4 = (f32[104,128]{1,0:T(8,128)S(1)}, f32[104,128]{1,0:T(8,128)S(1)}, u32[]{:S(2)}, u32[]{:S(2)}) collective-permute-start(f32[104,128]{1,0:T(8,128)S(1)} %get-tuple-element.21), channel_id=1, source_target_pairs={{0,24},{8,16},{16,8},{24,0},{1,25},{9,17},{17,9},{25,1},{2,26},{10... | collective-permute-start | bytes 159752 | tf_op jit(solution)/shard_map/ppermute | solution.py:612
  11.3 2.6 %collective-permute-start.3 = (f32[103,128]{1,0:T(8,128)S(1)}, f32[103,128]{1,0:T(8,128)S(1)}, u32[]{:S(2)}, u32[]{:S(2)}) collective-permute-start(f32[103,128]{1,0:T(8,128)S(1)} %get-tuple-element.20), channel_id=1, source_target_pairs={{0,8},{8,0},{16,24},{24,16},{1,9},{9,1},{17,25},{25,17},{2,10},{10... | collective-permute-start | bytes 158216 | tf_op jit(solution)/shard_map/ppermute | solution.py:610

commit v10 on v9

--- a/solution.py
+++ b/solution.py
@@ -419,7 +419,7 @@
 def finish(
     state_ref, rim_ref, slab_ref, rows_ref, within_ref, across_ref, upper_ref, lower_ref, edge_ref, numbers_ref,
     error_out, moved_out, patch_out,
-    wide, window, near_rows, columns, corners, above_rim, below, patch, error, sems,
+    wide, window, near_rows, columns, corners, above_rim, below, patch, error, aside, sems,
 ):
     rows, cols = state_ref.shape[1], state_ref.shape[2]
     right = slice(cols, cols + LANES)
@@ -432,8 +432,11 @@
 
     odd = is_odd()
     packed_half = SLAB // 2
-    beside = jnp.where(odd, within_ref[DOWN_ROWS - 8 : DOWN_ROWS - 1, :], across_ref[DOWN_ROWS - 8 : DOWN_ROWS - 1, :])
-    turned = jnp.concatenate([beside, jnp.zeros((LANES - 7, LANES), jnp.float32)], axis=0).T[rows - SLAB : rows]
+    last_rows = slice(DOWN_ROWS - 8, DOWN_ROWS - 1)
+    aside[0:7, :] = jnp.where(odd, within_ref[last_rows, :], across_ref[last_rows, :])
+    aside[7:8, :] = jnp.zeros((1, LANES), jnp.float32)
+    beside = aside[...]
+    turned = jnp.concatenate([beside, jnp.zeros((LANES - 8, LANES), jnp.float32)], axis=0).T[rows - SLAB : rows]
     lanes = lane_ids(packed_half)
     tiles = cols // LANES + 1
     for comp in range(3):
@@ -634,6 +637,7 @@
             [vmem(8, width)] * 3,
             [vmem(2 * PATCH, 2 * PATCH)] * 3,
             vmem(half, cols // 2),
+            vmem(8, LANES),
             pltpu.SemaphoreType.DMA((8,)),
         ],
         compiler_params=PARAMS,

time: 17.4 us -> 17.4 us (level)
  no operation moved by 1% of the time
where the time goes in v10:
time: 17.4 us; the launch traced here: 17.2 us
  starting transfers between devices  7.76 us (45%)
  Pallas kernels  4.77 us (27%)
  waiting for transfers between devices  2.38 us (14%)
  between operations  2.04 us (12%)
  local copies, waits for them, and re-layouts  0.3 us (2%)
    ppermute x1, starting transfers between devices, per_device(): from_right = in_vmem(lax.ppermute(to_left, 'col', around('col', -1)))  3.1 us
    ppermute x1, starting transfers between devices, per_device(): from_left = in_vmem(lax.ppermute(to_right, 'col', around('col', 1)))  2.96 us
    pallas_call x1, Pallas kernels, per_device(): pl.pallas_call(finish, out_shape=(f32(half, cols // 2), f32(3, rows, cols...  2.56 us
    ppermute x1, starting transfers between devices, per_device(): lax.ppermute(within, 'row', [(i, i ^ 1) for i in range(devices)])  1.33 us
    ppermute x1, waiting for transfers between devices, per_device(): from_left = in_vmem(lax.ppermute(to_right, 'col', around('col', 1)))  0.87 us
    pallas_call x1, Pallas kernels, per_device(): pl.pallas_call(lower_error, out_shape=(vmem(half - UPPER, cols // 2), vme...  0.84 us
    ppermute x1, waiting for transfers between devices, per_device(): lax.ppermute(across, 'row', [(i, (i + (1 if i % 2 else -1)) % devices) fo...  0.76 us
    pallas_call x1, Pallas kernels, per_device(): pl.pallas_call(upper_error, out_shape=vmem(UPPER, cols // 2), in_specs=[V...  0.73 us
  transfers between devices with their start and end apart: 5, of which 4 were waited for; matrix products, arithmetic and copies ran while one was open for 0% of the time, Pallas kernels for 12%

profile of v10, /device:TPU:0, one launch (start us, length us, event | category | flops | bytes accessed | tf_op | source)
XLA Modules:
  0.0 17.2 jit_solution(12172095365025423343)
XLA Ops:
  0.6 0.0 copy-start
  1.3 0.3 %copy-done = f32[3,128,256]{2,1,0:T(8,128)S(1)} copy-done((f32[3,128,256]{2,1,0:T(8,128)S(1)}, f32[3,128,256]{2,1,0:T(8,128)}, u32[]{:S(2)}) %copy-start) | copy-done | bytes 393240
  1.6 0.2 %pack_cols.1 = (f32[200,128]{1,0:T(8,128)S(1)}, f32[32,128]{1,0:T(8,128)S(1)}, f32[3,64,256]{2,1,0:T(8,128)S(1)}) custom-call(s32[1,1]{1,0:T(1,128)S(6)} %copy.8.row_count, f32[8,128]{1,0:T(8,128)S(1)} %ahead.1.blank_ref, f32[3,128,256]{2,1,0:T(8,128)S(1)} %copy-done), custom_call_target="tpu_custom_call" | custom-call | tf_op jit(solution)/shard_map/pack_cols/pallas_call | solution.py:566
  1.8 3.0 %collective-permute-start = (f32[200,128]{1,0:T(8,128)S(1)}, f32[200,128]{1,0:T(8,128)S(1)}, u32[]{:S(2)}, u32[]{:S(2)}) collective-permute-start(f32[200,128]{1,0:T(8,128)S(1)} %get-tuple-element.16), channel_id=1, source_target_pairs={{0,1},{1,2},{2,3},{3,4},{4,5},{5,6},{6,7},{7,0},{8,9},{9,10},{10,1... | collective-permute-start | bytes 307208 | tf_op jit(solution)/shard_map/ppermute | solution.py:577
  5.5 3.1 %collective-permute-start.1 = (f32[8,128]{1,0:T(8,128)S(1)}, f32[8,128]{1,0:T(8,128)S(1)}, u32[]{:S(2)}, u32[]{:S(2)}) collective-permute-start(f32[8,128]{1,0:T(8,128)S(1)} %get-tuple-element.17), channel_id=1, source_target_pairs={{0,7},{1,0},{2,1},{3,2},{4,3},{5,4},{6,5},{7,6},{8,15},{9,8},{10,9... | collective-permute-start | bytes 12296 | tf_op jit(solution)/shard_map/ppermute | solution.py:578
  8.6 0.0 collective-permute-start.2
  8.6 0.7 %upper_error.1.upper_ref = f32[32,128]{1,0:T(8,128)S(1)} custom-call(f32[3,128,256]{2,1,0:T(8,128)S(1)} %copy-done), custom_call_target="tpu_custom_call" | custom-call | flops 15000000 | bytes 300000 | tf_op jit(solution)/shard_map/upper_error/pallas_call | solution.py:580
  9.3 0.6 %collective-permute-done.1.right_ref = f32[8,128]{1,0:T(8,128)S(1)} collective-permute-done((f32[8,128]{1,0:T(8,128)S(1)}, f32[8,128]{1,0:T(8,128)S(1)}, u32[]{:S(2)}, u32[]{:S(2)}) %collective-permute-start.1) | collective-permute-done | bytes 4128 | tf_op jit(solution)/shard_map/ppermute | solution.py:578
  9.9 0.9 %collective-permute-done.left_ref = f32[200,128]{1,0:T(8,128)S(1)} collective-permute-done((f32[200,128]{1,0:T(8,128)S(1)}, f32[200,128]{1,0:T(8,128)S(1)}, u32[]{:S(2)}, u32[]{:S(2)}) %collective-permute-start) | collective-permute-done | bytes 102432 | tf_op jit(solution)/shard_map/ppermute | solution.py:577
  10.8 0.2 %pack_rows.1 = (f32[3,128,128]{2,1,0:T(8,128)S(1)}, f32[103,128]{1,0:T(8,128)S(1)}, f32[104,128]{1,0:T(8,128)S(1)}, f32[3,16,128]{2,1,0:T(8,128)S(1)}) custom-call(f32[8,128]{1,0:T(8,128)S(1)} %get-tuple-element.15.counts_ref, f32[32,128]{1,0:T(8,128)S(1)} %get-tuple-element.14.strip_ref, f32[200,128]{1,0:T(8,128)S(1)} %collective-permute-done.left_ref, ...), custom_call_target="tpu_custom_call" | custom-call | flops 3000000000 | bytes 600000 | tf_op jit(solution)/shard_map/pack_rows/pallas_call | solution.py:589
  10.9 0.4 %collective-permute-start.4 = (f32[104,128]{1,0:T(8,128)S(1)}, f32[104,128]{1,0:T(8,128)S(1)}, u32[]{:S(2)}, u32[]{:S(2)}) collective-permute-start(f32[104,128]{1,0:T(8,128)S(1)} %get-tuple-element.21), channel_id=1, source_target_pairs={{0,24},{8,16},{16,8},{24,0},{1,25},{9,17},{17,9},{25,1},{2,26},{10... | collective-permute-start | bytes 159752 | tf_op jit(solution)/shard_map/ppermute | solution.py:615
  11.3 1.3 %collective-permute-start.3 = (f32[103,128]{1,0:T(8,128)S(1)}, f32[103,128]{1,0:T(8,128)S(1)}, u32[]{:S(2)}, u32[]{:S(2)}) collective-permute-start(f32[103,128]{1,0:T(8,128)S(1)} %get-tuple-element.20), channel_id=1, source_target_pairs={{0,8},{8,0},{16,24},{24,16},{1,9},{9,1},{17,25},{25,17},{2,10},{10... | collective-permute-start | bytes 158216 | tf_op jit(solution)/shard_map/ppermute | solution.py:613
  12.6 0.8 %lower_error.1 = (f32[32,128]{1,0:T(8,128)S(1)}, f32[8,128]{1,0:T(8,128)S(1)}) custom-call(s32[1,1,2]{2,1,0:T(1,128)} %pos_ref.1, s32[1,1,2]{2,1,0:T(1,128)} %ext_ref.1, f32[3,128,256]{2,1,0:T(8,128)S(1)} %copy-done, f32[3,128,128]{2,1,0:T(8,128)S(1)} %get-tuple-element.18.rim_ref), custom_call_target="tpu_custom_call" | custom-call | flops 15000000 | bytes 300000 | tf_op jit(solution)/shard_map/lower_error/pallas_call | solution.py:598
  13.5 0.2 collective-permute-done.2.slab_ref
  13.6 0.3 %move_rows.1.rows_ref = f32[3,144,512]{2,1,0:T(8,128)S(1)} custom-call(f32[3,128,256]{2,1,0:T(8,128)S(1)} %copy-done, f32[3,128,128]{2,1,0:T(8,128)S(1)} %get-tuple-element.18.rim_ref, f32[3,64,256]{2,1,0:T(8,128)S(1)} %collective-permute-done.2.slab_ref), custom_call_target="tpu_custom_call" | custom-call | flops 3000000 | bytes 1000000 | tf_op jit(solution)/shard_map/move_rows/pallas_call | solution.py:617
  13.9 0.0 collective-permute-done.3.within_ref
  13.9 0.8 %collective-permute-done.4.across_ref = f32[104,128]{1,0:T(8,128)S(1)} collective-permute-done((f32[104,128]{1,0:T(8,128)S(1)}, f32[104,128]{1,0:T(8,128)S(1)}, u32[]{:S(2)}, u32[]{:S(2)}) %collective-permute-start.4) | collective-permute-done | bytes 53280 | tf_op jit(solution)/shard_map/ppermute | solution.py:615
  14.7 2.6 %finish.1 = (f32[64,128]{1,0:T(8,128)}, f32[3,128,256]{2,1,0:T(8,128)}, f32[3,128,128]{2,1,0:T(8,128)}) custom-call(f32[3,128,256]{2,1,0:T(8,128)S(1)} %copy-done, f32[3,128,128]{2,1,0:T(8,128)S(1)} %get-tuple-element.18.rim_ref, f32[3,64,256]{2,1,0:T(8,128)S(1)} %collective-permute-done.2.slab_ref, f32[3,144,512]{2,1,0:T(8,128)S(1)} %move_rows.1.rows_ref, ...), custom_call_target="tpu_custom_call" | custom-call | tf_op jit(solution)/shard_map/finish/pallas_call | solution.py:625
  (2 shorter events, 0.0 us)
Async XLA Ops:
  0.6 1.0 %copy-start = (f32[3,128,256]{2,1,0:T(8,128)S(1)}, f32[3,128,256]{2,1,0:T(8,128)}, u32[]{:S(2)}) copy-start(f32[3,128,256]{2,1,0:T(8,128)} %state_ref.11) | copy-start | bytes 1179652
  1.8 8.9 %collective-permute-start = (f32[200,128]{1,0:T(8,128)S(1)}, f32[200,128]{1,0:T(8,128)S(1)}, u32[]{:S(2)}, u32[]{:S(2)}) collective-permute-start(f32[200,128]{1,0:T(8,128)S(1)} %get-tuple-element.16), channel_id=1, source_target_pairs={{0,1},{1,2},{2,3},{3,4},{4,5},{5,6},{6,7},{7,0},{8,9},{9,10},{10,1... | collective-permute-start | bytes 307208 | tf_op jit(solution)/shard_map/ppermute | solution.py:577
  5.5 4.4 %collective-permute-start.1 = (f32[8,128]{1,0:T(8,128)S(1)}, f32[8,128]{1,0:T(8,128)S(1)}, u32[]{:S(2)}, u32[]{:S(2)}) collective-permute-start(f32[8,128]{1,0:T(8,128)S(1)} %get-tuple-element.17), channel_id=1, source_target_pairs={{0,7},{1,0},{2,1},{3,2},{4,3},{5,4},{6,5},{7,6},{8,15},{9,8},{10,9... | collective-permute-start | bytes 12296 | tf_op jit(solution)/shard_map/ppermute | solution.py:578
  8.6 5.1 %collective-permute-start.2 = (f32[3,64,256]{2,1,0:T(8,128)S(1)}, f32[3,64,256]{2,1,0:T(8,128)S(1)}, u32[]{:S(2)}, u32[]{:S(2)}) collective-permute-start(f32[3,64,256]{2,1,0:T(8,128)S(1)} %get-tuple-element.19), channel_id=1, source_target_pairs={{0,8},{8,16},{16,24},{24,0},{1,9},{9,17},{17,25},{25,1},{2,10},{10... | collective-permute-start | bytes 589832 | tf_op jit(solution)/shard_map/ppermute | solution.py:579
  10.9 3.7 %collective-permute-start.4 = (f32[104,128]{1,0:T(8,128)S(1)}, f32[104,128]{1,0:T(8,128)S(1)}, u32[]{:S(2)}, u32[]{:S(2)}) collective-permute-start(f32[104,128]{1,0:T(8,128)S(1)} %get-tuple-element.21), channel_id=1, source_target_pairs={{0,24},{8,16},{16,8},{24,0},{1,25},{9,17},{17,9},{25,1},{2,26},{10... | collective-permute-start | bytes 159752 | tf_op jit(solution)/shard_map/ppermute | solution.py:615
  11.3 2.6 %collective-permute-start.3 = (f32[103,128]{1,0:T(8,128)S(1)}, f32[103,128]{1,0:T(8,128)S(1)}, u32[]{:S(2)}, u32[]{:S(2)}) collective-permute-start(f32[103,128]{1,0:T(8,128)S(1)} %get-tuple-element.20), channel_id=1, source_target_pairs={{0,8},{8,0},{16,24},{24,16},{1,9},{9,1},{17,25},{25,17},{2,10},{10... | collective-permute-start | bytes 158216 | tf_op jit(solution)/shard_map/ppermute | solution.py:613

commit v11 on v10

--- a/solution.py
+++ b/solution.py
@@ -124,7 +124,7 @@
     out_ref[...] = jnp.zeros(out_ref.shape, jnp.float32)
 
 
-def pack_cols(row_count, blank_ref, state_ref, left_ref, strip_ref, slab_ref):
+def pack_cols(row_count, blank_ref, state_ref, left_ref, strip_ref):
     rows, cols = state_ref.shape[1], state_ref.shape[2]
     half = rows // 2
     rc = row_count[0, 0].astype(jnp.float32)
@@ -144,10 +144,10 @@
     left_ref[3 * half : 3 * half + 8, :] = jnp.full((8, LANES), rc)
     for comp in range(3):
         left_ref[3 * half + 2 * comp : 3 * half + 2 * comp + 2, :] = strip_ref[8 * comp + 2 : 8 * comp + 4, :]
-    slab_ref[...] = state_ref[:, rows - SLAB : rows, :]
-
-
-def pack_right(col_count, strip_ref, right_ref, counts_ref):
+
+
+def pack_right(col_count, strip_ref, state_ref, right_ref, counts_ref, slab_ref):
+    slab_ref[...] = state_ref[:, state_ref.shape[1] - SLAB :, :]
     cc = col_count[0, 0].astype(jnp.float32)
     counts = jnp.where(row_ids(8) == 6, strip_ref[24:32, :], cc)
     counts_ref[...] = counts
@@ -563,17 +563,21 @@
         cost_estimate=pl.CostEstimate(flops=10_000_000_000, bytes_accessed=10_000_000, transcendentals=0),
         name="ahead",
     )()
-    to_right, strip, slab = pl.pallas_call(
+    to_right, strip = pl.pallas_call(
         pack_cols,
-        out_shape=(vmem(3 * half + 8, LANES), vmem(32, LANES), vmem(3, SLAB, cols)),
+        out_shape=(vmem(3 * half + 8, LANES), vmem(32, LANES)),
         in_specs=[SMEM, VMEM, VMEM],
-        out_specs=(VMEM,) * 3,
+        out_specs=(VMEM,) * 2,
         name="pack_cols",
     )(row_count, in_vmem(ahead), here)
     strip = in_vmem(strip)
-    to_left, counts = pl.pallas_call(
-        pack_right, out_shape=(vmem(8, LANES), vmem(8, LANES)), in_specs=[SMEM, VMEM], out_specs=(VMEM,) * 2, name="pack_right"
-    )(col_count, strip)
+    to_left, counts, slab = pl.pallas_call(
+        pack_right,
+        out_shape=(vmem(8, LANES), vmem(8, LANES), vmem(3, SLAB, cols)),
+        in_specs=[SMEM, VMEM, VMEM],
+        out_specs=(VMEM,) * 3,
+        name="pack_right",
+    )(col_count, strip, here)
     from_left = in_vmem(lax.ppermute(to_right, "col", around("col", 1)))
     from_right = in_vmem(lax.ppermute(to_left, "col", around("col", -1)))
     slab_above = in_vmem(lax.ppermute(slab, "row", around("row", 1)))

time: 17.4 us -> 17.4 us (level)
  no operation moved by 1% of the time
where the time goes in v11:
time: 17.4 us; the launch traced here: 17.3 us
  starting transfers between devices  7.76 us (45%)
  Pallas kernels  4.77 us (27%)
  waiting for transfers between devices  2.38 us (14%)
  between operations  2.04 us (12%)
  local copies, waits for them, and re-layouts  0.3 us (2%)
    ppermute x1, starting transfers between devices, per_device(): from_right = in_vmem(lax.ppermute(to_left, 'col', around('col', -1)))  3.1 us
    ppermute x1, starting transfers between devices, per_device(): from_left = in_vmem(lax.ppermute(to_right, 'col', around('col', 1)))  2.96 us
    pallas_call x1, Pallas kernels, per_device(): pl.pallas_call(finish, out_shape=(f32(half, cols // 2), f32(3, rows, cols...  2.56 us
    ppermute x1, starting transfers between devices, per_device(): lax.ppermute(within, 'row', [(i, i ^ 1) for i in range(devices)])  1.32 us
    ppermute x1, waiting for transfers between devices, per_device(): from_left = in_vmem(lax.ppermute(to_right, 'col', around('col', 1)))  0.86 us
    pallas_call x1, Pallas kernels, per_device(): pl.pallas_call(lower_error, out_shape=(vmem(half - UPPER, cols // 2), vme...  0.84 us
    ppermute x1, waiting for transfers between devices, per_device(): lax.ppermute(across, 'row', [(i, (i + (1 if i % 2 else -1)) % devices) fo...  0.76 us
    pallas_call x1, Pallas kernels, per_device(): pl.pallas_call(upper_error, out_shape=vmem(UPPER, cols // 2), in_specs=[V...  0.73 us
  transfers between devices with their start and end apart: 5, of which 4 were waited for; matrix products, arithmetic and copies ran while one was open for 0% of the time, Pallas kernels for 12%

profile of v11, /device:TPU:0, one launch (start us, length us, event | category | flops | bytes accessed | tf_op | source)
XLA Modules:
  0.0 17.3 jit_solution(7315364849970154425)
XLA Ops:
  0.6 0.0 copy-start
  1.3 0.3 %copy-done = f32[3,128,256]{2,1,0:T(8,128)S(1)} copy-done((f32[3,128,256]{2,1,0:T(8,128)S(1)}, f32[3,128,256]{2,1,0:T(8,128)}, u32[]{:S(2)}) %copy-start) | copy-done | bytes 393240
  1.6 0.2 %pack_cols.1 = (f32[200,128]{1,0:T(8,128)S(1)}, f32[32,128]{1,0:T(8,128)S(1)}) custom-call(s32[1,1]{1,0:T(1,128)S(6)} %copy.8.row_count, f32[8,128]{1,0:T(8,128)S(1)} %ahead.1.blank_ref, f32[3,128,256]{2,1,0:T(8,128)S(1)} %copy-done), custom_call_target="tpu_custom_call" | custom-call | tf_op jit(solution)/shard_map/pack_cols/pallas_call | solution.py:566
  1.8 3.0 %collective-permute-start = (f32[200,128]{1,0:T(8,128)S(1)}, f32[200,128]{1,0:T(8,128)S(1)}, u32[]{:S(2)}, u32[]{:S(2)}) collective-permute-start(f32[200,128]{1,0:T(8,128)S(1)} %get-tuple-element.16), channel_id=1, source_target_pairs={{0,1},{1,2},{2,3},{3,4},{4,5},{5,6},{6,7},{7,0},{8,9},{9,10},{10,1... | collective-permute-start | bytes 307208 | tf_op jit(solution)/shard_map/ppermute | solution.py:581
  5.5 3.1 %collective-permute-start.1 = (f32[8,128]{1,0:T(8,128)S(1)}, f32[8,128]{1,0:T(8,128)S(1)}, u32[]{:S(2)}, u32[]{:S(2)}) collective-permute-start(f32[8,128]{1,0:T(8,128)S(1)} %get-tuple-element.17), channel_id=1, source_target_pairs={{0,7},{1,0},{2,1},{3,2},{4,3},{5,4},{6,5},{7,6},{8,15},{9,8},{10,9... | collective-permute-start | bytes 12296 | tf_op jit(solution)/shard_map/ppermute | solution.py:582
  8.6 0.0 collective-permute-start.2
  8.6 0.7 %upper_error.1.upper_ref = f32[32,128]{1,0:T(8,128)S(1)} custom-call(f32[3,128,256]{2,1,0:T(8,128)S(1)} %copy-done), custom_call_target="tpu_custom_call" | custom-call | flops 15000000 | bytes 300000 | tf_op jit(solution)/shard_map/upper_error/pallas_call | solution.py:584
  9.3 0.6 %collective-permute-done.1.right_ref = f32[8,128]{1,0:T(8,128)S(1)} collective-permute-done((f32[8,128]{1,0:T(8,128)S(1)}, f32[8,128]{1,0:T(8,128)S(1)}, u32[]{:S(2)}, u32[]{:S(2)}) %collective-permute-start.1) | collective-permute-done | bytes 4128 | tf_op jit(solution)/shard_map/ppermute | solution.py:582
  9.9 0.9 %collective-permute-done.left_ref = f32[200,128]{1,0:T(8,128)S(1)} collective-permute-done((f32[200,128]{1,0:T(8,128)S(1)}, f32[200,128]{1,0:T(8,128)S(1)}, u32[]{:S(2)}, u32[]{:S(2)}) %collective-permute-start) | collective-permute-done | bytes 102432 | tf_op jit(solution)/shard_map/ppermute | solution.py:581
  10.8 0.2 %pack_rows.1 = (f32[3,128,128]{2,1,0:T(8,128)S(1)}, f32[103,128]{1,0:T(8,128)S(1)}, f32[104,128]{1,0:T(8,128)S(1)}, f32[3,16,128]{2,1,0:T(8,128)S(1)}) custom-call(f32[8,128]{1,0:T(8,128)S(1)} %get-tuple-element.15.counts_ref, f32[32,128]{1,0:T(8,128)S(1)} %get-tuple-element.14.strip_ref, f32[200,128]{1,0:T(8,128)S(1)} %collective-permute-done.left_ref, ...), custom_call_target="tpu_custom_call" | custom-call | flops 3000000000 | bytes 600000 | tf_op jit(solution)/shard_map/pack_rows/pallas_call | solution.py:593
  10.9 0.4 %collective-permute-start.4 = (f32[104,128]{1,0:T(8,128)S(1)}, f32[104,128]{1,0:T(8,128)S(1)}, u32[]{:S(2)}, u32[]{:S(2)}) collective-permute-start(f32[104,128]{1,0:T(8,128)S(1)} %get-tuple-element.21), channel_id=1, source_target_pairs={{0,24},{8,16},{16,8},{24,0},{1,25},{9,17},{17,9},{25,1},{2,26},{10... | collective-permute-start | bytes 159752 | tf_op jit(solution)/shard_map/ppermute | solution.py:619
  11.3 1.3 %collective-permute-start.3 = (f32[103,128]{1,0:T(8,128)S(1)}, f32[103,128]{1,0:T(8,128)S(1)}, u32[]{:S(2)}, u32[]{:S(2)}) collective-permute-start(f32[103,128]{1,0:T(8,128)S(1)} %get-tuple-element.20), channel_id=1, source_target_pairs={{0,8},{8,0},{16,24},{24,16},{1,9},{9,1},{17,25},{25,17},{2,10},{10... | collective-permute-start | bytes 158216 | tf_op jit(solution)/shard_map/ppermute | solution.py:617
  12.6 0.8 %lower_error.1 = (f32[32,128]{1,0:T(8,128)S(1)}, f32[8,128]{1,0:T(8,128)S(1)}) custom-call(s32[1,1,2]{2,1,0:T(1,128)} %pos_ref.1, s32[1,1,2]{2,1,0:T(1,128)} %ext_ref.1, f32[3,128,256]{2,1,0:T(8,128)S(1)} %copy-done, f32[3,128,128]{2,1,0:T(8,128)S(1)} %get-tuple-element.18.rim_ref), custom_call_target="tpu_custom_call" | custom-call | flops 15000000 | bytes 300000 | tf_op jit(solution)/shard_map/lower_error/pallas_call | solution.py:602
  13.5 0.2 collective-permute-done.2.slab_ref
  13.7 0.3 %move_rows.1.rows_ref = f32[3,144,512]{2,1,0:T(8,128)S(1)} custom-call(f32[3,128,256]{2,1,0:T(8,128)S(1)} %copy-done, f32[3,128,128]{2,1,0:T(8,128)S(1)} %get-tuple-element.18.rim_ref, f32[3,64,256]{2,1,0:T(8,128)S(1)} %collective-permute-done.2.slab_ref), custom_call_target="tpu_custom_call" | custom-call | flops 3000000 | bytes 1000000 | tf_op jit(solution)/shard_map/move_rows/pallas_call | solution.py:621
  13.9 0.0 collective-permute-done.3.within_ref
  13.9 0.8 %collective-permute-done.4.across_ref = f32[104,128]{1,0:T(8,128)S(1)} collective-permute-done((f32[104,128]{1,0:T(8,128)S(1)}, f32[104,128]{1,0:T(8,128)S(1)}, u32[]{:S(2)}, u32[]{:S(2)}) %collective-permute-start.4) | collective-permute-done | bytes 53280 | tf_op jit(solution)/shard_map/ppermute | solution.py:619
  14.7 2.6 %finish.1 = (f32[64,128]{1,0:T(8,128)}, f32[3,128,256]{2,1,0:T(8,128)}, f32[3,128,128]{2,1,0:T(8,128)}) custom-call(f32[3,128,256]{2,1,0:T(8,128)S(1)} %copy-done, f32[3,128,128]{2,1,0:T(8,128)S(1)} %get-tuple-element.18.rim_ref, f32[3,64,256]{2,1,0:T(8,128)S(1)} %collective-permute-done.2.slab_ref, f32[3,144,512]{2,1,0:T(8,128)S(1)} %move_rows.1.rows_ref, ...), custom_call_target="tpu_custom_call" | custom-call | tf_op jit(solution)/shard_map/finish/pallas_call | solution.py:629
  (2 shorter events, 0.0 us)
Async XLA Ops:
  0.6 1.0 %copy-start = (f32[3,128,256]{2,1,0:T(8,128)S(1)}, f32[3,128,256]{2,1,0:T(8,128)}, u32[]{:S(2)}) copy-start(f32[3,128,256]{2,1,0:T(8,128)} %state_ref.13) | copy-start | bytes 1179652
  1.8 8.9 %collective-permute-start = (f32[200,128]{1,0:T(8,128)S(1)}, f32[200,128]{1,0:T(8,128)S(1)}, u32[]{:S(2)}, u32[]{:S(2)}) collective-permute-start(f32[200,128]{1,0:T(8,128)S(1)} %get-tuple-element.16), channel_id=1, source_target_pairs={{0,1},{1,2},{2,3},{3,4},{4,5},{5,6},{6,7},{7,0},{8,9},{9,10},{10,1... | collective-permute-start | bytes 307208 | tf_op jit(solution)/shard_map/ppermute | solution.py:581
  5.5 4.4 %collective-permute-start.1 = (f32[8,128]{1,0:T(8,128)S(1)}, f32[8,128]{1,0:T(8,128)S(1)}, u32[]{:S(2)}, u32[]{:S(2)}) collective-permute-start(f32[8,128]{1,0:T(8,128)S(1)} %get-tuple-element.17), channel_id=1, source_target_pairs={{0,7},{1,0},{2,1},{3,2},{4,3},{5,4},{6,5},{7,6},{8,15},{9,8},{10,9... | collective-permute-start | bytes 12296 | tf_op jit(solution)/shard_map/ppermute | solution.py:582
  8.6 5.1 %collective-permute-start.2 = (f32[3,64,256]{2,1,0:T(8,128)S(1)}, f32[3,64,256]{2,1,0:T(8,128)S(1)}, u32[]{:S(2)}, u32[]{:S(2)}) collective-permute-start(f32[3,64,256]{2,1,0:T(8,128)S(1)} %get-tuple-element.19), channel_id=1, source_target_pairs={{0,8},{8,16},{16,24},{24,0},{1,9},{9,17},{17,25},{25,1},{2,10},{10... | collective-permute-start | bytes 589832 | tf_op jit(solution)/shard_map/ppermute | solution.py:583
  10.9 3.7 %collective-permute-start.4 = (f32[104,128]{1,0:T(8,128)S(1)}, f32[104,128]{1,0:T(8,128)S(1)}, u32[]{:S(2)}, u32[]{:S(2)}) collective-permute-start(f32[104,128]{1,0:T(8,128)S(1)} %get-tuple-element.21), channel_id=1, source_target_pairs={{0,24},{8,16},{16,8},{24,0},{1,25},{9,17},{17,9},{25,1},{2,26},{10... | collective-permute-start | bytes 159752 | tf_op jit(solution)/shard_map/ppermute | solution.py:619
  11.3 2.6 %collective-permute-start.3 = (f32[103,128]{1,0:T(8,128)S(1)}, f32[103,128]{1,0:T(8,128)S(1)}, u32[]{:S(2)}, u32[]{:S(2)}) collective-permute-start(f32[103,128]{1,0:T(8,128)S(1)} %get-tuple-element.20), channel_id=1, source_target_pairs={{0,8},{8,0},{16,24},{24,16},{1,9},{9,1},{17,25},{25,17},{2,10},{10... | collective-permute-start | bytes 158216 | tf_op jit(solution)/shard_map/ppermute | solution.py:617
